TPU v7x, 32 devices: a whole 2x2x4 slice. The times are simulated.
32 devices in a mesh: groups: 2 (over x), seq: 8 (over z, y), head: 2 (over core).
Axes of the slice: x: 2, y: 2, z: 4, core: 2. Of those that a mesh axis runs over, the one named last changes fastest.
Arguments:
- queries: bfloat16 [2, 3072, 2048], P(None, ('groups', 'seq'), 'head'), parts along dimension 1, may hold values from -6 to 6
- keys: bfloat16 [2, 3072, 2048], P(None, ('groups', 'seq'), 'head'), parts along dimension 1, may hold values from -6 to 6
- values: bfloat16 [2, 3072, 2048], P(None, ('groups', 'seq'), 'head'), parts along dimension 1, may hold values from -6 to 6
- rates: float32 [2, 3072, 4], P(None, ('groups', 'seq'), 'head'), parts along dimension 1, may hold values from 0.0005638186 to 0.0056381864
- fast_init: bfloat16 [3, 4, 512, 512], P(None, 'head'), may hold values from -0.8838835 to 0.8838835
- out_proj: bfloat16 [2048, 2048], P('seq'), may hold values from -0.125 to 0.125
Outputs:
- projected: bfloat16 [2, 3072, 2048], P(None, ('groups', 'seq', 'head')), parts along dimension 1
There are 2 independent parts, one for each index of `groups`. A program takes and returns all parts, laid end to end along the dimension named above; an argument that names none is the same for every part. Nothing has to cross between parts.
All inputs are finite; a program needn't handle non-finite values.
Results may differ from a plain program's by a relative error of at most 0.012.
The roundings to bfloat16 on the way count: a program that leaves them out, or rounds other values in their place, can miss the bound.
Values may be sent and summed in bfloat16 or wider, within the bound.
No kernel may reach another device: no remote copies, remote signals or barrier semaphores. Data moves between devices by JAX's collectives and lax.ppermute only.
A program may use at most 128 MiB of HBM per device.

v0:
```python
import jax
import jax.numpy as jnp
from jax import lax
from jax.sharding import PartitionSpec as P


def silu_parts(value):
    sigma = jax.nn.sigmoid(value)
    return (value * sigma, sigma * (1.0 + value * (1.0 - sigma)))


def local_update(weights, keys_local, values_local, rates_local):
    gate_pre = jnp.einsum(
        "thi,hoi->tho", keys_local, weights[0], preferred_element_type=jnp.float32
    )
    up_pre = jnp.einsum("thi,hoi->tho", keys_local, weights[1], preferred_element_type=jnp.float32)
    gate_act, gate_slope = silu_parts(gate_pre)
    hidden = (gate_act * up_pre).astype(jnp.bfloat16)
    weighted = (rates_local[:, :, None] * values_local.astype(jnp.float32)).astype(jnp.bfloat16)
    back = jnp.einsum("tho,hog->thg", weighted, weights[2], preferred_element_type=jnp.float32)
    grad_gate = (back * up_pre * gate_slope).astype(jnp.bfloat16)
    grad_up = (back * gate_act).astype(jnp.bfloat16)
    return jnp.stack(
        [
            jnp.einsum("thg,thi->hgi", grad_gate, keys_local, preferred_element_type=jnp.float32),
            jnp.einsum("thg,thi->hgi", grad_up, keys_local, preferred_element_type=jnp.float32),
            jnp.einsum("tho,thg->hog", weighted, hidden, preferred_element_type=jnp.float32),
        ]
    )


def apply_local(weights, queries_local):
    gate_pre = jnp.einsum(
        "thi,hoi->tho", queries_local, weights[0], preferred_element_type=jnp.float32
    )
    up_pre = jnp.einsum(
        "thi,hoi->tho", queries_local, weights[1], preferred_element_type=jnp.float32
    )
    gate_act, gate_slope = silu_parts(gate_pre)
    applied = (gate_act * up_pre).astype(jnp.bfloat16)
    produced = jnp.einsum("thg,hog->tho", applied, weights[2], preferred_element_type=jnp.float32)
    return produced.astype(jnp.bfloat16).reshape(queries_local.shape[0], -1)


def local(queries, keys, values, rates, fast_init, out_proj):
    block_count, tok_count, width_here = queries.shape
    heads_here = fast_init.shape[1]
    head_width = fast_init.shape[2]
    init_float = fast_init.astype(jnp.float32)
    target = jnp.sqrt(jnp.mean(init_float * init_float, axis=-1, keepdims=True))
    row_count = head_width // lax.axis_size("seq")
    offset = lax.axis_index("seq") * row_count
    current = fast_init
    produced_list = []
    for block_idx in range(block_count):
        keys_local = keys[block_idx].reshape(tok_count, heads_here, head_width)
        values_local = values[block_idx].reshape(tok_count, heads_here, head_width)
        update = local_update(current, keys_local, values_local, rates[block_idx])
        shard = lax.psum_scatter(update, "seq", scatter_dimension=3, tiled=True)
        own = lax.dynamic_slice_in_dim(current, offset, row_count, 3).astype(jnp.float32) + shard
        squares = lax.psum(jnp.sum(own * own, axis=-1, keepdims=True), "seq")
        fresh = (own * target * lax.rsqrt(squares / head_width + 1e-06)).astype(jnp.bfloat16)
        current = lax.all_gather(fresh, "seq", axis=3, tiled=True)
        produced = apply_local(
            current, queries[block_idx].reshape(tok_count, heads_here, head_width)
        )
        produced_list.append(produced)
    mixed = lax.all_to_all(
        jnp.stack(produced_list), "head", split_axis=1, concat_axis=2, tiled=True
    )
    result = jnp.einsum(
        "ctf,fd->ctd",
        mixed,
        lax.all_gather(out_proj, "seq", axis=0, tiled=True),
        preferred_element_type=jnp.float32,
    )
    return result.astype(jnp.bfloat16)


def solution(mesh):
    in_specs = (
        P(None, ("groups", "seq"), "head"),
        P(None, ("groups", "seq"), "head"),
        P(None, ("groups", "seq"), "head"),
        P(None, ("groups", "seq"), "head"),
        P(None, "head", None, None),
        P("seq", None),
    )
    out_specs = P(None, ("groups", "seq", "head"), None)
    return jax.shard_map(local, mesh=mesh, in_specs=in_specs, out_specs=out_specs, check_vma=False)
```

profile of v0, /device:TPU:0, one launch (start us, length us, event | category | flops | bytes accessed | tf_op | source)
XLA Modules:
  0.0 821.1 jit_solution(14663553157097537215)
XLA Ops:
  6.5 2.1 fusion.79
  8.6 1.0 reshape_squeeze.14
  9.6 2.8 convolution_bitcast_fusion.13
  12.4 2.4 convolution_bitcast_fusion.14
  14.8 1.3 slice_convert_fusion
  16.1 2.7 reshape.12
  18.8 1.7 convolution_bitcast_fusion.15
  20.5 1.6 convolution_bitcast_fusion.4
  22.2 0.6 convolution_bitcast_fusion.5
  22.8 0.6 copy-done.3
  23.3 0.6 convolution_bitcast_fusion.3
  23.9 3.4 pad_maximum_fusion
  27.3 10.3 %copy.30 = f32[3,2,512,512]{2,1,0,3:T(2,128)} copy(f32[3,2,512,512]{3,2,1,0:T(8,128)} %pad_maximum_fusion) | data formatting | bytes 12582912 | tf_op jit(solution)/shard_map/stack | solution.py:23
  37.7 1.2 constant_dynamic-slice_fusion
  38.9 1.5 copy.52
  40.4 0.6 dynamic-slice
  41.6 0.7 multiply_reduce_fusion
  42.4 209.4 %all-reduce.5.cloned.1.call-done = f32[3,2,512,512]{2,1,0,3:T(2,128)} async-done(((f32[3,2,512,512]{2,1,0,3:T(2,128)}), f32[3,2,512,512]{2,1,0,3:T(2,128)}) %all-reduce.5.cloned.1.call-update) | async-done | bytes 6291472
  251.8 1.7 multiply_reduce_fusion.2
  253.5 35.2 %psum.14 = f32[3,2,512,1]{2,1,0,3:T(2,128)S(1)} all-reduce(f32[3,2,512,1]{2,1,0,3:T(2,128)S(1)} %bitcast.107), channel_id=1, replica_groups=mesh['groups'=2,'seq'=8,'head'=2] {'seq'}, use_global_device_ids=true, to_apply=%region_3.0 | all-reduce | flops 3072 | bytes 24576 | tf_op jit(solution)/shard_map/psum | solution.py:61
  288.6 2.4 multiply_convert_fusion.4
  291.1 0.2 all-reduce.7.cloned.1.call-start
  291.3 1.5 reshape.13
  292.9 0.3 reshape_squeeze.16
  293.1 55.8 %all-gather.4.cloned.1.call-done = bf16[3,2,512,512]{2,1,0,3:T(2,128)(2,1)} async-done(((bf16[3,2,512,64]{2,1,0,3:T(2,128)(2,1)}), bf16[3,2,512,512]{2,1,0,3:T(2,128)(2,1)}) %all-gather.4.cloned.1.call-update) | async-done | bytes 3145744 | tf_op jit(solution)/shard_map/all_gather | solution.py:63
  348.9 4.3 fusion.77
  353.2 1.4 copy.54
  354.7 1.5 copy.53
  356.2 2.5 copy.55
  358.6 0.5 convolution_bitcast_fusion.9
  359.1 0.5 convolution_bitcast_fusion.10
  359.8 0.4 convolution_bitcast_fusion.6
  360.2 0.5 convolution_bitcast_fusion.1
  360.7 0.6 convolution_bitcast_fusion.2
  361.3 0.6 convolution_bitcast_fusion
  361.9 3.4 pad_maximum_fusion.1
  365.3 10.3 %copy.42 = f32[3,2,512,512]{2,1,0,3:T(2,128)} copy(f32[3,2,512,512]{3,2,1,0:T(8,128)} %pad_maximum_fusion.1) | data formatting | bytes 12582912 | tf_op jit(solution)/shard_map/stack | solution.py:23
  375.6 210.0 %all-reduce.7.cloned.1.call-done = f32[3,2,512,512]{2,1,0,3:T(2,128)} async-done(((f32[3,2,512,512]{2,1,0,3:T(2,128)}), f32[3,2,512,512]{2,1,0,3:T(2,128)}) %all-reduce.7.cloned.1.call-update) | async-done | bytes 6291472
  585.6 1.8 multiply_reduce_fusion.1
  587.4 35.2 %psum.15 = f32[3,2,512,1]{2,1,0,3:T(2,128)S(1)} all-reduce(f32[3,2,512,1]{2,1,0,3:T(2,128)S(1)} %bitcast.108), channel_id=1, replica_groups=mesh['groups'=2,'seq'=8,'head'=2] {'seq'}, use_global_device_ids=true, to_apply=%region_6.0 | all-reduce | flops 3072 | bytes 24576 | tf_op jit(solution)/shard_map/psum | solution.py:61
  622.6 2.5 multiply_convert_fusion
  625.1 0.3 all-gather.8.cloned.1.call-start
  625.4 0.3 all-gather.8.cloned.1.call-update
  625.7 1.9 fusion.78
  627.6 2.0 reshape_squeeze.15
  629.6 1.0 reshape_squeeze.17
  630.7 2.4 convolution_bitcast_fusion.12
  633.1 2.1 fusion.9
  635.2 0.4 copy.36
  635.6 0.3 stack_reshape.6
  635.9 47.1 %all-gather.6.cloned.1.call-done = bf16[3,2,512,512]{2,1,0,3:T(2,128)(2,1)} async-done(((bf16[3,2,512,64]{2,1,0,3:T(2,128)(2,1)}), bf16[3,2,512,512]{2,1,0,3:T(2,128)(2,1)}) %all-gather.6.cloned.1.call-update) | async-done | bytes 3145744 | tf_op jit(solution)/shard_map/all_gather | solution.py:63
  682.9 4.3 fusion.76
  687.3 2.4 copy.57
  689.7 2.5 copy.56
  692.2 2.5 copy.58
  694.7 1.5 convolution_bitcast_fusion.8
  696.2 2.4 fusion.10
  698.6 0.4 copy.48
  699.0 0.3 stack_reshape.7
  699.4 0.8 copy.49
  700.2 4.4 all_to_all.18
  704.6 0.2 copy.50
  704.8 103.7 %all-gather.8.cloned.1.call-done = bf16[2048,2048]{1,0:T(8,128)(2,1)} async-done(((bf16[256,2048]{1,0:T(8,128)(2,1)}), bf16[2048,2048]{1,0:T(8,128)(2,1)}) %all-gather.8.cloned.1.call-update) | async-done | bytes 8388624 | tf_op jit(solution)/shard_map/all_gather | solution.py:74
  808.5 6.1 fusion.2
  (36 shorter events, 0.5 us)
Async XLA Ops:
  6.5 5.9 copy-start
  6.5 245.2 %all-reduce.5.cloned.1.call-start = ((), (), s32[]{:S(2)}) async-start(), calls=%async_computation.4 | async-start | bytes 12582912
  9.6 5.2 copy-start.6
  12.4 6.4 copy-start.8
  14.8 5.7 copy-start.7
  18.8 3.4 copy-start.10
  18.8 3.4 copy-start.11
  22.2 1.1 copy-start.3
  37.6 2.8 copy-start.9
  37.6 311.3 %all-gather.4.cloned.1.call-start = ((), (), s32[]{:S(2)}) async-start(), calls=%async_computation.1 | async-start | bytes 3538944 | tf_op jit(solution)/shard_map/all_gather | solution.py:63
  42.3 249.0 %copy-start.1 = (f32[1,192,1024]{2,1,0:T(8,128)S(1)}, f32[1,192,1024]{2,1,0:T(8,128)}, u32[]{:S(2)}) copy-start(f32[1,192,1024]{2,1,0:T(8,128)} %get-tuple-element.13) | copy-start | bytes 2359300
  42.3 250.5 %copy-start.4 = (bf16[1,192,1024]{2,1,0:T(8,128)(2,1)S(1)}, bf16[1,192,1024]{2,1,0:T(8,128)(2,1)}, u32[]{:S(2)}) copy-start(bf16[1,192,1024]{2,1,0:T(8,128)(2,1)} %get-tuple-element.15) | copy-start | bytes 1179652
  291.1 294.6 %all-reduce.7.cloned.1.call-start = ((), (), s32[]{:S(2)}) async-start(), calls=%async_computation.5 | async-start | bytes 12582912
  358.6 1.1 copy-start.2
  375.6 307.4 %all-gather.6.cloned.1.call-start = ((), (), s32[]{:S(2)}) async-start(), calls=%async_computation.2 | async-start | bytes 3538944 | tf_op jit(solution)/shard_map/all_gather | solution.py:63
  625.1 183.4 %all-gather.8.cloned.1.call-start = ((), (), s32[]{:S(2)}) async-start(), calls=%async_computation.3 | async-start | bytes 9437184 | tf_op jit(solution)/shard_map/all_gather | solution.py:74
  692.2 4.0 copy-start.5
Sparse Core Ops, SparseCore 0:
  37.8 213.9 all-reduce.4
  291.2 57.6 all-gather.3
  375.7 209.8 all-reduce.6
  625.2 57.6 all-gather.5
  684.9 123.5 all-gather.7
where the time goes:
time: 822 us; the launch traced here: 821 us
  waiting for transfers between devices  626 us (76%)
  blocking collectives  74.7 us (9%)
  local copies, waits for them, and re-layouts  61 us (7%)
  matrix products  27.2 us (3%)
  other arithmetic  17.2 us (2%)
  between operations  14.1 us (2%)
    unnamed x7, waiting for transfers between devices  420 us
    all_gather x1, waiting for transfers between devices, local(): lax.all_gather(out_proj, 'seq', axis=0, tiled=True)  104 us
    all_gather x2, waiting for transfers between devices, local(): current = lax.all_gather(fresh, 'seq', axis=3, tiled=True)  103 us
    psum x2, blocking collectives, local(): squares = lax.psum(jnp.sum(own * own, axis=-1, keepdims=True), 'seq')  70.3 us
    another operation x2, local copies, waits for them, and re-layouts, local_update(): jnp.stack([jnp.einsum('thg,thi->hgi', grad_gate, keys_local, preferred_el...  20.6 us
  transfers between devices with their start and end apart: 5, of which 5 were waited for; matrix products, arithmetic and copies ran while one was open for 4% of the time, Pallas kernels for 0%

commit v1 on v0

--- a/solution.py
+++ b/solution.py
@@ -1,12 +1,25 @@
+import functools
+
 import jax
 import jax.numpy as jnp
 from jax import lax
+from jax.experimental import pallas as pl
+from jax.experimental.pallas import tpu as pltpu
 from jax.sharding import PartitionSpec as P
+
+VMEM_LIMIT = 40 * 1024 * 1024
+BOTH = ("seq", "head")
 
 
 def silu_parts(value):
     sigma = jax.nn.sigmoid(value)
     return (value * sigma, sigma * (1.0 + value * (1.0 - sigma)))
+
+
+def dot(left, right, left_dim, right_dim):
+    return lax.dot_general(
+        left, right, (((left_dim,), (right_dim,)), ((), ())), preferred_element_type=jnp.float32
+    )
 
 
 def local_update(weights, keys_local, values_local, rates_local):
@@ -42,7 +55,7 @@
     return produced.astype(jnp.bfloat16).reshape(queries_local.shape[0], -1)
 
 
-def local(queries, keys, values, rates, fast_init, out_proj):
+def local_summed(queries, keys, values, rates, fast_init, out_proj):
     block_count, tok_count, width_here = queries.shape
     heads_here = fast_init.shape[1]
     head_width = fast_init.shape[2]
@@ -77,6 +90,272 @@
     return result.astype(jnp.bfloat16)
 
 
+def pack_kernel(place, keys, values, rates, *messages):
+    half, width = messages[0].shape[1:]
+    row = place[0]
+    for turn, message in enumerate(messages):
+        want = row ^ turn
+        head_bit, half_bit = want >> 1, want & 1
+        rows = pl.ds(pl.multiple_of(half_bit * half, half), half)
+        cols = pl.ds(pl.multiple_of(head_bit * width, width), width)
+        message[0] = keys[0, rows, cols]
+        rate = rates[0, rows, :]
+        rate = jnp.where(head_bit == 0, rate[:, 0:1], rate[:, 1:2])
+        message[1] = (rate * values[0, rows, cols].astype(jnp.float32)).astype(jnp.bfloat16)
+
+
+def pack_queries_kernel(place, queries, *messages):
+    half, width = messages[0].shape[1:]
+    row = place[0]
+    for turn, message in enumerate(messages):
+        want = row ^ turn
+        head_bit, half_bit = want >> 1, want & 1
+        rows = pl.ds(pl.multiple_of(half_bit * half, half), half)
+        cols = pl.ds(pl.multiple_of(head_bit * width, width), width)
+        for block in range(queries.shape[0]):
+            message[block] = queries[block, rows, cols]
+
+
+def pack(place, block, keys, values, rates):
+    tokens, both = keys.shape[1:]
+    shape = (2, tokens // 2, both // 2)
+    one = lambda arr: pl.BlockSpec((1,) + arr.shape[1:], lambda i, p: (block, 0, 0))
+    whole = pl.BlockSpec(shape, lambda i, p: (0, 0, 0))
+    return pl.pallas_call(
+        pack_kernel,
+        grid_spec=pltpu.PrefetchScalarGridSpec(
+            num_scalar_prefetch=1,
+            grid=(1,),
+            in_specs=[one(keys), one(values), one(rates)],
+            out_specs=[whole] * 4,
+        ),
+        out_shape=[jax.ShapeDtypeStruct(shape, jnp.bfloat16)] * 4,
+        name="pack",
+    )(place, keys, values, rates)
+
+
+def pack_queries(place, queries):
+    blocks, tokens, both = queries.shape
+    shape = (blocks, tokens // 2, both // 2)
+    whole = pl.BlockSpec(shape, lambda i, p: (0, 0, 0))
+    return pl.pallas_call(
+        pack_queries_kernel,
+        grid_spec=pltpu.PrefetchScalarGridSpec(
+            num_scalar_prefetch=1,
+            grid=(1,),
+            in_specs=[pl.BlockSpec(queries.shape, lambda i, p: (0, 0, 0))],
+            out_specs=[whole] * 4,
+        ),
+        out_shape=[jax.ShapeDtypeStruct(shape, jnp.bfloat16)] * 4,
+        name="pack_queries",
+    )(place, queries)
+
+
+def step_kernel(chunks, block, tile, place, *refs):
+    pieces = refs[:chunks]
+    asked = refs[chunks : chunks + 4]
+    weights, target = refs[chunks + 4 : chunks + 6]
+    fresh = refs[chunks + 6]
+    produced = refs[chunks + 7 : chunks + 11]
+    keys, values, hidden, grad_gate, grad_up, queries, sems = refs[chunks + 11 :]
+    half = pieces[0].shape[1]
+    copies = []
+    for idx, piece in enumerate(pieces):
+        rows = pl.ds(idx * half, half)
+        copies.append(pltpu.make_async_copy(piece.at[0], keys.at[rows], sems.at[2 * idx]))
+        copies.append(pltpu.make_async_copy(piece.at[1], values.at[rows], sems.at[2 * idx + 1]))
+    row, core = place[0], place[2]
+    shift = row ^ (2 * (row & 1) + core)
+    for turn, ask in enumerate(asked):
+        rows = pl.ds(pl.multiple_of((shift ^ turn) * half, half), half)
+        copies.append(
+            pltpu.make_async_copy(ask.at[block], queries.at[rows], sems.at[2 * chunks + turn])
+        )
+    for copy in copies:
+        copy.start()
+    for copy in copies:
+        copy.wait()
+
+    total = keys.shape[0]
+    for start in range(0, total, tile):
+        rows = pl.ds(start, tile)
+        key, value = keys[rows], values[rows]
+        gate_pre = dot(key, weights[0], 1, 1)
+        up_pre = dot(key, weights[1], 1, 1)
+        back = dot(value, weights[2], 1, 0)
+        gate_act, gate_slope = silu_parts(gate_pre)
+        hidden[rows] = (gate_act * up_pre).astype(jnp.bfloat16)
+        grad_gate[rows] = (back * up_pre * gate_slope).astype(jnp.bfloat16)
+        grad_up[rows] = (back * gate_act).astype(jnp.bfloat16)
+
+    for idx, (left, right) in enumerate(((grad_gate, keys), (grad_up, keys), (values, hidden))):
+        summed = weights[idx].astype(jnp.float32) + dot(left[...], right[...], 0, 0)
+        mean = jnp.mean(summed * summed, axis=-1, keepdims=True)
+        fresh[idx] = (summed * target[idx] * lax.rsqrt(mean + 1e-06)).astype(jnp.bfloat16)
+
+    query = queries[...]
+    gate_pre = dot(query, fresh[0], 1, 1)
+    up_pre = dot(query, fresh[1], 1, 1)
+    applied = (gate_pre * jax.nn.sigmoid(gate_pre) * up_pre).astype(jnp.bfloat16)
+    out = dot(applied, fresh[2], 1, 1).astype(jnp.bfloat16)
+    for idx, ref in enumerate(produced):
+        ref[...] = out[idx * half : (idx + 1) * half]
+
+
+def step(place, block, pieces, asked, weights, target):
+    half, width = pieces[0].shape[1:]
+    total = half * len(pieces)
+    tile = 256 if total % 256 == 0 else half
+    vmem = pl.BlockSpec(memory_space=pltpu.VMEM)
+    anywhere = pl.BlockSpec(memory_space=pl.ANY)
+    token_buf = pltpu.VMEM((total, width), jnp.bfloat16)
+    flops = 2 * width * width * (6 * total + 12 * half)
+    outs = pl.pallas_call(
+        functools.partial(step_kernel, len(pieces), block, tile),
+        in_specs=[pl.BlockSpec(memory_space=pltpu.SMEM)]
+        + [anywhere] * (len(pieces) + 4)
+        + [vmem, vmem],
+        out_specs=[vmem] * 5,
+        out_shape=[jax.ShapeDtypeStruct(weights.shape, jnp.bfloat16)]
+        + [jax.ShapeDtypeStruct((half, width), jnp.bfloat16)] * 4,
+        scratch_shapes=[token_buf] * 5
+        + [
+            pltpu.VMEM((4 * half, width), jnp.bfloat16),
+            pltpu.SemaphoreType.DMA((2 * len(pieces) + 4,)),
+        ],
+        compiler_params=pltpu.CompilerParams(vmem_limit_bytes=VMEM_LIMIT),
+        cost_estimate=pl.CostEstimate(
+            flops=flops, bytes_accessed=8 * 1024 * 1024, transcendentals=total * width
+        ),
+        name="step",
+    )(place, *pieces, *asked, weights, target)
+    return outs[0], outs[1:]
+
+
+def project_kernel(blocks, place, *refs):
+    slabs = refs[:8]
+    mixed = refs[8 : 8 + 4 * blocks]
+    out, matrix, sems = refs[8 + 4 * blocks :]
+    part = slabs[0].shape[1]
+    line, core, group = place[1], place[2], place[3]
+    copies = []
+    for idx, slab in enumerate(slabs):
+        here_line = line ^ (idx & 1)
+        here_group = group ^ ((idx >> 1) & 1)
+        here_core = core ^ (idx >> 2)
+        at = (here_line * 4 + here_group * 2 + here_core) * part
+        rows = pl.ds(pl.multiple_of(at, part), part)
+        copies.append(pltpu.make_async_copy(slab, matrix.at[:, rows], sems.at[idx]))
+    for copy in copies:
+        copy.start()
+    for copy in copies:
+        copy.wait()
+    for block in range(blocks):
+        total = None
+        for turn in range(4):
+            term = dot(mixed[4 * block + turn][...], matrix[turn], 1, 0)
+            total = term if total is None else total + term
+        out[block] = total.astype(jnp.bfloat16)
+
+
+def project(place, slabs, mixed):
+    blocks = len(mixed) // 4
+    half, width = mixed[0].shape
+    depth = slabs[0].shape[2]
+    vmem = pl.BlockSpec(memory_space=pltpu.VMEM)
+    anywhere = pl.BlockSpec(memory_space=pl.ANY)
+    return pl.pallas_call(
+        functools.partial(project_kernel, blocks),
+        in_specs=[pl.BlockSpec(memory_space=pltpu.SMEM)] + [anywhere] * 8 + [vmem] * len(mixed),
+        out_specs=vmem,
+        out_shape=jax.ShapeDtypeStruct((blocks, half, depth), jnp.bfloat16),
+        scratch_shapes=[
+            pltpu.VMEM((4, width, depth), jnp.bfloat16),
+            pltpu.SemaphoreType.DMA((8,)),
+        ],
+        compiler_params=pltpu.CompilerParams(vmem_limit_bytes=VMEM_LIMIT),
+        cost_estimate=pl.CostEstimate(
+            flops=2 * blocks * half * 4 * width * depth,
+            bytes_accessed=10 * 1024 * 1024,
+            transcendentals=0,
+        ),
+        name="project",
+    )(place, *slabs, *mixed)
+
+
+def routes(rule):
+    pairs = []
+    for row in range(4):
+        for line in range(2):
+            for core in range(2):
+                to_row, to_line, to_core = rule(row, line, core)
+                pairs.append(((row * 2 + line) * 2 + core, (to_row * 2 + to_line) * 2 + to_core))
+    return pairs
+
+
+def spread_rule(turn):
+    def rule(row, line, core):
+        want = row ^ turn
+        return (2 * core + (want >> 1), line, want & 1)
+
+    return rule
+
+
+def swap_line(arr):
+    return lax.ppermute(arr, BOTH, routes(lambda row, line, core: (row, 1 - line, core)))
+
+
+def swap_core(arr):
+    return lax.ppermute(arr, BOTH, routes(lambda row, line, core: (row, line, 1 - core)))
+
+
+def swap_row(arr, turn):
+    return lax.ppermute(arr, BOTH, routes(lambda row, line, core: (row ^ turn, line, core)))
+
+
+def swap_group(arr):
+    return lax.ppermute(arr, "groups", [(0, 1), (1, 0)])
+
+
+def spread(messages):
+    return [
+        lax.ppermute(message, BOTH, routes(spread_rule(turn)))
+        for turn, message in enumerate(messages)
+    ]
+
+
+def local_gathered(queries, keys, values, rates, fast_init, out_proj):
+    block_count = queries.shape[0]
+    seq, core, group = lax.axis_index("seq"), lax.axis_index("head"), lax.axis_index("groups")
+    row, line = seq // 2, seq % 2
+    place = jnp.stack([row, line, core, group]).astype(jnp.int32)
+
+    pieces = []
+    for block in range(block_count):
+        own = spread(pack(place, block, keys, values, rates))
+        lines = own + [swap_line(arr) for arr in own]
+        pieces.append(lines + [swap_core(arr) for arr in lines])
+    asked = spread(pack_queries(place, queries))
+
+    mine = lax.dynamic_index_in_dim(fast_init, row % 2, 1, keepdims=False)
+    weights = jnp.where(core == row // 2, mine, swap_core(mine))
+    init_float = weights.astype(jnp.float32)
+    target = jnp.sqrt(jnp.mean(init_float * init_float, axis=-1, keepdims=True))
+
+    part = out_proj.shape[0] // 4
+    quarter = lax.dynamic_slice_in_dim(out_proj, (2 * group + core) * part, part, 0)
+    slab = jnp.stack([quarter] + [swap_row(quarter, turn) for turn in (1, 2, 3)])
+    slab_line = swap_line(slab)
+    slabs = [slab, slab_line, swap_group(slab), swap_group(slab_line)]
+    slabs = slabs + [swap_core(arr) for arr in slabs]
+
+    mixed = []
+    for block in range(block_count):
+        weights, produced = step(place, block, pieces[block], asked, weights, target)
+        mixed += [produced[0]] + [swap_row(produced[turn], turn) for turn in (1, 2, 3)]
+    return project(place, slabs, mixed)
+
+
 def solution(mesh):
     in_specs = (
         P(None, ("groups", "seq"), "head"),
@@ -87,4 +366,6 @@
         P("seq", None),
     )
     out_specs = P(None, ("groups", "seq", "head"), None)
+    few = dict(mesh.shape) == {"groups": 2, "seq": 8, "head": 2}
+    local = local_gathered if few else local_summed
     return jax.shard_map(local, mesh=mesh, in_specs=in_specs, out_specs=out_specs, check_vma=False)

time: 822 us -> 255 us (0.31)
  waiting for transfers between devices: 626 us -> 108 us
  blocking collectives: 74.7 us -> 0 us
  starting transfers between devices: 0.57 us -> 69.6 us
  Pallas kernels: 0 us -> 38.6 us
  local copies, waits for them, and re-layouts: 61 us -> 33.5 us
  matrix products: 27.2 us -> 0 us
  between operations: 14.1 us -> 0.72 us
  other arithmetic: 17.2 us -> 3.85 us
    unnamed x7 -> x0, waiting for transfers between devices: 420 us -> none
    all_gather x3 -> x0, waiting for transfers between devices: 207 us -> none  [the longest x1 104 us: local(): lax.all_gather(out_proj, 'seq', axis=0, tiled=True)]
    ppermute x0 -> x53, waiting for transfers between devices: none -> 108 us  [the longest x9 38.2 us: swap_line(): lax.ppermute(arr, BOTH, routes(lambda row, line, core: (row, 1 - line, co...]
    psum x2 -> x0, blocking collectives: 70.3 us -> none  [local(): squares = lax.psum(jnp.sum(own * own, axis=-1, keepdims=True), 'seq')]
    ppermute x0 -> x53, starting transfers between devices: none -> 69.6 us  [the longest x12 37.2 us: spread(): lax.ppermute(message, BOTH, routes(spread_rule(turn)))]
    pallas_call x0 -> x6, Pallas kernels: none -> 38.6 us  [the longest x2 23.8 us: step(): pl.pallas_call(functools.partial(step_kernel, len(pieces), block, tile),...]
    dot_general x17 -> x0, matrix products: 27.2 us -> none  [the longest x1 6.06 us: local(): jnp.einsum('ctf,fd->ctd', mixed, lax.all_gather(out_proj, 'seq', axis=0,...]
    another operation x9 -> x1, local copies, waits for them, and re-layouts: 26.3 us -> 0.02 us  [local_gathered(): jnp.stack([quarter] + [swap_row(quarter, turn) for turn in (1, 2, 3)])]
  transfers between devices with their start and end apart: 5 -> 53, of which waited for: 5 -> 20; matrix products, arithmetic and copies ran while one was open for 4% -> 3% of each run, Pallas kernels for 0% -> 12%
where the time goes in v1:
time: 255 us; the launch traced here: 254 us
  waiting for transfers between devices  108 us (42%)
  starting transfers between devices  69.6 us (27%)
  Pallas kernels  38.6 us (15%)
  local copies, waits for them, and re-layouts  33.5 us (13%)
  other arithmetic  3.85 us (2%)
    ppermute x9, waiting for transfers between devices, swap_line(): lax.ppermute(arr, BOTH, routes(lambda row, line, core: (row, 1 - line, co...  38.2 us
    ppermute x12, starting transfers between devices, spread(): lax.ppermute(message, BOTH, routes(spread_rule(turn)))  37.2 us
    unnamed x129, local copies, waits for them, and re-layouts  29.5 us
    ppermute x2, waiting for transfers between devices, swap_group(): return lax.ppermute(arr, 'groups', [(0, 1), (1, 0)])  29.4 us
    pallas_call x2, Pallas kernels, step(): pl.pallas_call(functools.partial(step_kernel, len(pieces), block, tile),...  23.8 us
    ppermute x12, waiting for transfers between devices, spread(): lax.ppermute(message, BOTH, routes(spread_rule(turn)))  23.4 us
    ppermute x9, waiting for transfers between devices, swap_row(): lax.ppermute(arr, BOTH, routes(lambda row, line, core: (row ^ turn, line,...  15.8 us
    ppermute x9, starting transfers between devices, swap_row(): lax.ppermute(arr, BOTH, routes(lambda row, line, core: (row ^ turn, line,...  13.8 us
  transfers between devices with their start and end apart: 53, of which 20 were waited for; matrix products, arithmetic and copies ran while one was open for 3% of the time, Pallas kernels for 12%

profile of v1, /device:TPU:0, one launch (start us, length us, event | category | flops | bytes accessed | tf_op | source)
XLA Modules:
  0.0 254.4 jit_solution(12396804772298499604)
XLA Ops:
  0.0 1.6 copy.9.rates
  2.2 2.8 %pack.2 = (bf16[2,96,512]{2,1,0:T(8,128)(2,1)}, bf16[2,96,512]{2,1,0:T(8,128)(2,1)}, bf16[2,96,512]{2,1,0:T(8,128)(2,1)}, bf16[2,96,512]{2,1,0:T(8,128)(2,1)}) custom-call(s32[4]{0:T(128)} %pad_add_fusion.place, bf16[2,192,1024]{2,1,0:T(8,128)(2,1)} %keys.3, bf16[2,192,1024]{2,1,0:T(8,128)(2,1)} %values.3, f32[2,192,2]{2,1,0:T(8,128)} %copy.9.rates), custom_call_target="tpu_custom_call" | custom-call | tf_op jit(solution)/shard_map/pack/pallas_call | solution.py:124
  5.0 1.6 collective-permute-start.10
  6.6 4.5 %collective-permute-start.11 = (bf16[2,96,512]{2,1,0:T(8,128)(2,1)}, bf16[2,96,512]{2,1,0:T(8,128)(2,1)S(1)}, u32[]{:S(2)}, u32[]{:S(2)}) collective-permute-start(bf16[2,96,512]{2,1,0:T(8,128)(2,1)} %get-tuple-element.27), channel_id=1, source_target_pairs={{0,1},{1,9},{2,3},{3,11},{4,0},{5,8},{6,2},{7,10},{8,5},{9,13},{10... | collective-permute-start | bytes 589832 | tf_op jit(solution)/shard_map/ppermute | solution.py:322
  11.1 3.2 %collective-permute-start.13 = (bf16[2,96,512]{2,1,0:T(8,128)(2,1)}, bf16[2,96,512]{2,1,0:T(8,128)(2,1)S(1)}, u32[]{:S(2)}, u32[]{:S(2)}) collective-permute-start(bf16[2,96,512]{2,1,0:T(8,128)(2,1)} %get-tuple-element.29), channel_id=1, source_target_pairs={{0,5},{1,13},{2,7},{3,15},{4,4},{5,12},{6,6},{7,14},{8,1},{9,9},{1... | collective-permute-start | bytes 589832 | tf_op jit(solution)/shard_map/ppermute | solution.py:322
  14.3 2.7 %pack_queries.1 = (bf16[2,96,512]{2,1,0:T(8,128)(2,1)}, bf16[2,96,512]{2,1,0:T(8,128)(2,1)}, bf16[2,96,512]{2,1,0:T(8,128)(2,1)}, bf16[2,96,512]{2,1,0:T(8,128)(2,1)}) custom-call(s32[4]{0:T(128)} %pad_add_fusion.place, bf16[2,192,1024]{2,1,0:T(8,128)(2,1)} %queries.1), custom_call_target="tpu_custom_call" | custom-call | tf_op jit(solution)/shard_map/pack_queries/pallas_call | solution.py:141
  17.1 1.6 collective-permute-start.26
  18.7 3.3 %collective-permute-start = (bf16[64,2048]{1,0:T(8,128)(2,1)S(1)}, bf16[64,2048]{1,0:T(8,128)(2,1)S(1)}, u32[]{:S(2)}, u32[]{:S(2)}) collective-permute-start(bf16[64,2048]{1,0:T(8,128)(2,1)S(1)} %constant_dynamic-slice_fusion), channel_id=1, source_target_pairs={{0,4},{1,5},{2,6},{3,7},{4,0},{5,1},{6,2},{7,3},{8,12},{9,13},{10,... | collective-permute-start | bytes 786440 | tf_op jit(solution)/shard_map/ppermute | solution.py:313
  22.0 3.8 %collective-permute-start.1 = (bf16[64,2048]{1,0:T(8,128)(2,1)S(1)}, bf16[64,2048]{1,0:T(8,128)(2,1)S(1)}, u32[]{:S(2)}, u32[]{:S(2)}) collective-permute-start(bf16[64,2048]{1,0:T(8,128)(2,1)S(1)} %constant_dynamic-slice_fusion), channel_id=1, source_target_pairs={{0,8},{1,9},{2,10},{3,11},{4,12},{5,13},{6,14},{7,15},{8,0},{9,1},... | collective-permute-start | bytes 786440 | tf_op jit(solution)/shard_map/ppermute | solution.py:313
  25.7 4.4 %collective-permute-done.12.refs_2_ = bf16[2,96,512]{2,1,0:T(8,128)(2,1)S(1)} collective-permute-done((bf16[2,96,512]{2,1,0:T(8,128)(2,1)}, bf16[2,96,512]{2,1,0:T(8,128)(2,1)S(1)}, u32[]{:S(2)}, u32[]{:S(2)}) %collective-permute-start.12) | collective-permute-done | bytes 196640 | tf_op jit(solution)/shard_map/ppermute | solution.py:322
  30.2 2.7 %dynamic-slice_bitcast_fusion = bf16[3,512,512]{2,1,0:T(8,128)(2,1)} fusion(bf16[3,2,512,512]{3,2,1,0:T(8,128)(2,1)} %param.10, s32[]{:T(128)S(6)} %select_n.39), kind=kLoop, calls=%fused_computation.1 | loop fusion | bytes 3145732 | tf_op jit(solution)/shard_map/jit(dynamic_index_in_dim)/squeeze | solution.py:340
  32.9 3.0 %pack.3 = (bf16[2,96,512]{2,1,0:T(8,128)(2,1)}, bf16[2,96,512]{2,1,0:T(8,128)(2,1)}, bf16[2,96,512]{2,1,0:T(8,128)(2,1)}, bf16[2,96,512]{2,1,0:T(8,128)(2,1)}) custom-call(s32[4]{0:T(128)} %pad_add_fusion.place, bf16[2,192,1024]{2,1,0:T(8,128)(2,1)} %keys.3, bf16[2,192,1024]{2,1,0:T(8,128)(2,1)} %values.3, f32[2,192,2]{2,1,0:T(8,128)} %copy.9.rates), custom_call_target="tpu_custom_call" | custom-call | tf_op jit(solution)/shard_map/pack/pallas_call | solution.py:124
  35.9 12.4 %collective-permute-start.27 = (bf16[2,96,512]{2,1,0:T(8,128)(2,1)}, bf16[2,96,512]{2,1,0:T(8,128)(2,1)S(1)}, u32[]{:S(2)}, u32[]{:S(2)}) collective-permute-start(bf16[2,96,512]{2,1,0:T(8,128)(2,1)} %get-tuple-element.31), channel_id=1, source_target_pairs={{0,1},{1,9},{2,3},{3,11},{4,0},{5,8},{6,2},{7,10},{8,5},{9,13},{10... | collective-permute-start | bytes 589832 | tf_op jit(solution)/shard_map/ppermute | solution.py:322
  48.3 5.0 %collective-permute-start.28 = (bf16[2,96,512]{2,1,0:T(8,128)(2,1)S(1)}, bf16[2,96,512]{2,1,0:T(8,128)(2,1)S(1)}, u32[]{:S(2)}, u32[]{:S(2)}) collective-permute-start(bf16[2,96,512]{2,1,0:T(8,128)(2,1)S(1)} %copy-done.62), channel_id=1, source_target_pairs={{0,4},{1,12},{2,6},{3,14},{4,5},{5,13},{6,7},{7,15},{8,0},{9,8},{1... | collective-permute-start | bytes 589832 | tf_op jit(solution)/shard_map/ppermute | solution.py:322
  54.0 11.2 %collective-permute-done.28.refs_18_ = bf16[2,96,512]{2,1,0:T(8,128)(2,1)S(1)} collective-permute-done((bf16[2,96,512]{2,1,0:T(8,128)(2,1)S(1)}, bf16[2,96,512]{2,1,0:T(8,128)(2,1)S(1)}, u32[]{:S(2)}, u32[]{:S(2)}) %collective-permute-start.28) | collective-permute-done | bytes 196640 | tf_op jit(solution)/shard_map/ppermute | solution.py:322
  65.8 1.9 collective-permute-start.29
  67.7 1.6 collective-permute-start.34
  69.3 1.3 collective-permute-start.35
  70.6 1.7 collective-permute-start.36
  72.4 2.9 %collective-permute-done.29.refs_19_ = bf16[2,96,512]{2,1,0:T(8,128)(2,1)S(1)} collective-permute-done((bf16[2,96,512]{2,1,0:T(8,128)(2,1)S(1)}, bf16[2,96,512]{2,1,0:T(8,128)(2,1)S(1)}, u32[]{:S(2)}, u32[]{:S(2)}) %collective-permute-start.29) | collective-permute-done | bytes 196640 | tf_op jit(solution)/shard_map/ppermute | solution.py:322
  76.0 1.5 collective-permute-start.3
  77.6 2.5 collective-permute-start.37
  80.1 1.6 collective-permute-start.14
  81.7 4.9 %collective-permute-done.36.refs_2_ = bf16[2,96,512]{2,1,0:T(8,128)(2,1)S(1)} collective-permute-done((bf16[2,96,512]{2,1,0:T(8,128)(2,1)}, bf16[2,96,512]{2,1,0:T(8,128)(2,1)S(1)}, u32[]{:S(2)}, u32[]{:S(2)}) %collective-permute-start.36) | collective-permute-done | bytes 196640 | tf_op jit(solution)/shard_map/ppermute | solution.py:322
  86.6 2.7 %collective-permute-start.15 = (bf16[2,96,512]{2,1,0:T(8,128)(2,1)S(1)}, bf16[2,96,512]{2,1,0:T(8,128)(2,1)}, u32[]{:S(2)}, u32[]{:S(2)}) collective-permute-start(bf16[2,96,512]{2,1,0:T(8,128)(2,1)S(1)} %copy-done.6), channel_id=1, source_target_pairs={{0,2},{1,3},{2,0},{3,1},{4,6},{5,7},{6,4},{7,5},{8,10},{9,11},{10,... | collective-permute-start | bytes 589832 | tf_op jit(solution)/shard_map/ppermute | solution.py:305
  89.4 17.1 %collective-permute-done.14.refs_4_ = bf16[2,96,512]{2,1,0:T(8,128)(2,1)} collective-permute-done((bf16[2,96,512]{2,1,0:T(8,128)(2,1)S(1)}, bf16[2,96,512]{2,1,0:T(8,128)(2,1)}, u32[]{:S(2)}, u32[]{:S(2)}) %collective-permute-start.14) | collective-permute-done | bytes 196640 | tf_op jit(solution)/shard_map/ppermute | solution.py:305
  106.5 1.5 collective-permute-start.17
  108.0 2.7 %collective-permute-done.15.refs_5_ = bf16[2,96,512]{2,1,0:T(8,128)(2,1)} collective-permute-done((bf16[2,96,512]{2,1,0:T(8,128)(2,1)S(1)}, bf16[2,96,512]{2,1,0:T(8,128)(2,1)}, u32[]{:S(2)}, u32[]{:S(2)}) %collective-permute-start.15) | collective-permute-done | bytes 196640 | tf_op jit(solution)/shard_map/ppermute | solution.py:305
  110.7 4.1 %collective-permute-done.16.refs_6_ = bf16[2,96,512]{2,1,0:T(8,128)(2,1)S(1)} collective-permute-done((bf16[2,96,512]{2,1,0:T(8,128)(2,1)S(1)}, bf16[2,96,512]{2,1,0:T(8,128)(2,1)S(1)}, u32[]{:S(2)}, u32[]{:S(2)}) %collective-permute-start.16) | collective-permute-done | bytes 196640 | tf_op jit(solution)/shard_map/ppermute | solution.py:305
  114.8 2.7 %collective-permute-done.17.refs_7_ = bf16[2,96,512]{2,1,0:T(8,128)(2,1)S(1)} collective-permute-done((bf16[2,96,512]{2,1,0:T(8,128)(2,1)S(1)}, bf16[2,96,512]{2,1,0:T(8,128)(2,1)S(1)}, u32[]{:S(2)}, u32[]{:S(2)}) %collective-permute-start.17) | collective-permute-done | bytes 196640 | tf_op jit(solution)/shard_map/ppermute | solution.py:305
  119.3 1.5 collective-permute-start.38
  122.7 1.5 collective-permute-start.40
  124.2 2.9 %collective-permute-done.38.refs_4_ = bf16[2,96,512]{2,1,0:T(8,128)(2,1)S(1)} collective-permute-done((bf16[2,96,512]{2,1,0:T(8,128)(2,1)S(1)}, bf16[2,96,512]{2,1,0:T(8,128)(2,1)S(1)}, u32[]{:S(2)}, u32[]{:S(2)}) %collective-permute-start.38) | collective-permute-done | bytes 196640 | tf_op jit(solution)/shard_map/ppermute | solution.py:305
  127.1 1.5 collective-permute-start.41
  128.6 2.8 %collective-permute-done.39.refs_5_ = bf16[2,96,512]{2,1,0:T(8,128)(2,1)} collective-permute-done((bf16[2,96,512]{2,1,0:T(8,128)(2,1)S(1)}, bf16[2,96,512]{2,1,0:T(8,128)(2,1)}, u32[]{:S(2)}, u32[]{:S(2)}) %collective-permute-start.39) | collective-permute-done | bytes 196640 | tf_op jit(solution)/shard_map/ppermute | solution.py:305
  132.1 3.5 %collective-permute-done.40.refs_6_ = bf16[2,96,512]{2,1,0:T(8,128)(2,1)} collective-permute-done((bf16[2,96,512]{2,1,0:T(8,128)(2,1)S(1)}, bf16[2,96,512]{2,1,0:T(8,128)(2,1)}, u32[]{:S(2)}, u32[]{:S(2)}) %collective-permute-start.40) | collective-permute-done | bytes 196640 | tf_op jit(solution)/shard_map/ppermute | solution.py:305
  136.3 2.5 collective-permute-done.41.refs_7_
  138.8 1.5 collective-permute-start.4
  147.9 3.1 %multiply_reduce_fusion = (f32[3,512]{1,0:T(4,128)S(1)}, bf16[3,512,512]{2,1,0:T(8,128)(2,1)}) fusion(bf16[3,512,512]{2,1,0:T(8,128)(2,1)} %collective-permute-done.30, pred[]{:T(512)S(6)} %eq.6, bf16[3,2,512,512]{3,2,1,0:T(8,128)(2,1)} %param.10, s32[]{:T(128)S(6)} %select_n.39), kind=kLoop, calls=%fused_computation | loop fusion | flops 3144192 | bytes 4724741 | tf_op jit(solution)/shard_map/reduce_sum | solution.py:343
  154.5 1.2 copy.10.refs_21_
  156.3 8.8 %collective-permute-done.4.refs_2_ = bf16[4,64,2048]{2,1,0:T(8,128)(2,1)} collective-permute-done((bf16[4,64,2048]{2,1,0:T(8,128)(2,1)S(1)}, bf16[4,64,2048]{2,1,0:T(8,128)(2,1)}, u32[]{:S(2)}, u32[]{:S(2)}) %collective-permute-start.4) | collective-permute-done | bytes 1048608 | tf_op jit(solution)/shard_map/ppermute | solution.py:317
  165.0 20.6 %collective-permute-done.5.refs_3_ = bf16[4,64,2048]{2,1,0:T(8,128)(2,1)} collective-permute-done((bf16[4,64,2048]{2,1,0:T(8,128)(2,1)S(1)}, bf16[4,64,2048]{2,1,0:T(8,128)(2,1)}, u32[]{:S(2)}, u32[]{:S(2)}) %collective-permute-start.5) | collective-permute-done | bytes 1048608 | tf_op jit(solution)/shard_map/ppermute | solution.py:317
  185.7 1.4 copy-done.1
  187.1 1.1 copy-done.2
  189.1 0.9 copy-done.10
  190.1 0.9 copy-done.13
  191.0 0.9 copy-done.15
  191.9 0.9 copy-done.18
  192.8 0.9 copy-done.21
  193.8 0.9 copy-done.32
  195.6 0.9 copy-done.36
  196.5 0.9 copy-done.40
  197.5 0.9 copy-done.42
  198.4 0.9 copy-done.44
  199.3 0.9 copy-done.58
  201.3 11.5 %step.2 = (bf16[3,512,512]{2,1,0:T(8,128)(2,1)S(1)}, bf16[96,512]{1,0:T(8,128)(2,1)S(1)}, bf16[96,512]{1,0:T(8,128)(2,1)S(1)}, bf16[96,512]{1,0:T(8,128)(2,1)S(1)}, bf16[96,512]{1,0:T(8,128)(2,1)S(1)}) custom-call(s32[4]{0:T(128)S(1)} %copy-done.4, bf16[2,96,512]{2,1,0:T(8,128)(2,1)S(1)} %collective-permute-done.10.refs_0_, ...), custom_call_target="tpu_custom_call" | custom-call | flops 5435817984 | bytes 8388608 | tf_op jit(solution)/shard_map/step/pallas_call | solution.py:213
  213.0 12.3 %step.3 = (bf16[3,512,512]{2,1,0:T(8,128)(2,1)}, bf16[96,512]{1,0:T(8,128)(2,1)S(1)}, bf16[96,512]{1,0:T(8,128)(2,1)S(1)}, bf16[96,512]{1,0:T(8,128)(2,1)S(1)}, bf16[96,512]{1,0:T(8,128)(2,1)S(1)}) custom-call(s32[4]{0:T(128)S(1)} %copy-done.4, bf16[2,96,512]{2,1,0:T(8,128)(2,1)S(1)} %copy-done.24, bf16[2,96,512]{2,1,0:T(8,128)(2,1)S(1)} %copy-done.26, ...), custom_call_target="tpu_custom_call" | custom-call | flops 5435817984 | bytes 8388608 | tf_op jit(solution)/shard_map/step/pallas_call | solution.py:213
  225.4 2.9 %collective-permute-start.51 = (bf16[96,512]{1,0:T(8,128)(2,1)S(1)}, bf16[96,512]{1,0:T(8,128)(2,1)S(1)}, u32[]{:S(2)}, u32[]{:S(2)}) collective-permute-start(bf16[96,512]{1,0:T(8,128)(2,1)S(1)} %get-tuple-element.45), channel_id=1, source_target_pairs={{0,8},{1,9},{2,10},{3,11},{4,12},{5,13},{6,14},{7,15},{8,0},{9,1},... | collective-permute-start | bytes 294920 | tf_op jit(solution)/shard_map/ppermute | solution.py:313
  228.3 4.1 %collective-permute-done.50.refs_13_ = bf16[96,512]{1,0:T(8,128)(2,1)S(1)} collective-permute-done((bf16[96,512]{1,0:T(8,128)(2,1)S(1)}, bf16[96,512]{1,0:T(8,128)(2,1)S(1)}, u32[]{:S(2)}, u32[]{:S(2)}) %collective-permute-start.50) | collective-permute-done | bytes 98336 | tf_op jit(solution)/shard_map/ppermute | solution.py:313
  232.4 1.7 collective-permute-start.52
  234.1 5.6 %collective-permute-done.52.refs_15_ = bf16[96,512]{1,0:T(8,128)(2,1)S(1)} collective-permute-done((bf16[96,512]{1,0:T(8,128)(2,1)S(1)}, bf16[96,512]{1,0:T(8,128)(2,1)S(1)}, u32[]{:S(2)}, u32[]{:S(2)}) %collective-permute-start.52) | collective-permute-done | bytes 98336 | tf_op jit(solution)/shard_map/ppermute | solution.py:313
  240.3 2.1 collective-permute-start.33
  242.4 5.5 %collective-permute-done.32.refs_10_ = bf16[96,512]{1,0:T(8,128)(2,1)S(1)} collective-permute-done((bf16[96,512]{1,0:T(8,128)(2,1)S(1)}, bf16[96,512]{1,0:T(8,128)(2,1)S(1)}, u32[]{:S(2)}, u32[]{:S(2)}) %collective-permute-start.32) | collective-permute-done | bytes 98336 | tf_op jit(solution)/shard_map/ppermute | solution.py:313
  247.9 6.3 %project.1 = bf16[2,96,2048]{2,1,0:T(8,128)(2,1)} custom-call(s32[4]{0:T(128)S(1)} %copy-done.4, bf16[4,64,2048]{2,1,0:T(8,128)(2,1)S(1)} %pad_maximum_fusion.refs_0_, bf16[4,64,2048]{2,1,0:T(8,128)(2,1)S(1)} %collective-permute-done.3.refs_1_, bf16[4,64,2048]{2,1,0:T(8,128)(2,1)} %collective-permute-done.4.refs_2_, ...), custom_call_target="tpu_custom_call" | custom-call | flops 1610612736 | bytes 10485760 | tf_op jit(solution)/shard_map/project/pallas_call | solution.py:267
  (185 shorter events, 23.3 us)
Async XLA Ops:
  0.0 18.6 %copy-start = (bf16[256,2048]{1,0:T(8,128)(2,1)S(1)}, bf16[256,2048]{1,0:T(8,128)(2,1)}, u32[]{:S(2)}) copy-start(bf16[256,2048]{1,0:T(8,128)(2,1)} %param.11) | copy-start | bytes 3145732
  5.0 13.7 %collective-permute-start.10 = (bf16[2,96,512]{2,1,0:T(8,128)(2,1)}, bf16[2,96,512]{2,1,0:T(8,128)(2,1)S(1)}, u32[]{:S(2)}, u32[]{:S(2)}) collective-permute-start(bf16[2,96,512]{2,1,0:T(8,128)(2,1)} %get-tuple-element.26), channel_id=1, source_target_pairs={{0,0},{1,8},{2,2},{3,10},{4,1},{5,9},{6,3},{7,11},{8,4},{9,12},{10... | collective-permute-start | bytes 589832 | tf_op jit(solution)/shard_map/ppermute | solution.py:322
  6.6 15.4 %collective-permute-start.11 = (bf16[2,96,512]{2,1,0:T(8,128)(2,1)}, bf16[2,96,512]{2,1,0:T(8,128)(2,1)S(1)}, u32[]{:S(2)}, u32[]{:S(2)}) collective-permute-start(bf16[2,96,512]{2,1,0:T(8,128)(2,1)} %get-tuple-element.27), channel_id=1, source_target_pairs={{0,1},{1,9},{2,3},{3,11},{4,0},{5,8},{6,2},{7,10},{8,5},{9,13},{10... | collective-permute-start | bytes 589832 | tf_op jit(solution)/shard_map/ppermute | solution.py:322
  11.1 19.0 %collective-permute-start.12 = (bf16[2,96,512]{2,1,0:T(8,128)(2,1)}, bf16[2,96,512]{2,1,0:T(8,128)(2,1)S(1)}, u32[]{:S(2)}, u32[]{:S(2)}) collective-permute-start(bf16[2,96,512]{2,1,0:T(8,128)(2,1)} %get-tuple-element.28), channel_id=1, source_target_pairs={{0,4},{1,12},{2,6},{3,14},{4,5},{5,13},{6,7},{7,15},{8,0},{9,8},{1... | collective-permute-start | bytes 589832 | tf_op jit(solution)/shard_map/ppermute | solution.py:322
  11.1 24.8 %collective-permute-start.13 = (bf16[2,96,512]{2,1,0:T(8,128)(2,1)}, bf16[2,96,512]{2,1,0:T(8,128)(2,1)S(1)}, u32[]{:S(2)}, u32[]{:S(2)}) collective-permute-start(bf16[2,96,512]{2,1,0:T(8,128)(2,1)} %get-tuple-element.29), channel_id=1, source_target_pairs={{0,5},{1,13},{2,7},{3,15},{4,4},{5,12},{6,6},{7,14},{8,1},{9,9},{1... | collective-permute-start | bytes 589832 | tf_op jit(solution)/shard_map/ppermute | solution.py:322
  17.1 31.2 %collective-permute-start.26 = (bf16[2,96,512]{2,1,0:T(8,128)(2,1)}, bf16[2,96,512]{2,1,0:T(8,128)(2,1)S(1)}, u32[]{:S(2)}, u32[]{:S(2)}) collective-permute-start(bf16[2,96,512]{2,1,0:T(8,128)(2,1)} %get-tuple-element.30), channel_id=1, source_target_pairs={{0,0},{1,8},{2,2},{3,10},{4,1},{5,9},{6,3},{7,11},{8,4},{9,12},{10... | collective-permute-start | bytes 589832 | tf_op jit(solution)/shard_map/ppermute | solution.py:322
  18.7 49.0 %collective-permute-start = (bf16[64,2048]{1,0:T(8,128)(2,1)S(1)}, bf16[64,2048]{1,0:T(8,128)(2,1)S(1)}, u32[]{:S(2)}, u32[]{:S(2)}) collective-permute-start(bf16[64,2048]{1,0:T(8,128)(2,1)S(1)} %constant_dynamic-slice_fusion), channel_id=1, source_target_pairs={{0,4},{1,5},{2,6},{3,7},{4,0},{5,1},{6,2},{7,3},{8,12},{9,13},{10,... | collective-permute-start | bytes 786440 | tf_op jit(solution)/shard_map/ppermute | solution.py:313
  22.0 47.3 %collective-permute-start.1 = (bf16[64,2048]{1,0:T(8,128)(2,1)S(1)}, bf16[64,2048]{1,0:T(8,128)(2,1)S(1)}, u32[]{:S(2)}, u32[]{:S(2)}) collective-permute-start(bf16[64,2048]{1,0:T(8,128)(2,1)S(1)} %constant_dynamic-slice_fusion), channel_id=1, source_target_pairs={{0,8},{1,9},{2,10},{3,11},{4,12},{5,13},{6,14},{7,15},{8,0},{9,1},... | collective-permute-start | bytes 786440 | tf_op jit(solution)/shard_map/ppermute | solution.py:313
  30.2 40.4 %collective-permute-start.2 = (bf16[64,2048]{1,0:T(8,128)(2,1)S(1)}, bf16[64,2048]{1,0:T(8,128)(2,1)S(1)}, u32[]{:S(2)}, u32[]{:S(2)}) collective-permute-start(bf16[64,2048]{1,0:T(8,128)(2,1)S(1)} %constant_dynamic-slice_fusion), channel_id=1, source_target_pairs={{0,12},{1,13},{2,14},{3,15},{4,8},{5,9},{6,10},{7,11},{8,4},{9,5},... | collective-permute-start | bytes 786440 | tf_op jit(solution)/shard_map/ppermute | solution.py:313
  32.9 32.9 %copy-start.61 = (bf16[2,96,512]{2,1,0:T(8,128)(2,1)S(1)}, bf16[2,96,512]{2,1,0:T(8,128)(2,1)}, u32[]{:S(2)}) copy-start(bf16[2,96,512]{2,1,0:T(8,128)(2,1)} %get-tuple-element.33) | copy-start | bytes 589828
  35.9 41.7 %copy-start.63 = (bf16[2,96,512]{2,1,0:T(8,128)(2,1)S(1)}, bf16[2,96,512]{2,1,0:T(8,128)(2,1)}, u32[]{:S(2)}) copy-start(bf16[2,96,512]{2,1,0:T(8,128)(2,1)} %get-tuple-element.41) | copy-start | bytes 589828
  35.9 50.7 %copy-start.6 = (bf16[2,96,512]{2,1,0:T(8,128)(2,1)S(1)}, bf16[2,96,512]{2,1,0:T(8,128)(2,1)}, u32[]{:S(2)}) copy-start(bf16[2,96,512]{2,1,0:T(8,128)(2,1)} %copy-done.5) | copy-start | bytes 589828
  35.9 53.4 %copy-start.9 = (bf16[2,96,512]{2,1,0:T(8,128)(2,1)S(1)}, bf16[2,96,512]{2,1,0:T(8,128)(2,1)}, u32[]{:S(2)}) copy-start(bf16[2,96,512]{2,1,0:T(8,128)(2,1)} %copy-done.8) | copy-start | bytes 589828
  35.9 36.4 %copy-start.11 = (bf16[2,96,512]{2,1,0:T(8,128)(2,1)}, bf16[2,96,512]{2,1,0:T(8,128)(2,1)S(1)}, u32[]{:S(2)}) copy-start(bf16[2,96,512]{2,1,0:T(8,128)(2,1)S(1)} %collective-permute-done.13.refs_3_) | copy-start | bytes 589828
  35.9 17.4 %collective-permute-start.27 = (bf16[2,96,512]{2,1,0:T(8,128)(2,1)}, bf16[2,96,512]{2,1,0:T(8,128)(2,1)S(1)}, u32[]{:S(2)}, u32[]{:S(2)}) collective-permute-start(bf16[2,96,512]{2,1,0:T(8,128)(2,1)} %get-tuple-element.31), channel_id=1, source_target_pairs={{0,1},{1,9},{2,3},{3,11},{4,0},{5,8},{6,2},{7,10},{8,5},{9,13},{10... | collective-permute-start | bytes 589832 | tf_op jit(solution)/shard_map/ppermute | solution.py:322
  48.3 16.8 %collective-permute-start.28 = (bf16[2,96,512]{2,1,0:T(8,128)(2,1)S(1)}, bf16[2,96,512]{2,1,0:T(8,128)(2,1)S(1)}, u32[]{:S(2)}, u32[]{:S(2)}) collective-permute-start(bf16[2,96,512]{2,1,0:T(8,128)(2,1)S(1)} %copy-done.62), channel_id=1, source_target_pairs={{0,4},{1,12},{2,6},{3,14},{4,5},{5,13},{6,7},{7,15},{8,0},{9,8},{1... | collective-permute-start | bytes 589832 | tf_op jit(solution)/shard_map/ppermute | solution.py:322
  54.0 93.8 %collective-permute-start.30 = (bf16[3,512,512]{2,1,0:T(8,128)(2,1)}, bf16[3,512,512]{2,1,0:T(8,128)(2,1)}, u32[]{:S(2)}, u32[]{:S(2)}) collective-permute-start(bf16[3,512,512]{2,1,0:T(8,128)(2,1)} %dynamic-slice_bitcast_fusion), channel_id=1, source_target_pairs={{0,1},{1,0},{2,3},{3,2},{4,5},{5,4},{6,7},{7,6},{8,9},{9,8},{10,11... | collective-permute-start | bytes 4718600 | tf_op jit(solution)/shard_map/ppermute | solution.py:309
  65.8 9.6 %collective-permute-start.29 = (bf16[2,96,512]{2,1,0:T(8,128)(2,1)S(1)}, bf16[2,96,512]{2,1,0:T(8,128)(2,1)S(1)}, u32[]{:S(2)}, u32[]{:S(2)}) collective-permute-start(bf16[2,96,512]{2,1,0:T(8,128)(2,1)S(1)} %copy-done.61), channel_id=1, source_target_pairs={{0,5},{1,13},{2,7},{3,15},{4,4},{5,12},{6,6},{7,14},{8,1},{9,9},{1... | collective-permute-start | bytes 589832 | tf_op jit(solution)/shard_map/ppermute | solution.py:322
  67.7 9.8 %collective-permute-start.34 = (bf16[2,96,512]{2,1,0:T(8,128)(2,1)}, bf16[2,96,512]{2,1,0:T(8,128)(2,1)S(1)}, u32[]{:S(2)}, u32[]{:S(2)}) collective-permute-start(bf16[2,96,512]{2,1,0:T(8,128)(2,1)} %get-tuple-element.38), channel_id=1, source_target_pairs={{0,0},{1,8},{2,2},{3,10},{4,1},{5,9},{6,3},{7,11},{8,4},{9,12},{10... | collective-permute-start | bytes 589832 | tf_op jit(solution)/shard_map/ppermute | solution.py:322
  69.3 10.8 %collective-permute-start.35 = (bf16[2,96,512]{2,1,0:T(8,128)(2,1)}, bf16[2,96,512]{2,1,0:T(8,128)(2,1)S(1)}, u32[]{:S(2)}, u32[]{:S(2)}) collective-permute-start(bf16[2,96,512]{2,1,0:T(8,128)(2,1)} %get-tuple-element.39), channel_id=1, source_target_pairs={{0,1},{1,9},{2,3},{3,11},{4,0},{5,8},{6,2},{7,10},{8,5},{9,13},{10... | collective-permute-start | bytes 589832 | tf_op jit(solution)/shard_map/ppermute | solution.py:322
  70.6 16.0 %collective-permute-start.36 = (bf16[2,96,512]{2,1,0:T(8,128)(2,1)}, bf16[2,96,512]{2,1,0:T(8,128)(2,1)S(1)}, u32[]{:S(2)}, u32[]{:S(2)}) collective-permute-start(bf16[2,96,512]{2,1,0:T(8,128)(2,1)} %get-tuple-element.40), channel_id=1, source_target_pairs={{0,4},{1,12},{2,6},{3,14},{4,5},{5,13},{6,7},{7,15},{8,0},{9,8},{1... | collective-permute-start | bytes 589832 | tf_op jit(solution)/shard_map/ppermute | solution.py:322
  72.3 34.2 %copy-start.12 = (bf16[2,96,512]{2,1,0:T(8,128)(2,1)S(1)}, bf16[2,96,512]{2,1,0:T(8,128)(2,1)}, u32[]{:S(2)}) copy-start(bf16[2,96,512]{2,1,0:T(8,128)(2,1)} %copy-done.11) | copy-start | bytes 589828
  76.0 64.3 %collective-permute-start.3 = (bf16[4,64,2048]{2,1,0:T(8,128)(2,1)S(1)}, bf16[4,64,2048]{2,1,0:T(8,128)(2,1)S(1)}, u32[]{:S(2)}, u32[]{:S(2)}) collective-permute-start(bf16[4,64,2048]{2,1,0:T(8,128)(2,1)S(1)} %pad_maximum_fusion.refs_0_), channel_id=1, source_target_pairs={{0,2},{1,3},{2,0},{3,1},{4,6},{5,7},{6,4},{7,5},{8,10},{9,11},{10,... | collective-permute-start | bytes 3145736 | tf_op jit(solution)/shard_map/ppermute | solution.py:305
  77.6 11.7 %collective-permute-start.37 = (bf16[2,96,512]{2,1,0:T(8,128)(2,1)S(1)}, bf16[2,96,512]{2,1,0:T(8,128)(2,1)S(1)}, u32[]{:S(2)}, u32[]{:S(2)}) collective-permute-start(bf16[2,96,512]{2,1,0:T(8,128)(2,1)S(1)} %copy-done.63), channel_id=1, source_target_pairs={{0,5},{1,13},{2,7},{3,15},{4,4},{5,12},{6,6},{7,14},{8,1},{9,9},{1... | collective-permute-start | bytes 589832 | tf_op jit(solution)/shard_map/ppermute | solution.py:322
  80.1 26.3 %collective-permute-start.14 = (bf16[2,96,512]{2,1,0:T(8,128)(2,1)S(1)}, bf16[2,96,512]{2,1,0:T(8,128)(2,1)}, u32[]{:S(2)}, u32[]{:S(2)}) collective-permute-start(bf16[2,96,512]{2,1,0:T(8,128)(2,1)S(1)} %collective-permute-done.10.refs_0_), channel_id=1, source_target_pairs={{0,2},{1,3},{2,0},{3,1},{4,6},{5,7},{6,4},{7,5},{8,10},{9,11},{10,... | collective-permute-start | bytes 589832 | tf_op jit(solution)/shard_map/ppermute | solution.py:305
  86.6 24.1 %collective-permute-start.15 = (bf16[2,96,512]{2,1,0:T(8,128)(2,1)S(1)}, bf16[2,96,512]{2,1,0:T(8,128)(2,1)}, u32[]{:S(2)}, u32[]{:S(2)}) collective-permute-start(bf16[2,96,512]{2,1,0:T(8,128)(2,1)S(1)} %copy-done.6), channel_id=1, source_target_pairs={{0,2},{1,3},{2,0},{3,1},{4,6},{5,7},{6,4},{7,5},{8,10},{9,11},{10,... | collective-permute-start | bytes 589832 | tf_op jit(solution)/shard_map/ppermute | solution.py:305
  89.3 25.5 %collective-permute-start.16 = (bf16[2,96,512]{2,1,0:T(8,128)(2,1)S(1)}, bf16[2,96,512]{2,1,0:T(8,128)(2,1)S(1)}, u32[]{:S(2)}, u32[]{:S(2)}) collective-permute-start(bf16[2,96,512]{2,1,0:T(8,128)(2,1)S(1)} %copy-done.9), channel_id=1, source_target_pairs={{0,2},{1,3},{2,0},{3,1},{4,6},{5,7},{6,4},{7,5},{8,10},{9,11},{10,... | collective-permute-start | bytes 589832 | tf_op jit(solution)/shard_map/ppermute | solution.py:305
  106.5 11.0 %collective-permute-start.17 = (bf16[2,96,512]{2,1,0:T(8,128)(2,1)S(1)}, bf16[2,96,512]{2,1,0:T(8,128)(2,1)S(1)}, u32[]{:S(2)}, u32[]{:S(2)}) collective-permute-start(bf16[2,96,512]{2,1,0:T(8,128)(2,1)S(1)} %copy-done.12), channel_id=1, source_target_pairs={{0,2},{1,3},{2,0},{3,1},{4,6},{5,7},{6,4},{7,5},{8,10},{9,11},{10,... | collective-permute-start | bytes 589832 | tf_op jit(solution)/shard_map/ppermute | solution.py:305
  110.7 6.8 %collective-permute-start.18 = (bf16[2,96,512]{2,1,0:T(8,128)(2,1)S(1)}, bf16[2,96,512]{2,1,0:T(8,128)(2,1)S(1)}, u32[]{:S(2)}, u32[]{:S(2)}) collective-permute-start(bf16[2,96,512]{2,1,0:T(8,128)(2,1)S(1)} %collective-permute-done.10.refs_0_), channel_id=1, source_target_pairs={{0,1},{1,0},{2,3},{3,2},{4,5},{5,4},{6,7},{7,6},{8,9},{9,8},{10,11... | collective-permute-start | bytes 589832 | tf_op jit(solution)/shard_map/ppermute | solution.py:309
  114.8 30.0 %copy-start.31 = (bf16[2,96,512]{2,1,0:T(8,128)(2,1)}, bf16[2,96,512]{2,1,0:T(8,128)(2,1)S(1)}, u32[]{:S(2)}) copy-start(bf16[2,96,512]{2,1,0:T(8,128)(2,1)S(1)} %collective-permute-done.16.refs_6_) | copy-start | bytes 589828
  114.8 3.9 %collective-permute-start.19 = (bf16[2,96,512]{2,1,0:T(8,128)(2,1)S(1)}, bf16[2,96,512]{2,1,0:T(8,128)(2,1)S(1)}, u32[]{:S(2)}, u32[]{:S(2)}) collective-permute-start(bf16[2,96,512]{2,1,0:T(8,128)(2,1)S(1)} %copy-done.6), channel_id=1, source_target_pairs={{0,1},{1,0},{2,3},{3,2},{4,5},{5,4},{6,7},{7,6},{8,9},{9,8},{10,11... | collective-permute-start | bytes 589832 | tf_op jit(solution)/shard_map/ppermute | solution.py:309
  117.4 27.4 %copy-start.33 = (bf16[2,96,512]{2,1,0:T(8,128)(2,1)}, bf16[2,96,512]{2,1,0:T(8,128)(2,1)S(1)}, u32[]{:S(2)}) copy-start(bf16[2,96,512]{2,1,0:T(8,128)(2,1)S(1)} %collective-permute-done.17.refs_7_) | copy-start | bytes 589828
  117.4 3.4 %collective-permute-start.20 = (bf16[2,96,512]{2,1,0:T(8,128)(2,1)S(1)}, bf16[2,96,512]{2,1,0:T(8,128)(2,1)S(1)}, u32[]{:S(2)}, u32[]{:S(2)}) collective-permute-start(bf16[2,96,512]{2,1,0:T(8,128)(2,1)S(1)} %copy-done.9), channel_id=1, source_target_pairs={{0,1},{1,0},{2,3},{3,2},{4,5},{5,4},{6,7},{7,6},{8,9},{9,8},{10,11... | collective-permute-start | bytes 589832 | tf_op jit(solution)/shard_map/ppermute | solution.py:309
  118.2 3.9 %collective-permute-start.21 = (bf16[2,96,512]{2,1,0:T(8,128)(2,1)S(1)}, bf16[2,96,512]{2,1,0:T(8,128)(2,1)S(1)}, u32[]{:S(2)}, u32[]{:S(2)}) collective-permute-start(bf16[2,96,512]{2,1,0:T(8,128)(2,1)S(1)} %copy-done.12), channel_id=1, source_target_pairs={{0,1},{1,0},{2,3},{3,2},{4,5},{5,4},{6,7},{7,6},{8,9},{9,8},{10,11... | collective-permute-start | bytes 589832 | tf_op jit(solution)/shard_map/ppermute | solution.py:309
  119.3 7.8 %collective-permute-start.38 = (bf16[2,96,512]{2,1,0:T(8,128)(2,1)S(1)}, bf16[2,96,512]{2,1,0:T(8,128)(2,1)S(1)}, u32[]{:S(2)}, u32[]{:S(2)}) collective-permute-start(bf16[2,96,512]{2,1,0:T(8,128)(2,1)S(1)} %collective-permute-done.34.refs_0_), channel_id=1, source_target_pairs={{0,2},{1,3},{2,0},{3,1},{4,6},{5,7},{6,4},{7,5},{8,10},{9,11},{10,... | collective-permute-start | bytes 589832 | tf_op jit(solution)/shard_map/ppermute | solution.py:305
  121.5 9.9 %collective-permute-start.39 = (bf16[2,96,512]{2,1,0:T(8,128)(2,1)S(1)}, bf16[2,96,512]{2,1,0:T(8,128)(2,1)}, u32[]{:S(2)}, u32[]{:S(2)}) collective-permute-start(bf16[2,96,512]{2,1,0:T(8,128)(2,1)S(1)} %collective-permute-done.35.refs_1_), channel_id=1, source_target_pairs={{0,2},{1,3},{2,0},{3,1},{4,6},{5,7},{6,4},{7,5},{8,10},{9,11},{10,... | collective-permute-start | bytes 589832 | tf_op jit(solution)/shard_map/ppermute | solution.py:305
  122.7 12.9 %collective-permute-start.40 = (bf16[2,96,512]{2,1,0:T(8,128)(2,1)S(1)}, bf16[2,96,512]{2,1,0:T(8,128)(2,1)}, u32[]{:S(2)}, u32[]{:S(2)}) collective-permute-start(bf16[2,96,512]{2,1,0:T(8,128)(2,1)S(1)} %collective-permute-done.36.refs_2_), channel_id=1, source_target_pairs={{0,2},{1,3},{2,0},{3,1},{4,6},{5,7},{6,4},{7,5},{8,10},{9,11},{10,... | collective-permute-start | bytes 589832 | tf_op jit(solution)/shard_map/ppermute | solution.py:305
  127.1 17.7 %copy-start.37 = (bf16[2,96,512]{2,1,0:T(8,128)(2,1)}, bf16[2,96,512]{2,1,0:T(8,128)(2,1)S(1)}, u32[]{:S(2)}) copy-start(bf16[2,96,512]{2,1,0:T(8,128)(2,1)S(1)} %collective-permute-done.38.refs_4_) | copy-start | bytes 589828
  127.1 11.7 %collective-permute-start.41 = (bf16[2,96,512]{2,1,0:T(8,128)(2,1)S(1)}, bf16[2,96,512]{2,1,0:T(8,128)(2,1)S(1)}, u32[]{:S(2)}, u32[]{:S(2)}) collective-permute-start(bf16[2,96,512]{2,1,0:T(8,128)(2,1)S(1)} %collective-permute-done.37.refs_3_), channel_id=1, source_target_pairs={{0,2},{1,3},{2,0},{3,1},{4,6},{5,7},{6,4},{7,5},{8,10},{9,11},{10,... | collective-permute-start | bytes 589832 | tf_op jit(solution)/shard_map/ppermute | solution.py:305
  131.4 9.4 %collective-permute-start.42 = (bf16[2,96,512]{2,1,0:T(8,128)(2,1)S(1)}, bf16[2,96,512]{2,1,0:T(8,128)(2,1)S(1)}, u32[]{:S(2)}, u32[]{:S(2)}) collective-permute-start(bf16[2,96,512]{2,1,0:T(8,128)(2,1)S(1)} %collective-permute-done.34.refs_0_), channel_id=1, source_target_pairs={{0,1},{1,0},{2,3},{3,2},{4,5},{5,4},{6,7},{7,6},{8,9},{9,8},{10,11... | collective-permute-start | bytes 589832 | tf_op jit(solution)/shard_map/ppermute | solution.py:309
  135.6 6.6 %collective-permute-start.43 = (bf16[2,96,512]{2,1,0:T(8,128)(2,1)S(1)}, bf16[2,96,512]{2,1,0:T(8,128)(2,1)S(1)}, u32[]{:S(2)}, u32[]{:S(2)}) collective-permute-start(bf16[2,96,512]{2,1,0:T(8,128)(2,1)S(1)} %collective-permute-done.35.refs_1_), channel_id=1, source_target_pairs={{0,1},{1,0},{2,3},{3,2},{4,5},{5,4},{6,7},{7,6},{8,9},{9,8},{10,11... | collective-permute-start | bytes 589832 | tf_op jit(solution)/shard_map/ppermute | solution.py:309
  138.8 26.2 %collective-permute-start.4 = (bf16[4,64,2048]{2,1,0:T(8,128)(2,1)S(1)}, bf16[4,64,2048]{2,1,0:T(8,128)(2,1)}, u32[]{:S(2)}, u32[]{:S(2)}) collective-permute-start(bf16[4,64,2048]{2,1,0:T(8,128)(2,1)S(1)} %pad_maximum_fusion.refs_0_), channel_id=1, source_target_pairs={{0,16},{16,0},{1,17},{17,1},{2,18},{18,2},{3,19},{19,3},{4,20},{20... | collective-permute-start | bytes 3145736 | tf_op jit(solution)/shard_map/ppermute | solution.py:317
  140.3 45.3 %collective-permute-start.5 = (bf16[4,64,2048]{2,1,0:T(8,128)(2,1)S(1)}, bf16[4,64,2048]{2,1,0:T(8,128)(2,1)}, u32[]{:S(2)}, u32[]{:S(2)}) collective-permute-start(bf16[4,64,2048]{2,1,0:T(8,128)(2,1)S(1)} %collective-permute-done.3.refs_1_), channel_id=1, source_target_pairs={{0,16},{16,0},{1,17},{17,1},{2,18},{18,2},{3,19},{19,3},{4,20},{20... | collective-permute-start | bytes 3145736 | tf_op jit(solution)/shard_map/ppermute | solution.py:317
  141.5 2.6 %collective-permute-start.44 = (bf16[2,96,512]{2,1,0:T(8,128)(2,1)S(1)}, bf16[2,96,512]{2,1,0:T(8,128)(2,1)S(1)}, u32[]{:S(2)}, u32[]{:S(2)}) collective-permute-start(bf16[2,96,512]{2,1,0:T(8,128)(2,1)S(1)} %collective-permute-done.36.refs_2_), channel_id=1, source_target_pairs={{0,1},{1,0},{2,3},{3,2},{4,5},{5,4},{6,7},{7,6},{8,9},{9,8},{10,11... | collective-permute-start | bytes 589832 | tf_op jit(solution)/shard_map/ppermute | solution.py:309
  142.9 1.9 collective-permute-start.45
  144.8 1.8 collective-permute-start.22
  145.5 1.9 collective-permute-start.23
  146.0 39.6 %copy-start.4 = (s32[4]{0:T(128)S(1)}, s32[4]{0:T(128)}, u32[]{:S(2)}) copy-start(s32[4]{0:T(128)} %pad_add_fusion.place) | copy-start | bytes 52
  146.6 4.5 %collective-permute-start.24 = (bf16[2,96,512]{2,1,0:T(8,128)(2,1)}, bf16[2,96,512]{2,1,0:T(8,128)(2,1)S(1)}, u32[]{:S(2)}, u32[]{:S(2)}) collective-permute-start(bf16[2,96,512]{2,1,0:T(8,128)(2,1)} %copy-done.31), channel_id=1, source_target_pairs={{0,1},{1,0},{2,3},{3,2},{4,5},{5,4},{6,7},{7,6},{8,9},{9,8},{10,11... | collective-permute-start | bytes 589832 | tf_op jit(solution)/shard_map/ppermute | solution.py:309
  147.4 5.2 %collective-permute-start.25 = (bf16[2,96,512]{2,1,0:T(8,128)(2,1)}, bf16[2,96,512]{2,1,0:T(8,128)(2,1)S(1)}, u32[]{:S(2)}, u32[]{:S(2)}) collective-permute-start(bf16[2,96,512]{2,1,0:T(8,128)(2,1)} %copy-done.33), channel_id=1, source_target_pairs={{0,1},{1,0},{2,3},{3,2},{4,5},{5,4},{6,7},{7,6},{8,9},{9,8},{10,11... | collective-permute-start | bytes 589832 | tf_op jit(solution)/shard_map/ppermute | solution.py:309
  147.8 5.5 %collective-permute-start.46 = (bf16[2,96,512]{2,1,0:T(8,128)(2,1)}, bf16[2,96,512]{2,1,0:T(8,128)(2,1)S(1)}, u32[]{:S(2)}, u32[]{:S(2)}) collective-permute-start(bf16[2,96,512]{2,1,0:T(8,128)(2,1)} %copy-done.37), channel_id=1, source_target_pairs={{0,1},{1,0},{2,3},{3,2},{4,5},{5,4},{6,7},{7,6},{8,9},{9,8},{10,11... | collective-permute-start | bytes 589832 | tf_op jit(solution)/shard_map/ppermute | solution.py:309
  151.8 73.6 %collective-permute-start.6 = (bf16[4,64,2048]{2,1,0:T(8,128)(2,1)S(1)}, bf16[4,64,2048]{2,1,0:T(8,128)(2,1)}, u32[]{:S(2)}, u32[]{:S(2)}) collective-permute-start(bf16[4,64,2048]{2,1,0:T(8,128)(2,1)S(1)} %pad_maximum_fusion.refs_0_), channel_id=1, source_target_pairs={{0,1},{1,0},{2,3},{3,2},{4,5},{5,4},{6,7},{7,6},{8,9},{9,8},{10,11... | collective-permute-start | bytes 3145736 | tf_op jit(solution)/shard_map/ppermute | solution.py:309
  153.3 2.4 collective-permute-start.47
  154.0 1.9 collective-permute-start.48
  155.7 57.1 %collective-permute-start.49 = (bf16[2,96,512]{2,1,0:T(8,128)(2,1)}, bf16[2,96,512]{2,1,0:T(8,128)(2,1)S(1)}, u32[]{:S(2)}, u32[]{:S(2)}) collective-permute-start(bf16[2,96,512]{2,1,0:T(8,128)(2,1)} %copy-done.45), channel_id=1, source_target_pairs={{0,1},{1,0},{2,3},{3,2},{4,5},{5,4},{6,7},{7,6},{8,9},{9,8},{10,11... | collective-permute-start | bytes 589832 | tf_op jit(solution)/shard_map/ppermute | solution.py:309
  155.9 92.0 %collective-permute-start.7 = (bf16[4,64,2048]{2,1,0:T(8,128)(2,1)S(1)}, bf16[4,64,2048]{2,1,0:T(8,128)(2,1)S(1)}, u32[]{:S(2)}, u32[]{:S(2)}) collective-permute-start(bf16[4,64,2048]{2,1,0:T(8,128)(2,1)S(1)} %collective-permute-done.3.refs_1_), channel_id=1, source_target_pairs={{0,1},{1,0},{2,3},{3,2},{4,5},{5,4},{6,7},{7,6},{8,9},{9,8},{10,11... | collective-permute-start | bytes 3145736 | tf_op jit(solution)/shard_map/ppermute | solution.py:309
  165.0 82.9 %collective-permute-start.8 = (bf16[4,64,2048]{2,1,0:T(8,128)(2,1)}, bf16[4,64,2048]{2,1,0:T(8,128)(2,1)S(1)}, u32[]{:S(2)}, u32[]{:S(2)}) collective-permute-start(bf16[4,64,2048]{2,1,0:T(8,128)(2,1)} %collective-permute-done.4.refs_2_), channel_id=1, source_target_pairs={{0,1},{1,0},{2,3},{3,2},{4,5},{5,4},{6,7},{7,6},{8,9},{9,8},{10,11... | collective-permute-start | bytes 3145736 | tf_op jit(solution)/shard_map/ppermute | solution.py:309
  185.6 62.3 %collective-permute-start.9 = (bf16[4,64,2048]{2,1,0:T(8,128)(2,1)}, bf16[4,64,2048]{2,1,0:T(8,128)(2,1)S(1)}, u32[]{:S(2)}, u32[]{:S(2)}) collective-permute-start(bf16[4,64,2048]{2,1,0:T(8,128)(2,1)} %collective-permute-done.5.refs_3_), channel_id=1, source_target_pairs={{0,1},{1,0},{2,3},{3,2},{4,5},{5,4},{6,7},{7,6},{8,9},{9,8},{10,11... | collective-permute-start | bytes 3145736 | tf_op jit(solution)/shard_map/ppermute | solution.py:309
  225.3 7.1 %collective-permute-start.50 = (bf16[96,512]{1,0:T(8,128)(2,1)S(1)}, bf16[96,512]{1,0:T(8,128)(2,1)S(1)}, u32[]{:S(2)}, u32[]{:S(2)}) collective-permute-start(bf16[96,512]{1,0:T(8,128)(2,1)S(1)} %get-tuple-element.44), channel_id=1, source_target_pairs={{0,4},{1,5},{2,6},{3,7},{4,0},{5,1},{6,2},{7,3},{8,12},{9,13},{10,... | collective-permute-start | bytes 294920 | tf_op jit(solution)/shard_map/ppermute | solution.py:313
  225.4 8.7 %collective-permute-start.51 = (bf16[96,512]{1,0:T(8,128)(2,1)S(1)}, bf16[96,512]{1,0:T(8,128)(2,1)S(1)}, u32[]{:S(2)}, u32[]{:S(2)}) collective-permute-start(bf16[96,512]{1,0:T(8,128)(2,1)S(1)} %get-tuple-element.45), channel_id=1, source_target_pairs={{0,8},{1,9},{2,10},{3,11},{4,12},{5,13},{6,14},{7,15},{8,0},{9,1},... | collective-permute-start | bytes 294920 | tf_op jit(solution)/shard_map/ppermute | solution.py:313
  232.4 7.3 %collective-permute-start.52 = (bf16[96,512]{1,0:T(8,128)(2,1)S(1)}, bf16[96,512]{1,0:T(8,128)(2,1)S(1)}, u32[]{:S(2)}, u32[]{:S(2)}) collective-permute-start(bf16[96,512]{1,0:T(8,128)(2,1)S(1)} %get-tuple-element.46), channel_id=1, source_target_pairs={{0,12},{1,13},{2,14},{3,15},{4,8},{5,9},{6,10},{7,11},{8,4},{9,5},... | collective-permute-start | bytes 294920 | tf_op jit(solution)/shard_map/ppermute | solution.py:313
  234.1 6.2 %collective-permute-start.31 = (bf16[96,512]{1,0:T(8,128)(2,1)S(1)}, bf16[96,512]{1,0:T(8,128)(2,1)S(1)}, u32[]{:S(2)}, u32[]{:S(2)}) collective-permute-start(bf16[96,512]{1,0:T(8,128)(2,1)S(1)} %get-tuple-element.35), channel_id=1, source_target_pairs={{0,4},{1,5},{2,6},{3,7},{4,0},{5,1},{6,2},{7,3},{8,12},{9,13},{10,... | collective-permute-start | bytes 294920 | tf_op jit(solution)/shard_map/ppermute | solution.py:313
  239.7 8.2 %collective-permute-start.32 = (bf16[96,512]{1,0:T(8,128)(2,1)S(1)}, bf16[96,512]{1,0:T(8,128)(2,1)S(1)}, u32[]{:S(2)}, u32[]{:S(2)}) collective-permute-start(bf16[96,512]{1,0:T(8,128)(2,1)S(1)} %get-tuple-element.36), channel_id=1, source_target_pairs={{0,8},{1,9},{2,10},{3,11},{4,12},{5,13},{6,14},{7,15},{8,0},{9,1},... | collective-permute-start | bytes 294920 | tf_op jit(solution)/shard_map/ppermute | solution.py:313
  240.3 7.6 %collective-permute-start.33 = (bf16[96,512]{1,0:T(8,128)(2,1)S(1)}, bf16[96,512]{1,0:T(8,128)(2,1)S(1)}, u32[]{:S(2)}, u32[]{:S(2)}) collective-permute-start(bf16[96,512]{1,0:T(8,128)(2,1)S(1)} %get-tuple-element.37), channel_id=1, source_target_pairs={{0,12},{1,13},{2,14},{3,15},{4,8},{5,9},{6,10},{7,11},{8,4},{9,5},... | collective-permute-start | bytes 294920 | tf_op jit(solution)/shard_map/ppermute | solution.py:313
  (53 other events, 237.7 us)

commit v2 on v1

--- a/solution.py
+++ b/solution.py
@@ -90,65 +90,91 @@
     return result.astype(jnp.bfloat16)
 
 
-def pack_kernel(place, keys, values, rates, *messages):
-    half, width = messages[0].shape[1:]
+def pack_kernel(place, queries, keys, values, rates, *refs):
+    packed, asked = refs[:8], refs[8:12]
+    keys_in, values_in, queries_in, load_sems, sems = refs[12:]
+    half, width = asked[0].shape[1:]
     row = place[0]
-    for turn, message in enumerate(messages):
+    blocks = keys_in.shape[0]
+    loads = []
+    for block in range(blocks):
+        for source, target in ((keys, keys_in), (values, values_in), (queries, queries_in)):
+            sem = load_sems.at[len(loads)]
+            loads.append(pltpu.make_async_copy(source.at[block], target.at[block], sem))
+            loads[-1].start()
+    spots = []
+    for turn in range(4):
         want = row ^ turn
-        head_bit, half_bit = want >> 1, want & 1
-        rows = pl.ds(pl.multiple_of(half_bit * half, half), half)
-        cols = pl.ds(pl.multiple_of(head_bit * width, width), width)
-        message[0] = keys[0, rows, cols]
-        rate = rates[0, rows, :]
-        rate = jnp.where(head_bit == 0, rate[:, 0:1], rate[:, 1:2])
-        message[1] = (rate * values[0, rows, cols].astype(jnp.float32)).astype(jnp.bfloat16)
-
-
-def pack_queries_kernel(place, queries, *messages):
-    half, width = messages[0].shape[1:]
-    row = place[0]
-    for turn, message in enumerate(messages):
-        want = row ^ turn
-        head_bit, half_bit = want >> 1, want & 1
-        rows = pl.ds(pl.multiple_of(half_bit * half, half), half)
-        cols = pl.ds(pl.multiple_of(head_bit * width, width), width)
-        for block in range(queries.shape[0]):
-            message[block] = queries[block, rows, cols]
-
-
-def pack(place, block, keys, values, rates):
-    tokens, both = keys.shape[1:]
-    shape = (2, tokens // 2, both // 2)
-    one = lambda arr: pl.BlockSpec((1,) + arr.shape[1:], lambda i, p: (block, 0, 0))
-    whole = pl.BlockSpec(shape, lambda i, p: (0, 0, 0))
+        rows = pl.ds(pl.multiple_of((want & 1) * half, half), half)
+        cols = pl.ds(pl.multiple_of((want >> 1) * width, width), width)
+        spots.append((rows, cols))
+    copies = []
+
+    def send(source, target):
+        copies.append(pltpu.make_async_copy(source, target, sems.at[len(copies)]))
+        copies[-1].start()
+
+    for block in range(blocks):
+        loads[3 * block].wait()
+        for turn, (rows, cols) in enumerate(spots):
+            send(keys_in.at[block, rows, cols], packed[4 * block + turn].at[0])
+        loads[3 * block + 1].wait()
+        rate = rates[block].T
+        for head in range(2):
+            cols = slice(head * width, (head + 1) * width)
+            scaled = rate[:, head : head + 1] * values_in[block, :, cols].astype(jnp.float32)
+            values_in[block, :, cols] = scaled.astype(jnp.bfloat16)
+        for turn, (rows, cols) in enumerate(spots):
+            send(values_in.at[block, rows, cols], packed[4 * block + turn].at[1])
+    for block in range(blocks):
+        loads[3 * block + 2].wait()
+        for turn, (rows, cols) in enumerate(spots):
+            send(queries_in.at[block, rows, cols], asked[turn].at[block])
+    for copy in copies:
+        copy.wait()
+
+
+def pack(place, queries, keys, values, rates):
+    blocks, tokens, both = keys.shape
+    half, width = tokens // 2, both // 2
+    vmem = pl.BlockSpec(memory_space=pltpu.VMEM)
+    hbm = pl.BlockSpec(memory_space=pltpu.HBM)
+    anywhere = pl.BlockSpec(memory_space=pl.ANY)
+    outs = pl.pallas_call(
+        pack_kernel,
+        in_specs=[pl.BlockSpec(memory_space=pltpu.SMEM), hbm, hbm, hbm, vmem],
+        out_specs=[anywhere] * 12,
+        out_shape=[jax.ShapeDtypeStruct((2, half, width), jnp.bfloat16)] * 8
+        + [jax.ShapeDtypeStruct((blocks, half, width), jnp.bfloat16)] * 4,
+        scratch_shapes=[
+            pltpu.VMEM(keys.shape, jnp.bfloat16),
+            pltpu.VMEM(keys.shape, jnp.bfloat16),
+            pltpu.VMEM(keys.shape, jnp.bfloat16),
+            pltpu.SemaphoreType.DMA((3 * blocks,)),
+            pltpu.SemaphoreType.DMA((12 * blocks,)),
+        ],
+        name="pack",
+    )(place, queries, keys, values, rates)
+    return outs[:4], outs[4:8], outs[8:]
+
+
+def collect_kernel(*refs):
+    rounds, out = refs[:4], refs[4]
+    half = rounds[0].shape[1]
+    for idx, message in enumerate(rounds):
+        out[:, idx * half : (idx + 1) * half] = message[...]
+
+
+def collect(rounds):
+    kinds, half, width = rounds[0].shape
+    vmem = pl.BlockSpec(memory_space=pltpu.VMEM)
     return pl.pallas_call(
-        pack_kernel,
-        grid_spec=pltpu.PrefetchScalarGridSpec(
-            num_scalar_prefetch=1,
-            grid=(1,),
-            in_specs=[one(keys), one(values), one(rates)],
-            out_specs=[whole] * 4,
-        ),
-        out_shape=[jax.ShapeDtypeStruct(shape, jnp.bfloat16)] * 4,
-        name="pack",
-    )(place, keys, values, rates)
-
-
-def pack_queries(place, queries):
-    blocks, tokens, both = queries.shape
-    shape = (blocks, tokens // 2, both // 2)
-    whole = pl.BlockSpec(shape, lambda i, p: (0, 0, 0))
-    return pl.pallas_call(
-        pack_queries_kernel,
-        grid_spec=pltpu.PrefetchScalarGridSpec(
-            num_scalar_prefetch=1,
-            grid=(1,),
-            in_specs=[pl.BlockSpec(queries.shape, lambda i, p: (0, 0, 0))],
-            out_specs=[whole] * 4,
-        ),
-        out_shape=[jax.ShapeDtypeStruct(shape, jnp.bfloat16)] * 4,
-        name="pack_queries",
-    )(place, queries)
+        collect_kernel,
+        in_specs=[vmem] * 4,
+        out_specs=vmem,
+        out_shape=jax.ShapeDtypeStruct((kinds, 4 * half, width), jnp.bfloat16),
+        name="collect",
+    )(*rounds)
 
 
 def step_kernel(chunks, block, tile, place, *refs):
@@ -158,10 +184,10 @@
     fresh = refs[chunks + 6]
     produced = refs[chunks + 7 : chunks + 11]
     keys, values, hidden, grad_gate, grad_up, queries, sems = refs[chunks + 11 :]
-    half = pieces[0].shape[1]
+    size, half = pieces[0].shape[1], produced[0].shape[0]
     copies = []
     for idx, piece in enumerate(pieces):
-        rows = pl.ds(idx * half, half)
+        rows = pl.ds(idx * size, size)
         copies.append(pltpu.make_async_copy(piece.at[0], keys.at[rows], sems.at[2 * idx]))
         copies.append(pltpu.make_async_copy(piece.at[1], values.at[rows], sems.at[2 * idx + 1]))
     row, core = place[0], place[2]
@@ -203,11 +229,11 @@
 
 
 def step(place, block, pieces, asked, weights, target):
-    half, width = pieces[0].shape[1:]
-    total = half * len(pieces)
+    half, width = asked[0].shape[1:]
+    total = pieces[0].shape[1] * len(pieces)
     tile = 256 if total % 256 == 0 else half
     vmem = pl.BlockSpec(memory_space=pltpu.VMEM)
-    anywhere = pl.BlockSpec(memory_space=pl.ANY)
+    anywhere = pl.BlockSpec(memory_space=pltpu.HBM)
     token_buf = pltpu.VMEM((total, width), jnp.bfloat16)
     flops = 2 * width * width * (6 * total + 12 * half)
     outs = pl.pallas_call(
@@ -232,55 +258,80 @@
     return outs[0], outs[1:]
 
 
-def project_kernel(blocks, place, *refs):
-    slabs = refs[:8]
-    mixed = refs[8 : 8 + 4 * blocks]
-    out, matrix, sems = refs[8 + 4 * blocks :]
+def place_kernel(place, *refs):
+    shard = refs[0]
+    slabs = refs[1:9]
+    matrix, sems = refs[9:]
     part = slabs[0].shape[1]
     line, core, group = place[1], place[2], place[3]
-    copies = []
+    rows = pl.ds(pl.multiple_of(line * 4 * part, 4 * part), 4 * part)
+    copies = [pltpu.make_async_copy(shard, matrix.at[0, rows], sems.at[8])]
     for idx, slab in enumerate(slabs):
-        here_line = line ^ (idx & 1)
-        here_group = group ^ ((idx >> 1) & 1)
+        here_line = line ^ ((idx >> 1) & 1)
+        here_group = group ^ (idx & 1)
         here_core = core ^ (idx >> 2)
         at = (here_line * 4 + here_group * 2 + here_core) * part
         rows = pl.ds(pl.multiple_of(at, part), part)
-        copies.append(pltpu.make_async_copy(slab, matrix.at[:, rows], sems.at[idx]))
+        turns = pl.ds(4 - slab.shape[0], slab.shape[0])
+        copies.append(pltpu.make_async_copy(slab, matrix.at[turns, rows], sems.at[idx]))
     for copy in copies:
         copy.start()
     for copy in copies:
         copy.wait()
-    for block in range(blocks):
-        total = None
-        for turn in range(4):
-            term = dot(mixed[4 * block + turn][...], matrix[turn], 1, 0)
-            total = term if total is None else total + term
-        out[block] = total.astype(jnp.bfloat16)
-
-
-def project(place, slabs, mixed):
-    blocks = len(mixed) // 4
+
+
+def place_slabs(place, shard, slabs):
+    depth = shard.shape[1]
+    anywhere = pl.BlockSpec(memory_space=pltpu.HBM)
+    return pl.pallas_call(
+        place_kernel,
+        in_specs=[pl.BlockSpec(memory_space=pltpu.SMEM)] + [anywhere] * 9,
+        out_specs=pl.BlockSpec(memory_space=pltpu.VMEM),
+        out_shape=jax.ShapeDtypeStruct((4, 2 * shard.shape[0], depth), jnp.bfloat16),
+        scratch_shapes=[pltpu.SemaphoreType.DMA((9,))],
+        compiler_params=pltpu.CompilerParams(vmem_limit_bytes=VMEM_LIMIT // 2),
+        cost_estimate=pl.CostEstimate(
+            flops=0, bytes_accessed=17 * 1024 * 1024, transcendentals=0
+        ),
+        name="place_slabs",
+    )(place, shard, *slabs)
+
+
+def project_rows(out, mixed, matrix):
+    total = None
+    for turn in range(4):
+        term = dot(mixed[turn][...], matrix[turn], 1, 0)
+        total = term if total is None else total + term
+    out[...] = total.astype(jnp.bfloat16)
+
+
+def first_kernel(*refs):
+    project_rows(refs[5], refs[:4], refs[4])
+
+
+def second_kernel(*refs):
+    mixed, first, matrix, out = refs[:4], refs[4], refs[5], refs[6]
+    out[0] = first[...]
+    project_rows(out.at[1], mixed, matrix)
+
+
+def project(mixed, first, matrix):
     half, width = mixed[0].shape
-    depth = slabs[0].shape[2]
+    depth = matrix.shape[2]
+    shape = (half, depth) if first is None else (2, half, depth)
+    args = (*mixed, matrix) if first is None else (*mixed, first, matrix)
     vmem = pl.BlockSpec(memory_space=pltpu.VMEM)
-    anywhere = pl.BlockSpec(memory_space=pl.ANY)
     return pl.pallas_call(
-        functools.partial(project_kernel, blocks),
-        in_specs=[pl.BlockSpec(memory_space=pltpu.SMEM)] + [anywhere] * 8 + [vmem] * len(mixed),
+        first_kernel if first is None else second_kernel,
+        in_specs=[vmem] * len(args),
         out_specs=vmem,
-        out_shape=jax.ShapeDtypeStruct((blocks, half, depth), jnp.bfloat16),
-        scratch_shapes=[
-            pltpu.VMEM((4, width, depth), jnp.bfloat16),
-            pltpu.SemaphoreType.DMA((8,)),
-        ],
-        compiler_params=pltpu.CompilerParams(vmem_limit_bytes=VMEM_LIMIT),
+        out_shape=jax.ShapeDtypeStruct(shape, jnp.bfloat16),
+        compiler_params=pltpu.CompilerParams(vmem_limit_bytes=VMEM_LIMIT // 2),
         cost_estimate=pl.CostEstimate(
-            flops=2 * blocks * half * 4 * width * depth,
-            bytes_accessed=10 * 1024 * 1024,
-            transcendentals=0,
+            flops=2 * half * 4 * width * depth, bytes_accessed=9 * 1024 * 1024, transcendentals=0
         ),
         name="project",
-    )(place, *slabs, *mixed)
+    )(*args)
 
 
 def routes(rule):
@@ -317,43 +368,72 @@
     return lax.ppermute(arr, "groups", [(0, 1), (1, 0)])
 
 
-def spread(messages):
-    return [
-        lax.ppermute(message, BOTH, routes(spread_rule(turn)))
-        for turn, message in enumerate(messages)
-    ]
+def after(arr, *earlier):
+    return lax.optimization_barrier((arr,) + earlier)[0]
+
+
+class Queue:
+    def __init__(self, depth):
+        self.depth, self.ended = depth, []
+
+    def send(self, swap, arr, *args):
+        if len(self.ended) >= self.depth:
+            arr = after(arr, self.ended[-self.depth])
+        got = swap(arr, *args)
+        self.ended.append(got)
+        return got
+
+
+def spread(message, turn):
+    return lax.ppermute(message, BOTH, routes(spread_rule(turn)))
 
 
 def local_gathered(queries, keys, values, rates, fast_init, out_proj):
-    block_count = queries.shape[0]
     seq, core, group = lax.axis_index("seq"), lax.axis_index("head"), lax.axis_index("groups")
     row, line = seq // 2, seq % 2
     place = jnp.stack([row, line, core, group]).astype(jnp.int32)
-
-    pieces = []
-    for block in range(block_count):
-        own = spread(pack(place, block, keys, values, rates))
-        lines = own + [swap_line(arr) for arr in own]
-        pieces.append(lines + [swap_core(arr) for arr in lines])
-    asked = spread(pack_queries(place, queries))
+    rates = rates.transpose(0, 2, 1)
+    rows = Queue(2)
+
+    part = out_proj.shape[0] // 4
+    quarter = lax.dynamic_slice_in_dim(out_proj, (2 * group + core) * part, part, 0)
+    own_line = swap_line(quarter)
+    slab_rows = [rows.send(swap_row, quarter, 1)]
+    packed = pack(place, queries, keys, values, rates)
+    quarter = after(quarter, packed[0][0])
+    slab_rows += [rows.send(swap_row, quarter, turn) for turn in (2, 3)]
+
+    arrived = [
+        [rows.send(spread, message, turn) for turn, message in enumerate(messages)]
+        for messages in packed
+    ]
+    asked = arrived[2]
 
     mine = lax.dynamic_index_in_dim(fast_init, row % 2, 1, keepdims=False)
     weights = jnp.where(core == row // 2, mine, swap_core(mine))
     init_float = weights.astype(jnp.float32)
     target = jnp.sqrt(jnp.mean(init_float * init_float, axis=-1, keepdims=True))
 
-    part = out_proj.shape[0] // 4
-    quarter = lax.dynamic_slice_in_dim(out_proj, (2 * group + core) * part, part, 0)
-    slab = jnp.stack([quarter] + [swap_row(quarter, turn) for turn in (1, 2, 3)])
-    slab_line = swap_line(slab)
-    slabs = [slab, slab_line, swap_group(slab), swap_group(slab_line)]
-    slabs = slabs + [swap_core(arr) for arr in slabs]
-
-    mixed = []
-    for block in range(block_count):
+    slab = jnp.stack(slab_rows)
+    slab_group = swap_group(slab)
+    slab_line = jnp.concatenate([own_line[None], swap_line(slab)])
+    slab_both = swap_group(slab_line)
+
+    mixed, produced_all, pieces = [], [], []
+    for block in range(2):
+        own = collect(arrived[block])
+        other = swap_line(own)
+        pieces.append([own, swap_core(own), other, swap_core(other)])
+    for block in range(2):
         weights, produced = step(place, block, pieces[block], asked, weights, target)
-        mixed += [produced[0]] + [swap_row(produced[turn], turn) for turn in (1, 2, 3)]
-    return project(place, slabs, mixed)
+        mixed.append(
+            [produced[0]] + [rows.send(swap_row, produced[turn], turn) for turn in (1, 2, 3)]
+        )
+        if block == 0:
+            slabs = [slab, slab_group, slab_line, slab_both]
+            slabs = slabs + [swap_core(after(arr, pieces[1][0])) for arr in slabs]
+    matrix = place_slabs(place, out_proj, slabs)
+    return project(mixed[1], project(mixed[0], None, matrix), matrix)
 
 
 def solution(mesh):

time: 255 us -> 170 us (0.67)
  waiting for transfers between devices: 108 us -> 57.7 us
  local copies, waits for them, and re-layouts: 33.5 us -> 16 us
  starting transfers between devices: 69.6 us -> 58.8 us
  Pallas kernels: 38.6 us -> 33.1 us
    ppermute x9 -> x4, waiting for transfers between devices: 38.2 us -> 0.01 us  [swap_line(): lax.ppermute(arr, BOTH, routes(lambda row, line, core: (row, 1 - line, co...]
    ppermute x2, waiting for transfers between devices: 29.4 us -> 0.01 us  [swap_group(): return lax.ppermute(arr, 'groups', [(0, 1), (1, 0)])]
    unnamed x129 -> x62, local copies, waits for them, and re-layouts: 29.5 us -> 11.1 us
    ppermute x9, waiting for transfers between devices: 15.8 us -> 30.8 us  [swap_row(): lax.ppermute(arr, BOTH, routes(lambda row, line, core: (row ^ turn, line,...]
    ppermute x9 -> x4, starting transfers between devices: 12.5 us -> 4.34 us  [swap_line(): lax.ppermute(arr, BOTH, routes(lambda row, line, core: (row, 1 - line, co...]
    pallas_call x2, Pallas kernels: 23.8 us -> 19.1 us  [step(): pl.pallas_call(functools.partial(step_kernel, len(pieces), block, tile),...]
    ppermute x12, waiting for transfers between devices: 23.4 us -> 26.9 us  [spread(): return lax.ppermute(message, BOTH, routes(spread_rule(turn)))]
    pallas_call x4 -> x6, Pallas kernels: 14.8 us -> 14 us  [the longest x2 4.3 us: collect(): pl.pallas_call(collect_kernel, in_specs=[vmem] * 4, out_specs=vmem, out_s...]
  transfers between devices with their start and end apart: 53 -> 36, of which waited for: 20 -> 11; matrix products, arithmetic and copies ran while one was open for 3% -> 4% of each run, Pallas kernels for 12% -> 18%
where the time goes in v2:
time: 170 us; the launch traced here: 169 us
  starting transfers between devices  58.8 us (35%)
  waiting for transfers between devices  57.7 us (34%)
  Pallas kernels  33.1 us (19%)
  local copies, waits for them, and re-layouts  16 us (9%)
  other arithmetic  2.89 us (2%)
    ppermute x12, starting transfers between devices, spread(): return lax.ppermute(message, BOTH, routes(spread_rule(turn)))  36.5 us
    ppermute x9, waiting for transfers between devices, swap_row(): lax.ppermute(arr, BOTH, routes(lambda row, line, core: (row ^ turn, line,...  30.8 us
    ppermute x12, waiting for transfers between devices, spread(): return lax.ppermute(message, BOTH, routes(spread_rule(turn)))  26.9 us
    pallas_call x2, Pallas kernels, step(): pl.pallas_call(functools.partial(step_kernel, len(pieces), block, tile),...  19.1 us
    ppermute x9, starting transfers between devices, swap_row(): lax.ppermute(arr, BOTH, routes(lambda row, line, core: (row ^ turn, line,...  13.2 us
    unnamed x62, local copies, waits for them, and re-layouts  11.1 us
    ppermute x4, starting transfers between devices, swap_line(): lax.ppermute(arr, BOTH, routes(lambda row, line, core: (row, 1 - line, co...  4.34 us
    pallas_call x2, Pallas kernels, collect(): pl.pallas_call(collect_kernel, in_specs=[vmem] * 4, out_specs=vmem, out_s...  4.3 us
  transfers between devices with their start and end apart: 36, of which 11 were waited for; matrix products, arithmetic and copies ran while one was open for 4% of the time, Pallas kernels for 18%

profile of v2, /device:TPU:0, one launch (start us, length us, event | category | flops | bytes accessed | tf_op | source)
XLA Modules:
  0.0 168.9 jit_solution(6641661853600064430)
XLA Ops:
  0.0 1.0 constant_dynamic-slice_fusion
  1.0 3.1 %collective-permute-start.4 = (bf16[64,2048]{1,0:T(8,128)(2,1)S(1)}, bf16[64,2048]{1,0:T(8,128)(2,1)S(1)}, u32[]{:S(2)}, u32[]{:S(2)}) collective-permute-start(bf16[64,2048]{1,0:T(8,128)(2,1)S(1)} %constant_dynamic-slice_fusion), channel_id=1, source_target_pairs={{0,4},{1,5},{2,6},{3,7},{4,0},{5,1},{6,2},{7,3},{8,12},{9,13},{10,... | collective-permute-start | bytes 786440 | tf_op jit(solution)/shard_map/ppermute | solution.py:364
  4.1 0.7 pad_add_fusion.place
  4.7 3.8 %pack.1 = (bf16[2,96,512]{2,1,0:T(8,128)(2,1)}, bf16[2,96,512]{2,1,0:T(8,128)(2,1)}, bf16[2,96,512]{2,1,0:T(8,128)(2,1)}, bf16[2,96,512]{2,1,0:T(8,128)(2,1)}, b...) custom-call(s32[4]{0:T(128)} %pad_add_fusion.place, ...), custom_call_target="tpu_custom_call" | custom-call | tf_op jit(solution)/shard_map/pack/pallas_call | solution.py:143
  8.5 2.7 %collective-permute-start = (bf16[64,2048]{1,0:T(8,128)(2,1)S(1)}, bf16[64,2048]{1,0:T(8,128)(2,1)S(1)}, u32[]{:S(2)}, u32[]{:S(2)}) collective-permute-start(bf16[64,2048]{1,0:T(8,128)(2,1)S(1)} %constant_dynamic-slice_fusion), channel_id=1, source_target_pairs={{0,8},{1,9},{2,10},{3,11},{4,12},{5,13},{6,14},{7,15},{8,0},{9,1},... | collective-permute-start | bytes 786440 | tf_op jit(solution)/shard_map/ppermute | solution.py:364
  11.2 3.0 %collective-permute-start.5 = (bf16[64,2048]{1,0:T(8,128)(2,1)S(1)}, bf16[64,2048]{1,0:T(8,128)(2,1)S(1)}, u32[]{:S(2)}, u32[]{:S(2)}) collective-permute-start(bf16[64,2048]{1,0:T(8,128)(2,1)S(1)} %constant_dynamic-slice_fusion), channel_id=1, source_target_pairs={{0,12},{1,13},{2,14},{3,15},{4,8},{5,9},{6,10},{7,11},{8,4},{9,5},... | collective-permute-start | bytes 786440 | tf_op jit(solution)/shard_map/ppermute | solution.py:364
  14.1 15.0 %collective-permute-done = bf16[64,2048]{1,0:T(8,128)(2,1)S(1)} collective-permute-done((bf16[64,2048]{1,0:T(8,128)(2,1)S(1)}, bf16[64,2048]{1,0:T(8,128)(2,1)S(1)}, u32[]{:S(2)}, u32[]{:S(2)}) %collective-permute-start) | collective-permute-done | bytes 262176 | tf_op jit(solution)/shard_map/ppermute | solution.py:364
  29.3 1.6 collective-permute-start.30
  30.9 2.7 %dynamic-slice_bitcast_fusion = bf16[3,512,512]{2,1,0:T(8,128)(2,1)} fusion(bf16[3,2,512,512]{3,2,1,0:T(8,128)(2,1)} %param.10, s32[]{:T(128)S(6)} %select_n.39), kind=kLoop, calls=%fused_computation.1 | loop fusion | bytes 3145732 | tf_op jit(solution)/shard_map/jit(dynamic_index_in_dim)/squeeze | solution.py:412
  33.6 0.5 collective-permute-start.29
  34.1 0.7 collective-permute-start.1
  34.8 7.9 %collective-permute-start.6 = (bf16[2,96,512]{2,1,0:T(8,128)(2,1)S(1)}, bf16[2,96,512]{2,1,0:T(8,128)(2,1)S(1)}, u32[]{:S(2)}, u32[]{:S(2)}) collective-permute-start(bf16[2,96,512]{2,1,0:T(8,128)(2,1)S(1)} %copy-done.29), channel_id=1, source_target_pairs={{0,1},{1,9},{2,3},{3,11},{4,0},{5,8},{6,2},{7,10},{8,5},{9,13},{10... | collective-permute-start | bytes 589832 | tf_op jit(solution)/shard_map/ppermute | solution.py:388
  42.7 10.7 %collective-permute-start.2 = (bf16[2,96,512]{2,1,0:T(8,128)(2,1)S(1)}, bf16[2,96,512]{2,1,0:T(8,128)(2,1)S(1)}, u32[]{:S(2)}, u32[]{:S(2)}) collective-permute-start(bf16[2,96,512]{2,1,0:T(8,128)(2,1)S(1)} %copy-done.28), channel_id=1, source_target_pairs={{0,4},{1,12},{2,6},{3,14},{4,5},{5,13},{6,7},{7,15},{8,0},{9,8},{1... | collective-permute-start | bytes 589832 | tf_op jit(solution)/shard_map/ppermute | solution.py:388
  53.4 3.7 %collective-permute-start.7 = (bf16[2,96,512]{2,1,0:T(8,128)(2,1)S(1)}, bf16[2,96,512]{2,1,0:T(8,128)(2,1)}, u32[]{:S(2)}, u32[]{:S(2)}) collective-permute-start(bf16[2,96,512]{2,1,0:T(8,128)(2,1)S(1)} %copy-done.27), channel_id=1, source_target_pairs={{0,5},{1,13},{2,7},{3,15},{4,4},{5,12},{6,6},{7,14},{8,1},{9,9},{1... | collective-permute-start | bytes 589832 | tf_op jit(solution)/shard_map/ppermute | solution.py:388
  57.2 0.1 pad_maximum_fusion.refs_3_
  57.3 1.6 collective-permute-start.31
  58.9 0.7 copy-done.24
  59.5 1.6 collective-permute-start.3
  61.1 3.3 %collective-permute-done.7.refs_3_ = bf16[2,96,512]{2,1,0:T(8,128)(2,1)} collective-permute-done((bf16[2,96,512]{2,1,0:T(8,128)(2,1)S(1)}, bf16[2,96,512]{2,1,0:T(8,128)(2,1)}, u32[]{:S(2)}, u32[]{:S(2)}) %collective-permute-start.7) | collective-permute-done | bytes 196640 | tf_op jit(solution)/shard_map/ppermute | solution.py:388
  64.5 2.2 %collect.3.refs_0_ = bf16[2,384,512]{2,1,0:T(8,128)(2,1)} custom-call(bf16[2,96,512]{2,1,0:T(8,128)(2,1)} %copy-done.21, bf16[2,96,512]{2,1,0:T(8,128)(2,1)} %copy-done.22, bf16[2,96,512]{2,1,0:T(8,128)(2,1)} %copy-done.24, bf16[2,96,512]{2,1,0:T(8,128)(2,1)} %collective-permute-done.7.refs_3_), custom_call_target="tpu_custom_call" | custom-call | tf_op jit(solution)/shard_map/collect/pallas_call | solution.py:171
  66.6 1.5 collective-permute-start.19
  68.2 1.9 %collective-permute-start.9 = (bf16[2,96,512]{2,1,0:T(8,128)(2,1)}, bf16[2,96,512]{2,1,0:T(8,128)(2,1)S(1)}, u32[]{:S(2)}, u32[]{:S(2)}) collective-permute-start(bf16[2,96,512]{2,1,0:T(8,128)(2,1)} %get-tuple-element.65), channel_id=1, source_target_pairs={{0,4},{1,12},{2,6},{3,14},{4,5},{5,13},{6,7},{7,15},{8,0},{9,8},{1... | collective-permute-start | bytes 589832 | tf_op jit(solution)/shard_map/ppermute | solution.py:388
  70.1 9.0 %collective-permute-done.9.refs_2_ = bf16[2,96,512]{2,1,0:T(8,128)(2,1)S(1)} collective-permute-done((bf16[2,96,512]{2,1,0:T(8,128)(2,1)}, bf16[2,96,512]{2,1,0:T(8,128)(2,1)S(1)}, u32[]{:S(2)}, u32[]{:S(2)}) %collective-permute-start.9) | collective-permute-done | bytes 196640 | tf_op jit(solution)/shard_map/ppermute | solution.py:388
  79.1 1.6 collective-permute-start.14
  80.7 4.9 %collective-permute-start.10 = (bf16[2,96,512]{2,1,0:T(8,128)(2,1)}, bf16[2,96,512]{2,1,0:T(8,128)(2,1)S(1)}, u32[]{:S(2)}, u32[]{:S(2)}) collective-permute-start(bf16[2,96,512]{2,1,0:T(8,128)(2,1)} %get-tuple-element.67), channel_id=1, source_target_pairs={{0,5},{1,13},{2,7},{3,15},{4,4},{5,12},{6,6},{7,14},{8,1},{9,9},{1... | collective-permute-start | bytes 589832 | tf_op jit(solution)/shard_map/ppermute | solution.py:388
  85.7 0.7 copy-done.8
  86.3 0.4 collective-permute-start.16
  86.7 5.6 %collective-permute-done.10.refs_3_ = bf16[2,96,512]{2,1,0:T(8,128)(2,1)S(1)} collective-permute-done((bf16[2,96,512]{2,1,0:T(8,128)(2,1)}, bf16[2,96,512]{2,1,0:T(8,128)(2,1)S(1)}, u32[]{:S(2)}, u32[]{:S(2)}) %collective-permute-start.10) | collective-permute-done | bytes 196640 | tf_op jit(solution)/shard_map/ppermute | solution.py:388
  92.3 0.7 copy-done.26
  93.0 2.1 %collect.2.refs_0_ = bf16[2,384,512]{2,1,0:T(8,128)(2,1)} custom-call(bf16[2,96,512]{2,1,0:T(8,128)(2,1)} %copy-done.20, bf16[2,96,512]{2,1,0:T(8,128)(2,1)} %copy-done.25, bf16[2,96,512]{2,1,0:T(8,128)(2,1)} %copy-done.23, bf16[2,96,512]{2,1,0:T(8,128)(2,1)} %copy-done.26), custom_call_target="tpu_custom_call" | custom-call | tf_op jit(solution)/shard_map/collect/pallas_call | solution.py:171
  95.2 0.7 copy-done.11
  95.9 0.7 collective-permute-start.12
  96.6 2.3 %collective-permute-done.15.refs_5_ = bf16[2,96,512]{2,1,0:T(8,128)(2,1)S(1)} collective-permute-done((bf16[2,96,512]{2,1,0:T(8,128)(2,1)}, bf16[2,96,512]{2,1,0:T(8,128)(2,1)S(1)}, u32[]{:S(2)}, u32[]{:S(2)}) %collective-permute-start.15) | collective-permute-done | bytes 196640 | tf_op jit(solution)/shard_map/ppermute | solution.py:388
  98.9 0.7 copy-done.14
  99.6 0.5 collective-permute-start.20
  100.1 3.2 %collective-permute-start.17 = (bf16[2,96,512]{2,1,0:T(8,128)(2,1)}, bf16[2,96,512]{2,1,0:T(8,128)(2,1)S(1)}, u32[]{:S(2)}, u32[]{:S(2)}) collective-permute-start(bf16[2,96,512]{2,1,0:T(8,128)(2,1)} %get-tuple-element.75), channel_id=1, source_target_pairs={{0,5},{1,13},{2,7},{3,15},{4,4},{5,12},{6,6},{7,14},{8,1},{9,9},{1... | collective-permute-start | bytes 589832 | tf_op jit(solution)/shard_map/ppermute | solution.py:388
  103.3 6.6 %collective-permute-done.17.refs_7_ = bf16[2,96,512]{2,1,0:T(8,128)(2,1)S(1)} collective-permute-done((bf16[2,96,512]{2,1,0:T(8,128)(2,1)}, bf16[2,96,512]{2,1,0:T(8,128)(2,1)S(1)}, u32[]{:S(2)}, u32[]{:S(2)}) %collective-permute-start.17) | collective-permute-done | bytes 196640 | tf_op jit(solution)/shard_map/ppermute | solution.py:388
  109.8 0.7 copy-done.17
  110.5 1.2 collective-permute-start.28
  111.7 1.0 copy-done.1
  112.7 0.3 collective-permute-start.11
  113.0 2.0 %multiply_reduce_fusion = (f32[3,512]{1,0:T(4,128)S(1)}, bf16[3,512,512]{2,1,0:T(8,128)(2,1)S(1)}) fusion(bf16[3,512,512]{2,1,0:T(8,128)(2,1)} %collective-permute-done.21, pred[]{:T(512)S(6)} %eq.6, bf16[3,2,512,512]{3,2,1,0:T(8,128)(2,1)} %param.10, s32[]{:T(128)S(6)} %select_n.39), kind=kLoop, calls=%fused_computation | loop fusion | flops 3144192 | bytes 4724741 | tf_op jit(solution)/shard_map/reduce_sum | solution.py:415
  115.0 1.2 copy.7.refs_9_
  116.3 0.7 collective-permute-start.13
  117.1 0.4 collective-permute-start.35
  117.5 1.1 copy-done.3
  118.6 1.1 copy-done.5
  119.8 0.9 copy-done.9
  120.7 0.9 copy-done.12
  121.6 0.9 copy-done.15
  122.6 0.9 copy-done.18
  123.5 9.1 %step.2 = (bf16[3,512,512]{2,1,0:T(8,128)(2,1)S(1)}, bf16[96,512]{1,0:T(8,128)(2,1)S(1)}, bf16[96,512]{1,0:T(8,128)(2,1)S(1)}, bf16[96,512]{1,0:T(8,128)(2,1)S(1)}, bf16[96,512]{1,0:T(8,128)(2,1)S(1)}) custom-call(s32[4]{0:T(128)S(1)} %copy-done.7, bf16[2,384,512]{2,1,0:T(8,128)(2,1)S(1)} %copy-done.3, bf16[2,384,512]{2,1,0:T(8,128)(2,1)} %collective-permute-done.18.refs_1_, ...), custom_call_target="tpu_custom_call" | custom-call | flops 5435817984 | bytes 8388608 | tf_op jit(solution)/shard_map/step/pallas_call | solution.py:239
  132.8 0.4 collective-permute-start.22
  133.1 5.6 %collective-permute-done.24.refs_1_ = bf16[96,512]{1,0:T(8,128)(2,1)S(1)} collective-permute-done((bf16[96,512]{1,0:T(8,128)(2,1)S(1)}, bf16[96,512]{1,0:T(8,128)(2,1)S(1)}, u32[]{:S(2)}, u32[]{:S(2)}) %collective-permute-start.24) | collective-permute-done | bytes 98336 | tf_op jit(solution)/shard_map/ppermute | solution.py:364
  138.7 2.0 %collective-permute-done.22.refs_2_ = bf16[96,512]{1,0:T(8,128)(2,1)S(1)} collective-permute-done((bf16[96,512]{1,0:T(8,128)(2,1)S(1)}, bf16[96,512]{1,0:T(8,128)(2,1)S(1)}, u32[]{:S(2)}, u32[]{:S(2)}) %collective-permute-start.22) | collective-permute-done | bytes 98336 | tf_op jit(solution)/shard_map/ppermute | solution.py:364
  140.7 1.4 collective-permute-start.25
  142.1 10.0 %step.3 = (bf16[3,512,512]{2,1,0:T(8,128)(2,1)}, bf16[96,512]{1,0:T(8,128)(2,1)S(1)}, bf16[96,512]{1,0:T(8,128)(2,1)S(1)}, bf16[96,512]{1,0:T(8,128)(2,1)S(1)}, bf16[96,512]{1,0:T(8,128)(2,1)S(1)}) custom-call(s32[4]{0:T(128)S(1)} %copy-done.7, bf16[2,384,512]{2,1,0:T(8,128)(2,1)S(1)} %copy-done.4, bf16[2,384,512]{2,1,0:T(8,128)(2,1)} %collective-permute-done.11.refs_1_, ...), custom_call_target="tpu_custom_call" | custom-call | flops 5435817984 | bytes 8388608 | tf_op jit(solution)/shard_map/step/pallas_call | solution.py:239
  152.2 4.9 %collective-permute-done.23.refs_1_ = bf16[96,512]{1,0:T(8,128)(2,1)S(1)} collective-permute-done((bf16[96,512]{1,0:T(8,128)(2,1)S(1)}, bf16[96,512]{1,0:T(8,128)(2,1)S(1)}, u32[]{:S(2)}, u32[]{:S(2)}) %collective-permute-start.23) | collective-permute-done | bytes 98336 | tf_op jit(solution)/shard_map/ppermute | solution.py:364
  157.1 1.3 collective-permute-start.26
  158.4 1.4 collective-permute-start.27
  159.8 2.0 %place_slabs.1.refs_4_.refs_5_ = bf16[4,512,2048]{2,1,0:T(8,128)(2,1)S(1)} custom-call(s32[4]{0:T(128)S(1)} %copy-done.7, bf16[256,2048]{1,0:T(8,128)(2,1)S(1)} %copy-done, bf16[3,64,2048]{2,1,0:T(8,128)(2,1)S(1)} %pad_maximum_fusion.1.refs_1_, bf16[3,64,2048]{2,1,0:T(8,128)(2,1)} %collective-permute-done.28.refs_2_, ...), custom_call_target="tpu_custom_call" | custom-call | bytes 17825792 | tf_op jit(solution)/shard_map/place_slabs/pallas_call | solution.py:286
  161.7 1.5 project.2.refs_4_
  163.3 3.3 %collective-permute-done.26.refs_2_ = bf16[96,512]{1,0:T(8,128)(2,1)S(1)} collective-permute-done((bf16[96,512]{1,0:T(8,128)(2,1)S(1)}, bf16[96,512]{1,0:T(8,128)(2,1)S(1)}, u32[]{:S(2)}, u32[]{:S(2)}) %collective-permute-start.26) | collective-permute-done | bytes 98336 | tf_op jit(solution)/shard_map/ppermute | solution.py:364
  166.5 2.4 %project.3 = bf16[2,96,2048]{2,1,0:T(8,128)(2,1)} custom-call(bf16[96,512]{1,0:T(8,128)(2,1)S(1)} %get-tuple-element.77.refs_0_, bf16[96,512]{1,0:T(8,128)(2,1)S(1)} %collective-permute-done.23.refs_1_, bf16[96,512]{1,0:T(8,128)(2,1)S(1)} %collective-permute-done.26.refs_2_, bf16[96,512]{1,0:T(8,128)(2,1)S(1)} %collective-permute-done.27.refs_3_, ...), custom_call_target="tpu_custom_call" | custom-call | flops 805306368 | bytes 9437184 | tf_op jit(solution)/shard_map/project/pallas_call | solution.py:324
  (86 shorter events, 0.5 us)
Async XLA Ops:
  1.0 10.2 %collective-permute-start.4 = (bf16[64,2048]{1,0:T(8,128)(2,1)S(1)}, bf16[64,2048]{1,0:T(8,128)(2,1)S(1)}, u32[]{:S(2)}, u32[]{:S(2)}) collective-permute-start(bf16[64,2048]{1,0:T(8,128)(2,1)S(1)} %constant_dynamic-slice_fusion), channel_id=1, source_target_pairs={{0,4},{1,5},{2,6},{3,7},{4,0},{5,1},{6,2},{7,3},{8,12},{9,13},{10,... | collective-permute-start | bytes 786440 | tf_op jit(solution)/shard_map/ppermute | solution.py:364
  8.5 20.7 %collective-permute-start = (bf16[64,2048]{1,0:T(8,128)(2,1)S(1)}, bf16[64,2048]{1,0:T(8,128)(2,1)S(1)}, u32[]{:S(2)}, u32[]{:S(2)}) collective-permute-start(bf16[64,2048]{1,0:T(8,128)(2,1)S(1)} %constant_dynamic-slice_fusion), channel_id=1, source_target_pairs={{0,8},{1,9},{2,10},{3,11},{4,12},{5,13},{6,14},{7,15},{8,0},{9,1},... | collective-permute-start | bytes 786440 | tf_op jit(solution)/shard_map/ppermute | solution.py:364
  11.2 18.0 %collective-permute-start.5 = (bf16[64,2048]{1,0:T(8,128)(2,1)S(1)}, bf16[64,2048]{1,0:T(8,128)(2,1)S(1)}, u32[]{:S(2)}, u32[]{:S(2)}) collective-permute-start(bf16[64,2048]{1,0:T(8,128)(2,1)S(1)} %constant_dynamic-slice_fusion), channel_id=1, source_target_pairs={{0,12},{1,13},{2,14},{3,15},{4,8},{5,9},{6,10},{7,11},{8,4},{9,5},... | collective-permute-start | bytes 786440 | tf_op jit(solution)/shard_map/ppermute | solution.py:364
  29.3 27.9 %collective-permute-start.30 = (bf16[3,64,2048]{2,1,0:T(8,128)(2,1)S(1)}, bf16[3,64,2048]{2,1,0:T(8,128)(2,1)S(1)}, u32[]{:S(2)}, u32[]{:S(2)}) collective-permute-start(bf16[3,64,2048]{2,1,0:T(8,128)(2,1)S(1)} %pad_maximum_fusion.1.refs_1_), channel_id=1, source_target_pairs={{0,2},{1,3},{2,0},{3,1},{4,6},{5,7},{6,4},{7,5},{8,10},{9,11},{10,... | collective-permute-start | bytes 2359304 | tf_op jit(solution)/shard_map/ppermute | solution.py:356
  30.9 3.2 %copy-start.30 = (bf16[2,96,512]{2,1,0:T(8,128)(2,1)S(1)}, bf16[2,96,512]{2,1,0:T(8,128)(2,1)}, u32[]{:S(2)}) copy-start(bf16[2,96,512]{2,1,0:T(8,128)(2,1)} %get-tuple-element.54) | copy-start | bytes 589828
  30.9 3.9 %copy-start.29 = (bf16[2,96,512]{2,1,0:T(8,128)(2,1)S(1)}, bf16[2,96,512]{2,1,0:T(8,128)(2,1)}, u32[]{:S(2)}) copy-start(bf16[2,96,512]{2,1,0:T(8,128)(2,1)} %get-tuple-element.61) | copy-start | bytes 589828
  30.9 11.8 %copy-start.28 = (bf16[2,96,512]{2,1,0:T(8,128)(2,1)S(1)}, bf16[2,96,512]{2,1,0:T(8,128)(2,1)}, u32[]{:S(2)}) copy-start(bf16[2,96,512]{2,1,0:T(8,128)(2,1)} %get-tuple-element.55) | copy-start | bytes 589828
  30.9 22.5 %copy-start.27 = (bf16[2,96,512]{2,1,0:T(8,128)(2,1)S(1)}, bf16[2,96,512]{2,1,0:T(8,128)(2,1)}, u32[]{:S(2)}) copy-start(bf16[2,96,512]{2,1,0:T(8,128)(2,1)} %get-tuple-element.62) | copy-start | bytes 589828
  33.6 66.4 %collective-permute-start.21 = (bf16[3,512,512]{2,1,0:T(8,128)(2,1)}, bf16[3,512,512]{2,1,0:T(8,128)(2,1)}, u32[]{:S(2)}, u32[]{:S(2)}) collective-permute-start(bf16[3,512,512]{2,1,0:T(8,128)(2,1)} %dynamic-slice_bitcast_fusion), channel_id=1, source_target_pairs={{0,1},{1,0},{2,3},{3,2},{4,5},{5,4},{6,7},{7,6},{8,9},{9,8},{10,11... | collective-permute-start | bytes 4718600 | tf_op jit(solution)/shard_map/ppermute | solution.py:360
  33.6 23.5 %collective-permute-start.29 = (bf16[64,2048]{1,0:T(8,128)(2,1)S(1)}, bf16[64,2048]{1,0:T(8,128)(2,1)S(1)}, u32[]{:S(2)}, u32[]{:S(2)}) collective-permute-start(bf16[64,2048]{1,0:T(8,128)(2,1)S(1)} %constant_dynamic-slice_fusion), channel_id=1, source_target_pairs={{0,2},{1,3},{2,0},{3,1},{4,6},{5,7},{6,4},{7,5},{8,10},{9,11},{10,... | collective-permute-start | bytes 786440 | tf_op jit(solution)/shard_map/ppermute | solution.py:356
  34.1 8.6 %collective-permute-start.1 = (bf16[2,96,512]{2,1,0:T(8,128)(2,1)S(1)}, bf16[2,96,512]{2,1,0:T(8,128)(2,1)S(1)}, u32[]{:S(2)}, u32[]{:S(2)}) collective-permute-start(bf16[2,96,512]{2,1,0:T(8,128)(2,1)S(1)} %copy-done.30), channel_id=1, source_target_pairs={{0,0},{1,8},{2,2},{3,10},{4,1},{5,9},{6,3},{7,11},{8,4},{9,12},{10... | collective-permute-start | bytes 589832 | tf_op jit(solution)/shard_map/ppermute | solution.py:388
  34.8 18.6 %collective-permute-start.6 = (bf16[2,96,512]{2,1,0:T(8,128)(2,1)S(1)}, bf16[2,96,512]{2,1,0:T(8,128)(2,1)S(1)}, u32[]{:S(2)}, u32[]{:S(2)}) collective-permute-start(bf16[2,96,512]{2,1,0:T(8,128)(2,1)S(1)} %copy-done.29), channel_id=1, source_target_pairs={{0,1},{1,9},{2,3},{3,11},{4,0},{5,8},{6,2},{7,10},{8,5},{9,13},{10... | collective-permute-start | bytes 589832 | tf_op jit(solution)/shard_map/ppermute | solution.py:388
  42.7 21.8 %copy-start.21 = (bf16[2,96,512]{2,1,0:T(8,128)(2,1)}, bf16[2,96,512]{2,1,0:T(8,128)(2,1)S(1)}, u32[]{:S(2)}) copy-start(bf16[2,96,512]{2,1,0:T(8,128)(2,1)S(1)} %collective-permute-done.1.refs_0_) | copy-start | bytes 589828
  42.7 16.2 %collective-permute-start.2 = (bf16[2,96,512]{2,1,0:T(8,128)(2,1)S(1)}, bf16[2,96,512]{2,1,0:T(8,128)(2,1)S(1)}, u32[]{:S(2)}, u32[]{:S(2)}) collective-permute-start(bf16[2,96,512]{2,1,0:T(8,128)(2,1)S(1)} %copy-done.28), channel_id=1, source_target_pairs={{0,4},{1,12},{2,6},{3,14},{4,5},{5,13},{6,7},{7,15},{8,0},{9,8},{1... | collective-permute-start | bytes 589832 | tf_op jit(solution)/shard_map/ppermute | solution.py:388
  53.4 11.1 %copy-start.22 = (bf16[2,96,512]{2,1,0:T(8,128)(2,1)}, bf16[2,96,512]{2,1,0:T(8,128)(2,1)S(1)}, u32[]{:S(2)}) copy-start(bf16[2,96,512]{2,1,0:T(8,128)(2,1)S(1)} %collective-permute-done.6.refs_1_) | copy-start | bytes 589828
  53.4 11.0 %collective-permute-start.7 = (bf16[2,96,512]{2,1,0:T(8,128)(2,1)S(1)}, bf16[2,96,512]{2,1,0:T(8,128)(2,1)}, u32[]{:S(2)}, u32[]{:S(2)}) collective-permute-start(bf16[2,96,512]{2,1,0:T(8,128)(2,1)S(1)} %copy-done.27), channel_id=1, source_target_pairs={{0,5},{1,13},{2,7},{3,15},{4,4},{5,12},{6,6},{7,14},{8,1},{9,9},{1... | collective-permute-start | bytes 589832 | tf_op jit(solution)/shard_map/ppermute | solution.py:388
  57.3 54.4 %collective-permute-start.31 = (bf16[4,64,2048]{2,1,0:T(8,128)(2,1)S(1)}, bf16[4,64,2048]{2,1,0:T(8,128)(2,1)S(1)}, u32[]{:S(2)}, u32[]{:S(2)}) collective-permute-start(bf16[4,64,2048]{2,1,0:T(8,128)(2,1)S(1)} %pad_maximum_fusion.refs_3_), channel_id=1, source_target_pairs={{0,16},{16,0},{1,17},{17,1},{2,18},{18,2},{3,19},{19,3},{4,20},{20... | collective-permute-start | bytes 3145736 | tf_op jit(solution)/shard_map/ppermute | solution.py:368
  58.9 0.7 copy-start.24
  59.5 8.6 %collective-permute-start.3 = (bf16[2,96,512]{2,1,0:T(8,128)(2,1)}, bf16[2,96,512]{2,1,0:T(8,128)(2,1)S(1)}, u32[]{:S(2)}, u32[]{:S(2)}) collective-permute-start(bf16[2,96,512]{2,1,0:T(8,128)(2,1)} %get-tuple-element.56), channel_id=1, source_target_pairs={{0,0},{1,8},{2,2},{3,10},{4,1},{5,9},{6,3},{7,11},{8,4},{9,12},{10... | collective-permute-start | bytes 589832 | tf_op jit(solution)/shard_map/ppermute | solution.py:388
  66.6 32.9 %collective-permute-start.19 = (bf16[2,384,512]{2,1,0:T(8,128)(2,1)}, bf16[2,384,512]{2,1,0:T(8,128)(2,1)}, u32[]{:S(2)}, u32[]{:S(2)}) collective-permute-start(bf16[2,384,512]{2,1,0:T(8,128)(2,1)} %collect.3.refs_0_), channel_id=1, source_target_pairs={{0,2},{1,3},{2,0},{3,1},{4,6},{5,7},{6,4},{7,5},{8,10},{9,11},{10,... | collective-permute-start | bytes 2359304 | tf_op jit(solution)/shard_map/ppermute | solution.py:356
  68.2 24.8 %copy-start.20 = (bf16[2,96,512]{2,1,0:T(8,128)(2,1)}, bf16[2,96,512]{2,1,0:T(8,128)(2,1)S(1)}, u32[]{:S(2)}) copy-start(bf16[2,96,512]{2,1,0:T(8,128)(2,1)S(1)} %collective-permute-done.3.refs_0_) | copy-start | bytes 589828
  68.2 11.0 %collective-permute-start.9 = (bf16[2,96,512]{2,1,0:T(8,128)(2,1)}, bf16[2,96,512]{2,1,0:T(8,128)(2,1)S(1)}, u32[]{:S(2)}, u32[]{:S(2)}) collective-permute-start(bf16[2,96,512]{2,1,0:T(8,128)(2,1)} %get-tuple-element.65), channel_id=1, source_target_pairs={{0,4},{1,12},{2,6},{3,14},{4,5},{5,13},{6,7},{7,15},{8,0},{9,8},{1... | collective-permute-start | bytes 589832 | tf_op jit(solution)/shard_map/ppermute | solution.py:388
  70.1 10.6 %collective-permute-start.8 = (bf16[2,96,512]{2,1,0:T(8,128)(2,1)}, bf16[2,96,512]{2,1,0:T(8,128)(2,1)S(1)}, u32[]{:S(2)}, u32[]{:S(2)}) collective-permute-start(bf16[2,96,512]{2,1,0:T(8,128)(2,1)} %get-tuple-element.63), channel_id=1, source_target_pairs={{0,1},{1,9},{2,3},{3,11},{4,0},{5,8},{6,2},{7,10},{8,5},{9,13},{10... | collective-permute-start | bytes 589832 | tf_op jit(solution)/shard_map/ppermute | solution.py:388
  79.1 6.5 %copy-start.23 = (bf16[2,96,512]{2,1,0:T(8,128)(2,1)}, bf16[2,96,512]{2,1,0:T(8,128)(2,1)S(1)}, u32[]{:S(2)}) copy-start(bf16[2,96,512]{2,1,0:T(8,128)(2,1)S(1)} %collective-permute-done.9.refs_2_) | copy-start | bytes 589828
  79.1 6.5 %collective-permute-start.14 = (bf16[2,96,512]{2,1,0:T(8,128)(2,1)}, bf16[2,96,512]{2,1,0:T(8,128)(2,1)S(1)}, u32[]{:S(2)}, u32[]{:S(2)}) collective-permute-start(bf16[2,96,512]{2,1,0:T(8,128)(2,1)} %get-tuple-element.69), channel_id=1, source_target_pairs={{0,0},{1,8},{2,2},{3,10},{4,1},{5,9},{6,3},{7,11},{8,4},{9,12},{10... | collective-permute-start | bytes 589832 | tf_op jit(solution)/shard_map/ppermute | solution.py:388
  80.7 11.6 %copy-start.25 = (bf16[2,96,512]{2,1,0:T(8,128)(2,1)}, bf16[2,96,512]{2,1,0:T(8,128)(2,1)S(1)}, u32[]{:S(2)}) copy-start(bf16[2,96,512]{2,1,0:T(8,128)(2,1)S(1)} %collective-permute-done.8.refs_1_) | copy-start | bytes 589828
  80.7 11.6 %collective-permute-start.10 = (bf16[2,96,512]{2,1,0:T(8,128)(2,1)}, bf16[2,96,512]{2,1,0:T(8,128)(2,1)S(1)}, u32[]{:S(2)}, u32[]{:S(2)}) collective-permute-start(bf16[2,96,512]{2,1,0:T(8,128)(2,1)} %get-tuple-element.67), channel_id=1, source_target_pairs={{0,5},{1,13},{2,7},{3,15},{4,4},{5,12},{6,6},{7,14},{8,1},{9,9},{1... | collective-permute-start | bytes 589832 | tf_op jit(solution)/shard_map/ppermute | solution.py:388
  86.3 8.9 %collective-permute-start.16 = (bf16[2,96,512]{2,1,0:T(8,128)(2,1)}, bf16[2,96,512]{2,1,0:T(8,128)(2,1)S(1)}, u32[]{:S(2)}, u32[]{:S(2)}) collective-permute-start(bf16[2,96,512]{2,1,0:T(8,128)(2,1)} %get-tuple-element.73), channel_id=1, source_target_pairs={{0,4},{1,12},{2,6},{3,14},{4,5},{5,13},{6,7},{7,15},{8,0},{9,8},{1... | collective-permute-start | bytes 589832 | tf_op jit(solution)/shard_map/ppermute | solution.py:388
  93.0 5.9 %collective-permute-start.15 = (bf16[2,96,512]{2,1,0:T(8,128)(2,1)}, bf16[2,96,512]{2,1,0:T(8,128)(2,1)S(1)}, u32[]{:S(2)}, u32[]{:S(2)}) collective-permute-start(bf16[2,96,512]{2,1,0:T(8,128)(2,1)} %get-tuple-element.71), channel_id=1, source_target_pairs={{0,1},{1,9},{2,3},{3,11},{4,0},{5,8},{6,2},{7,10},{8,5},{9,13},{10... | collective-permute-start | bytes 589832 | tf_op jit(solution)/shard_map/ppermute | solution.py:388
  95.2 0.7 copy-start.11
  95.9 20.4 %collective-permute-start.12 = (bf16[2,384,512]{2,1,0:T(8,128)(2,1)}, bf16[2,384,512]{2,1,0:T(8,128)(2,1)}, u32[]{:S(2)}, u32[]{:S(2)}) collective-permute-start(bf16[2,384,512]{2,1,0:T(8,128)(2,1)} %collect.2.refs_0_), channel_id=1, source_target_pairs={{0,2},{1,3},{2,0},{3,1},{4,6},{5,7},{6,4},{7,5},{8,10},{9,11},{10,... | collective-permute-start | bytes 2359304 | tf_op jit(solution)/shard_map/ppermute | solution.py:356
  98.9 0.7 copy-start.14
  99.6 17.4 %collective-permute-start.18 = (bf16[2,384,512]{2,1,0:T(8,128)(2,1)}, bf16[2,384,512]{2,1,0:T(8,128)(2,1)}, u32[]{:S(2)}, u32[]{:S(2)}) collective-permute-start(bf16[2,384,512]{2,1,0:T(8,128)(2,1)} %collect.3.refs_0_), channel_id=1, source_target_pairs={{0,1},{1,0},{2,3},{3,2},{4,5},{5,4},{6,7},{7,6},{8,9},{9,8},{10,11... | collective-permute-start | bytes 2359304 | tf_op jit(solution)/shard_map/ppermute | solution.py:360
  99.6 17.5 %collective-permute-start.20 = (bf16[2,384,512]{2,1,0:T(8,128)(2,1)}, bf16[2,384,512]{2,1,0:T(8,128)(2,1)}, u32[]{:S(2)}, u32[]{:S(2)}) collective-permute-start(bf16[2,384,512]{2,1,0:T(8,128)(2,1)} %collective-permute-done.19.refs_2_), channel_id=1, source_target_pairs={{0,1},{1,0},{2,3},{3,2},{4,5},{5,4},{6,7},{7,6},{8,9},{9,8},{10,11... | collective-permute-start | bytes 2359304 | tf_op jit(solution)/shard_map/ppermute | solution.py:360
  100.1 9.8 %collective-permute-start.17 = (bf16[2,96,512]{2,1,0:T(8,128)(2,1)}, bf16[2,96,512]{2,1,0:T(8,128)(2,1)S(1)}, u32[]{:S(2)}, u32[]{:S(2)}) collective-permute-start(bf16[2,96,512]{2,1,0:T(8,128)(2,1)} %get-tuple-element.75), channel_id=1, source_target_pairs={{0,5},{1,13},{2,7},{3,15},{4,4},{5,12},{6,6},{7,14},{8,1},{9,9},{1... | collective-permute-start | bytes 589832 | tf_op jit(solution)/shard_map/ppermute | solution.py:388
  103.3 14.2 %copy-start.7 = (s32[4]{0:T(128)S(1)}, s32[4]{0:T(128)}, u32[]{:S(2)}) copy-start(s32[4]{0:T(128)} %pad_add_fusion.place) | copy-start | bytes 52
  110.5 22.1 %collective-permute-start.28 = (bf16[3,64,2048]{2,1,0:T(8,128)(2,1)S(1)}, bf16[3,64,2048]{2,1,0:T(8,128)(2,1)}, u32[]{:S(2)}, u32[]{:S(2)}) collective-permute-start(bf16[3,64,2048]{2,1,0:T(8,128)(2,1)S(1)} %pad_maximum_fusion.1.refs_1_), channel_id=1, source_target_pairs={{0,16},{16,0},{1,17},{17,1},{2,18},{18,2},{3,19},{19,3},{4,20},{20... | collective-permute-start | bytes 2359304 | tf_op jit(solution)/shard_map/ppermute | solution.py:368
  111.7 1.0 copy-start.1
  112.7 20.0 %collective-permute-start.11 = (bf16[2,384,512]{2,1,0:T(8,128)(2,1)}, bf16[2,384,512]{2,1,0:T(8,128)(2,1)}, u32[]{:S(2)}, u32[]{:S(2)}) collective-permute-start(bf16[2,384,512]{2,1,0:T(8,128)(2,1)} %collect.2.refs_0_), channel_id=1, source_target_pairs={{0,1},{1,0},{2,3},{3,2},{4,5},{5,4},{6,7},{7,6},{8,9},{9,8},{10,11... | collective-permute-start | bytes 2359304 | tf_op jit(solution)/shard_map/ppermute | solution.py:360
  116.3 24.4 %collective-permute-start.13 = (bf16[2,384,512]{2,1,0:T(8,128)(2,1)}, bf16[2,384,512]{2,1,0:T(8,128)(2,1)S(1)}, u32[]{:S(2)}, u32[]{:S(2)}) collective-permute-start(bf16[2,384,512]{2,1,0:T(8,128)(2,1)} %collective-permute-done.12.refs_2_), channel_id=1, source_target_pairs={{0,1},{1,0},{2,3},{3,2},{4,5},{5,4},{6,7},{7,6},{8,9},{9,8},{10,11... | collective-permute-start | bytes 2359304 | tf_op jit(solution)/shard_map/ppermute | solution.py:360
  117.0 42.7 %collective-permute-start.34 = (bf16[4,64,2048]{2,1,0:T(8,128)(2,1)S(1)}, bf16[4,64,2048]{2,1,0:T(8,128)(2,1)S(1)}, u32[]{:S(2)}, u32[]{:S(2)}) collective-permute-start(bf16[4,64,2048]{2,1,0:T(8,128)(2,1)S(1)} %pad_maximum_fusion.refs_3_), channel_id=1, source_target_pairs={{0,1},{1,0},{2,3},{3,2},{4,5},{5,4},{6,7},{7,6},{8,9},{9,8},{10,11... | collective-permute-start | bytes 3145736 | tf_op jit(solution)/shard_map/ppermute | solution.py:360
  117.1 42.7 %collective-permute-start.35 = (bf16[4,64,2048]{2,1,0:T(8,128)(2,1)}, bf16[4,64,2048]{2,1,0:T(8,128)(2,1)S(1)}, u32[]{:S(2)}, u32[]{:S(2)}) collective-permute-start(bf16[4,64,2048]{2,1,0:T(8,128)(2,1)} %copy-done.1), channel_id=1, source_target_pairs={{0,1},{1,0},{2,3},{3,2},{4,5},{5,4},{6,7},{7,6},{8,9},{9,8},{10,11... | collective-permute-start | bytes 3145736 | tf_op jit(solution)/shard_map/ppermute | solution.py:360
  117.5 1.1 copy-start.3
  118.6 1.1 copy-start.5
  119.8 0.9 copy-start.9
  120.7 0.9 copy-start.12
  121.6 0.9 copy-start.15
  122.6 0.9 copy-start.18
  123.5 18.5 %copy-start.4 = (bf16[2,384,512]{2,1,0:T(8,128)(2,1)S(1)}, bf16[2,384,512]{2,1,0:T(8,128)(2,1)}, u32[]{:S(2)}) copy-start(bf16[2,384,512]{2,1,0:T(8,128)(2,1)} %collect.2.refs_0_) | copy-start | bytes 2359300
  123.5 18.5 %copy-start.6 = (f32[3,512,1]{2,1,0:T(8,128)S(1)}, f32[3,512,1]{2,1,0:T(8,128)}, u32[]{:S(2)}) copy-start(f32[3,512,1]{2,1,0:T(8,128)} %copy.7.refs_9_) | copy-start | bytes 18436
  123.5 18.5 %copy-start.10 = (bf16[2,96,512]{2,1,0:T(8,128)(2,1)S(1)}, bf16[2,96,512]{2,1,0:T(8,128)(2,1)}, u32[]{:S(2)}) copy-start(bf16[2,96,512]{2,1,0:T(8,128)(2,1)} %copy-done.8) | copy-start | bytes 589828
  123.5 18.5 %copy-start.13 = (bf16[2,96,512]{2,1,0:T(8,128)(2,1)S(1)}, bf16[2,96,512]{2,1,0:T(8,128)(2,1)}, u32[]{:S(2)}) copy-start(bf16[2,96,512]{2,1,0:T(8,128)(2,1)} %copy-done.11) | copy-start | bytes 589828
  123.5 18.5 %copy-start.16 = (bf16[2,96,512]{2,1,0:T(8,128)(2,1)S(1)}, bf16[2,96,512]{2,1,0:T(8,128)(2,1)}, u32[]{:S(2)}) copy-start(bf16[2,96,512]{2,1,0:T(8,128)(2,1)} %copy-done.14) | copy-start | bytes 589828
  123.5 18.5 %copy-start.19 = (bf16[2,96,512]{2,1,0:T(8,128)(2,1)S(1)}, bf16[2,96,512]{2,1,0:T(8,128)(2,1)}, u32[]{:S(2)}) copy-start(bf16[2,96,512]{2,1,0:T(8,128)(2,1)} %copy-done.17) | copy-start | bytes 589828
  132.7 6.0 %collective-permute-start.24 = (bf16[96,512]{1,0:T(8,128)(2,1)S(1)}, bf16[96,512]{1,0:T(8,128)(2,1)S(1)}, u32[]{:S(2)}, u32[]{:S(2)}) collective-permute-start(bf16[96,512]{1,0:T(8,128)(2,1)S(1)} %get-tuple-element.85), channel_id=1, source_target_pairs={{0,4},{1,5},{2,6},{3,7},{4,0},{5,1},{6,2},{7,3},{8,12},{9,13},{10,... | collective-permute-start | bytes 294920 | tf_op jit(solution)/shard_map/ppermute | solution.py:364
  132.8 7.9 %collective-permute-start.22 = (bf16[96,512]{1,0:T(8,128)(2,1)S(1)}, bf16[96,512]{1,0:T(8,128)(2,1)S(1)}, u32[]{:S(2)}, u32[]{:S(2)}) collective-permute-start(bf16[96,512]{1,0:T(8,128)(2,1)S(1)} %get-tuple-element.80), channel_id=1, source_target_pairs={{0,8},{1,9},{2,10},{3,11},{4,12},{5,13},{6,14},{7,15},{8,0},{9,1},... | collective-permute-start | bytes 294920 | tf_op jit(solution)/shard_map/ppermute | solution.py:364
  138.7 19.7 %collective-permute-start.32 = (bf16[3,64,2048]{2,1,0:T(8,128)(2,1)S(1)}, bf16[3,64,2048]{2,1,0:T(8,128)(2,1)S(1)}, u32[]{:S(2)}, u32[]{:S(2)}) collective-permute-start(bf16[3,64,2048]{2,1,0:T(8,128)(2,1)S(1)} %pad_maximum_fusion.1.refs_1_), channel_id=1, source_target_pairs={{0,1},{1,0},{2,3},{3,2},{4,5},{5,4},{6,7},{7,6},{8,9},{9,8},{10,11... | collective-permute-start | bytes 2359304 | tf_op jit(solution)/shard_map/ppermute | solution.py:360
  140.6 19.1 %collective-permute-start.33 = (bf16[3,64,2048]{2,1,0:T(8,128)(2,1)}, bf16[3,64,2048]{2,1,0:T(8,128)(2,1)S(1)}, u32[]{:S(2)}, u32[]{:S(2)}) collective-permute-start(bf16[3,64,2048]{2,1,0:T(8,128)(2,1)} %collective-permute-done.28.refs_2_), channel_id=1, source_target_pairs={{0,1},{1,0},{2,3},{3,2},{4,5},{5,4},{6,7},{7,6},{8,9},{9,8},{10,11... | collective-permute-start | bytes 2359304 | tf_op jit(solution)/shard_map/ppermute | solution.py:360
  140.7 11.4 %collective-permute-start.25 = (bf16[96,512]{1,0:T(8,128)(2,1)S(1)}, bf16[96,512]{1,0:T(8,128)(2,1)S(1)}, u32[]{:S(2)}, u32[]{:S(2)}) collective-permute-start(bf16[96,512]{1,0:T(8,128)(2,1)S(1)} %get-tuple-element.86), channel_id=1, source_target_pairs={{0,12},{1,13},{2,14},{3,15},{4,8},{5,9},{6,10},{7,11},{8,4},{9,5},... | collective-permute-start | bytes 294920 | tf_op jit(solution)/shard_map/ppermute | solution.py:364
  142.0 17.7 %copy-start = (bf16[256,2048]{1,0:T(8,128)(2,1)S(1)}, bf16[256,2048]{1,0:T(8,128)(2,1)}, u32[]{:S(2)}) copy-start(bf16[256,2048]{1,0:T(8,128)(2,1)} %refs_0_.1) | copy-start | bytes 3145732
  142.1 17.7 %copy-start.2 = (bf16[4,64,2048]{2,1,0:T(8,128)(2,1)S(1)}, bf16[4,64,2048]{2,1,0:T(8,128)(2,1)}, u32[]{:S(2)}) copy-start(bf16[4,64,2048]{2,1,0:T(8,128)(2,1)} %copy-done.1) | copy-start | bytes 3145732
  152.1 5.0 %collective-permute-start.23 = (bf16[96,512]{1,0:T(8,128)(2,1)S(1)}, bf16[96,512]{1,0:T(8,128)(2,1)S(1)}, u32[]{:S(2)}, u32[]{:S(2)}) collective-permute-start(bf16[96,512]{1,0:T(8,128)(2,1)S(1)} %get-tuple-element.81), channel_id=1, source_target_pairs={{0,4},{1,5},{2,6},{3,7},{4,0},{5,1},{6,2},{7,3},{8,12},{9,13},{10,... | collective-permute-start | bytes 294920 | tf_op jit(solution)/shard_map/ppermute | solution.py:364
  157.1 9.5 %collective-permute-start.26 = (bf16[96,512]{1,0:T(8,128)(2,1)S(1)}, bf16[96,512]{1,0:T(8,128)(2,1)S(1)}, u32[]{:S(2)}, u32[]{:S(2)}) collective-permute-start(bf16[96,512]{1,0:T(8,128)(2,1)S(1)} %get-tuple-element.87), channel_id=1, source_target_pairs={{0,8},{1,9},{2,10},{3,11},{4,12},{5,13},{6,14},{7,15},{8,0},{9,1},... | collective-permute-start | bytes 294920 | tf_op jit(solution)/shard_map/ppermute | solution.py:364
  158.4 8.2 %collective-permute-start.27 = (bf16[96,512]{1,0:T(8,128)(2,1)S(1)}, bf16[96,512]{1,0:T(8,128)(2,1)S(1)}, u32[]{:S(2)}, u32[]{:S(2)}) collective-permute-start(bf16[96,512]{1,0:T(8,128)(2,1)S(1)} %get-tuple-element.89), channel_id=1, source_target_pairs={{0,12},{1,13},{2,14},{3,15},{4,8},{5,9},{6,10},{7,11},{8,4},{9,5},... | collective-permute-start | bytes 294920 | tf_op jit(solution)/shard_map/ppermute | solution.py:364
  (3 other events, 2.0 us)

commit v3 on v0

--- a/solution.py
+++ b/solution.py
@@ -1,12 +1,27 @@
+import functools
+
 import jax
 import jax.numpy as jnp
 from jax import lax
+from jax.experimental import pallas as pl
+from jax.experimental.pallas import tpu as pltpu
 from jax.sharding import PartitionSpec as P
+
+VMEM_LIMIT = 24 * 1024 * 1024
+UPDATE_LIMIT = 60 * 1024 * 1024
+BOTH = ("seq", "head")
+SMALL = pl.CostEstimate(flops=1, bytes_accessed=1, transcendentals=0)
 
 
 def silu_parts(value):
     sigma = jax.nn.sigmoid(value)
     return (value * sigma, sigma * (1.0 + value * (1.0 - sigma)))
+
+
+def dot(left, right, left_dim, right_dim):
+    return lax.dot_general(
+        left, right, (((left_dim,), (right_dim,)), ((), ())), preferred_element_type=jnp.float32
+    )
 
 
 def local_update(weights, keys_local, values_local, rates_local):
@@ -42,7 +57,7 @@
     return produced.astype(jnp.bfloat16).reshape(queries_local.shape[0], -1)
 
 
-def local(queries, keys, values, rates, fast_init, out_proj):
+def local_summed(queries, keys, values, rates, fast_init, out_proj):
     block_count, tok_count, width_here = queries.shape
     heads_here = fast_init.shape[1]
     head_width = fast_init.shape[2]
@@ -77,6 +92,387 @@
     return result.astype(jnp.bfloat16)
 
 
+def pack_kernel(place, queries, keys, values, rates, kept, sent, keys_in, values_in, queries_in, *sems):
+    load_sems, out_sems = sems
+    half = kept.shape[1]
+    blocks = keys_in.shape[0]
+    core = place[2]
+    loads = []
+    for block in range(blocks):
+        for source, target in ((values, values_in), (keys, keys_in), (queries, queries_in)):
+            sem = load_sems.at[len(loads)]
+            loads.append(pltpu.make_async_copy(source.at[block], target.at[block], sem))
+            loads[-1].start()
+    copies = []
+
+    def send(source, block, slot):
+        for out, which in ((sent, 1 - core), (kept, core)):
+            rows = pl.ds(pl.multiple_of(which * half, half), half)
+            sem = out_sems.at[len(copies)]
+            copies.append(pltpu.make_async_copy(source.at[block, rows], out.at[slot], sem))
+            copies[-1].start()
+
+    for block in range(blocks):
+        for load in loads[3 * block : 3 * block + 3]:
+            load.wait()
+        send(keys_in, block, 2 * block)
+        send(queries_in, block, 2 * blocks + block)
+        rate = rates[block].T
+        width = keys_in.shape[2] // 2
+        for head in range(2):
+            cols = slice(head * width, (head + 1) * width)
+            scaled = rate[:, head : head + 1] * values_in[block, :, cols].astype(jnp.float32)
+            values_in[block, :, cols] = scaled.astype(jnp.bfloat16)
+        send(values_in, block, 2 * block + 1)
+    for copy in copies:
+        copy.wait()
+
+
+def pack(place, queries, keys, values, rates):
+    blocks, tokens, both = keys.shape
+    out = jax.ShapeDtypeStruct((3 * blocks, tokens // 2, both), jnp.bfloat16)
+    return pl.pallas_call(
+        pack_kernel,
+        in_specs=[smem(), hbm(), hbm(), hbm(), vmem()],
+        out_specs=[pl.BlockSpec(memory_space=pl.ANY)] * 2,
+        out_shape=[out, out],
+        scratch_shapes=[pltpu.VMEM(keys.shape, jnp.bfloat16)] * 3
+        + [pltpu.SemaphoreType.DMA((3 * blocks,)), pltpu.SemaphoreType.DMA((6 * blocks,))],
+        cost_estimate=SMALL,
+        name="pack",
+    )(place, queries, keys, values, rates)
+
+
+def deal_kernel(place, kept, got, *refs):
+    outs, (held, load_sems, sems) = refs[:-3], refs[-3:]
+    width = outs[0].shape[3]
+    core = place[2]
+    loads = [
+        pltpu.make_async_copy(kept, held.at[core], load_sems.at[0]),
+        pltpu.make_async_copy(got, held.at[1 - core], load_sems.at[1]),
+    ]
+    for load in loads:
+        load.start()
+    for load in loads:
+        load.wait()
+    copies = []
+    for idx, out in enumerate(outs):
+        for head in range(4):
+            source = held.at[head // 2, pl.ds(2 * idx, 2), :, pl.ds((head % 2) * width, width)]
+            copies.append(pltpu.make_async_copy(source, out.at[head], sems.at[len(copies)]))
+            copies[-1].start()
+    for copy in copies:
+        copy.wait()
+
+
+def deal(place, kept, got):
+    kinds, half, both = kept.shape
+    out = jax.ShapeDtypeStruct((4, 2, half, both // 2), jnp.bfloat16)
+    return pl.pallas_call(
+        deal_kernel,
+        in_specs=[smem(), hbm(), hbm()],
+        out_specs=[pl.BlockSpec(memory_space=pl.ANY)] * (kinds // 2),
+        out_shape=[out] * (kinds // 2),
+        scratch_shapes=[
+            pltpu.VMEM((2,) + kept.shape, jnp.bfloat16),
+            pltpu.SemaphoreType.DMA((2,)),
+            pltpu.SemaphoreType.DMA((2 * kinds,)),
+        ],
+        cost_estimate=SMALL,
+        name="deal",
+    )(place, kept, got)
+
+
+def form_update(pieces, weights, target, fresh, scratch):
+    keys, values, hidden, grad_gate, grad_up, sems = scratch
+    count, half = pieces[0].shape[0], pieces[0].shape[2]
+    copies = []
+    for idx, piece in enumerate(pieces):
+        for source in range(count):
+            rows = pl.ds((count * idx + source) * half, half)
+            for kind, buf in enumerate((keys, values)):
+                sem = sems.at[len(copies)]
+                copies.append(pltpu.make_async_copy(piece.at[source, kind], buf.at[rows], sem))
+                copies[-1].start()
+    tile = count * half
+    for idx in range(len(pieces)):
+        for copy in copies[2 * count * idx : 2 * count * (idx + 1)]:
+            copy.wait()
+        rows = pl.ds(idx * tile, tile)
+        key, value = keys[rows], values[rows]
+        gate_pre = dot(key, weights[0], 1, 1)
+        up_pre = dot(key, weights[1], 1, 1)
+        back = dot(value, weights[2], 1, 0)
+        gate_act, gate_slope = silu_parts(gate_pre)
+        hidden[rows] = (gate_act * up_pre).astype(jnp.bfloat16)
+        grad_gate[rows] = (back * up_pre * gate_slope).astype(jnp.bfloat16)
+        grad_up[rows] = (back * gate_act).astype(jnp.bfloat16)
+    for idx, (left, right) in enumerate(((grad_gate, keys), (grad_up, keys), (values, hidden))):
+        summed = weights[idx].astype(jnp.float32) + dot(left[...], right[...], 0, 0)
+        mean = jnp.mean(summed * summed, axis=-1, keepdims=True)
+        fresh[idx] = (summed * target[idx] * lax.rsqrt(mean + 1e-06)).astype(jnp.bfloat16)
+
+
+def start_queries(block, place, asked, queries, sems):
+    half = asked.shape[2]
+    row = place[0]
+    copies = []
+    for source in range(asked.shape[0]):
+        rows = pl.ds(pl.multiple_of((row ^ source) * half, half), half)
+        copies.append(
+            pltpu.make_async_copy(asked.at[source, block], queries.at[rows], sems.at[source])
+        )
+        copies[-1].start()
+    return copies
+
+
+def form_outputs(query, weights, produced):
+    half = produced[0].shape[0]
+    gate_pre = dot(query, weights[0], 1, 1)
+    up_pre = dot(query, weights[1], 1, 1)
+    applied = (gate_pre * jax.nn.sigmoid(gate_pre) * up_pre).astype(jnp.bfloat16)
+    out = dot(applied, weights[2], 1, 1).astype(jnp.bfloat16)
+    for idx, ref in enumerate(produced):
+        ref[...] = out[idx * half : (idx + 1) * half]
+
+
+def step_kernel(block, place, *refs):
+    pieces, asked, weights, target, fresh = refs[:4], refs[4], refs[5], refs[6], refs[7]
+    produced, (queries, query_sems) = refs[8:12], refs[12:14]
+    copies = start_queries(block, place, asked, queries, query_sems)
+    form_update(pieces, weights, target, fresh, refs[14:])
+    for copy in copies:
+        copy.wait()
+    form_outputs(queries[...], fresh, produced)
+
+
+def update_kernel(*refs):
+    form_update(refs[:4], refs[4], refs[5], refs[6], refs[7:])
+
+
+def apply_kernel(block, place, *refs):
+    asked, weights, produced, queries, sems = refs[0], refs[1], refs[2:6], refs[6], refs[7]
+    for copy in start_queries(block, place, asked, queries, sems):
+        copy.wait()
+    form_outputs(queries[...], weights, produced)
+
+
+def vmem():
+    return pl.BlockSpec(memory_space=pltpu.VMEM)
+
+
+def hbm():
+    return pl.BlockSpec(memory_space=pltpu.HBM)
+
+
+def smem():
+    return pl.BlockSpec(memory_space=pltpu.SMEM)
+
+
+def update_scratch(pieces):
+    count, _, half, width = pieces[0].shape
+    buf = pltpu.VMEM((count * len(pieces) * half, width), jnp.bfloat16)
+    return [buf] * 5 + [pltpu.SemaphoreType.DMA((2 * count * len(pieces),))]
+
+
+def query_scratch(asked):
+    count, _, half, width = asked.shape
+    return [
+        pltpu.VMEM((count * half, width), jnp.bfloat16),
+        pltpu.SemaphoreType.DMA((count,)),
+    ]
+
+
+def update(pieces, weights, target):
+    return pl.pallas_call(
+        update_kernel,
+        in_specs=[hbm()] * 4 + [vmem(), vmem()],
+        out_specs=vmem(),
+        out_shape=jax.ShapeDtypeStruct(weights.shape, jnp.bfloat16),
+        scratch_shapes=update_scratch(pieces),
+        compiler_params=pltpu.CompilerParams(vmem_limit_bytes=UPDATE_LIMIT),
+        cost_estimate=SMALL,
+        name="update",
+    )(*pieces, weights, target)
+
+
+def apply(place, block, asked, weights):
+    return pl.pallas_call(
+        functools.partial(apply_kernel, block),
+        in_specs=[smem(), hbm(), vmem()],
+        out_specs=[vmem()] * 4,
+        out_shape=[jax.ShapeDtypeStruct(asked.shape[2:], jnp.bfloat16)] * 4,
+        scratch_shapes=query_scratch(asked),
+        compiler_params=pltpu.CompilerParams(vmem_limit_bytes=VMEM_LIMIT),
+        cost_estimate=SMALL,
+        name="apply",
+    )(place, asked, weights)
+
+
+def step(place, block, pieces, asked, weights, target):
+    outs = pl.pallas_call(
+        functools.partial(step_kernel, block),
+        in_specs=[smem()] + [hbm()] * 5 + [vmem(), vmem()],
+        out_specs=[vmem()] * 5,
+        out_shape=[jax.ShapeDtypeStruct(weights.shape, jnp.bfloat16)]
+        + [jax.ShapeDtypeStruct(asked.shape[2:], jnp.bfloat16)] * 4,
+        scratch_shapes=query_scratch(asked) + update_scratch(pieces),
+        compiler_params=pltpu.CompilerParams(vmem_limit_bytes=UPDATE_LIMIT),
+        cost_estimate=SMALL,
+        name="step",
+    )(place, *pieces, asked, weights, target)
+    return outs[1:]
+
+
+def place_kernel(place, *refs):
+    shard, slabs, matrix, sems = refs[0], refs[1:9], refs[9], refs[10]
+    part = slabs[0].shape[1]
+    line, core, group = place[1], place[2], place[3]
+    rows = pl.ds(pl.multiple_of(line * 4 * part, 4 * part), 4 * part)
+    copies = [pltpu.make_async_copy(shard, matrix.at[0, rows], sems.at[8])]
+    copies[0].start()
+    for idx, slab in enumerate(slabs):
+        here_line = line ^ ((idx >> 1) & 1)
+        here_group = group ^ (idx & 1)
+        here_core = core ^ (idx >> 2)
+        at = (here_line * 4 + here_group * 2 + here_core) * part
+        rows = pl.ds(pl.multiple_of(at, part), part)
+        turns = pl.ds(4 - slab.shape[0], slab.shape[0])
+        copies.append(pltpu.make_async_copy(slab, matrix.at[turns, rows], sems.at[idx]))
+        copies[-1].start()
+    for copy in copies:
+        copy.wait()
+
+
+def place_slabs(place, shard, slabs):
+    return pl.pallas_call(
+        place_kernel,
+        in_specs=[smem()] + [hbm()] * 9,
+        out_specs=vmem(),
+        out_shape=jax.ShapeDtypeStruct((4, 2 * shard.shape[0], shard.shape[1]), jnp.bfloat16),
+        scratch_shapes=[pltpu.SemaphoreType.DMA((9,))],
+        compiler_params=pltpu.CompilerParams(vmem_limit_bytes=VMEM_LIMIT),
+        cost_estimate=SMALL,
+        name="place_slabs",
+    )(place, shard, *slabs)
+
+
+def project_rows(out, mixed, matrix):
+    total = None
+    for turn in range(4):
+        term = dot(mixed[turn][...], matrix[turn], 1, 0)
+        total = term if total is None else total + term
+    out[...] = total.astype(jnp.bfloat16)
+
+
+def first_kernel(*refs):
+    project_rows(refs[5], refs[:4], refs[4])
+
+
+def second_kernel(*refs):
+    mixed, first, matrix, out = refs[:4], refs[4], refs[5], refs[6]
+    out[0] = first[...]
+    project_rows(out.at[1], mixed, matrix)
+
+
+def project(mixed, first, matrix):
+    half, width = mixed[0].shape
+    depth = matrix.shape[2]
+    shape = (half, depth) if first is None else (2, half, depth)
+    args = (*mixed, matrix) if first is None else (*mixed, first, matrix)
+    vmem = pl.BlockSpec(memory_space=pltpu.VMEM)
+    return pl.pallas_call(
+        first_kernel if first is None else second_kernel,
+        in_specs=[vmem] * len(args),
+        out_specs=vmem,
+        out_shape=jax.ShapeDtypeStruct(shape, jnp.bfloat16),
+        compiler_params=pltpu.CompilerParams(vmem_limit_bytes=VMEM_LIMIT),
+        cost_estimate=SMALL,
+        name="project",
+    )(*args)
+
+
+def routes(rule):
+    pairs = []
+    for row in range(4):
+        for line in range(2):
+            for core in range(2):
+                to_row, to_line, to_core = rule(row, line, core)
+                pairs.append(((row * 2 + line) * 2 + core, (to_row * 2 + to_line) * 2 + to_core))
+    return pairs
+
+
+def swap_line(arr):
+    return lax.ppermute(arr, BOTH, routes(lambda row, line, core: (row, 1 - line, core)))
+
+
+def swap_core(arr):
+    return lax.ppermute(arr, BOTH, routes(lambda row, line, core: (row, line, 1 - core)))
+
+
+def swap_row(arr, turn):
+    return lax.ppermute(arr, BOTH, routes(lambda row, line, core: (row ^ turn, line, core)))
+
+
+def swap_group(arr):
+    return lax.ppermute(arr, "groups", [(0, 1), (1, 0)])
+
+
+def after(arr, *earlier):
+    return lax.optimization_barrier((arr,) + earlier)[0]
+
+
+def exchange(arr):
+    groups = [[2 * row + line for row in range(4)] for line in range(2)]
+    return lax.all_to_all(arr, "seq", 0, 0, axis_index_groups=groups, tiled=True)
+
+
+def local_gathered(queries, keys, values, rates, fast_init, out_proj):
+    seq, core, group = lax.axis_index("seq"), lax.axis_index("head"), lax.axis_index("groups")
+    row, line = seq // 2, seq % 2
+    place = jnp.stack([row, line, core, group]).astype(jnp.int32)
+    rates = rates.transpose(0, 2, 1)
+
+    part = out_proj.shape[0] // 4
+    quarter = lax.dynamic_slice_in_dim(out_proj, (2 * group + core) * part, part, 0)
+    own_line = swap_line(quarter)
+    slab_rows = [swap_row(quarter, turn) for turn in (1, 2)]
+    kept, sent = pack(place, queries, keys, values, rates)
+    slab_rows.append(swap_row(after(quarter, kept), 3))
+    dealt = deal(place, kept, swap_core(after(sent, own_line, *slab_rows[:2])))
+
+    mine = lax.dynamic_index_in_dim(after(fast_init, kept), row % 2, 1, keepdims=False)
+    weights = jnp.where(core == row // 2, mine, swap_core(mine))
+    init_float = weights.astype(jnp.float32)
+    target = jnp.sqrt(jnp.mean(init_float * init_float, axis=-1, keepdims=True))
+
+    own = exchange(after(dealt[0], target, *slab_rows))
+    slab = jnp.stack(slab_rows)
+    slab_line = swap_line(slab)
+    slab_group = swap_group(slab)
+    own_next = exchange(after(dealt[1], slab_line, slab_group, own))
+    slab_line = jnp.concatenate([own_line[None], slab_line])
+    other = swap_line(own)
+    own_core = swap_core(own)
+    slab_both = swap_group(slab_line)
+    asked = exchange(after(dealt[2], own_next, own_core, other))
+    other_next = swap_line(own_next)
+    own_next_core = swap_core(own_next)
+    first = update([own, own_core, other, swap_core(other)], weights, target)
+    produced = apply(place, 0, asked, first)
+    mixed = [[produced[0]] + [swap_row(produced[turn], turn) for turn in (1, 2, 3)]]
+    other_next_core = swap_core(after(other_next, produced[0]))
+    slabs = [slab, slab_group, slab_line, slab_both]
+    slabs = slabs + [swap_core(after(arr, first)) for arr in slabs]
+    pieces = [own_next, own_next_core, other_next, other_next_core]
+    produced = step(place, 1, pieces, asked, after(first, *slabs[4:]), target)
+    produced = [produced[0]] + [after(arr, *mixed[0][1:]) for arr in produced[1:]]
+    mixed += [[produced[0]] + [swap_row(produced[turn], turn) for turn in (1, 2, 3)]]
+
+    matrix = place_slabs(place, out_proj, slabs)
+    return project(mixed[1], project(mixed[0], None, matrix), matrix)
+
+
 def solution(mesh):
     in_specs = (
         P(None, ("groups", "seq"), "head"),
@@ -87,4 +483,6 @@
         P("seq", None),
     )
     out_specs = P(None, ("groups", "seq", "head"), None)
+    few = dict(mesh.shape) == {"groups": 2, "seq": 8, "head": 2}
+    local = local_gathered if few else local_summed
     return jax.shard_map(local, mesh=mesh, in_specs=in_specs, out_specs=out_specs, check_vma=False)

time: 822 us -> 145 us (0.18)
  waiting for transfers between devices: 626 us -> 45.8 us
  blocking collectives: 74.7 us -> 0 us
  local copies, waits for them, and re-layouts: 61 us -> 10.2 us
  starting transfers between devices: 0.57 us -> 43.3 us
  Pallas kernels: 0 us -> 39.7 us
  matrix products: 27.2 us -> 0 us
  between operations: 14.1 us -> 0.22 us
  other arithmetic: 17.2 us -> 4.67 us
    unnamed x7 -> x0, waiting for transfers between devices: 420 us -> none
    all_gather x3 -> x0, waiting for transfers between devices: 207 us -> none  [the longest x1 104 us: local(): lax.all_gather(out_proj, 'seq', axis=0, tiled=True)]
    psum x2 -> x0, blocking collectives: 70.3 us -> none  [local(): squares = lax.psum(jnp.sum(own * own, axis=-1, keepdims=True), 'seq')]
    pallas_call x0 -> x8, Pallas kernels: none -> 39.7 us  [the longest x1 11.4 us: step(): pl.pallas_call(functools.partial(step_kernel, block), in_specs=[smem()] +...]
    ppermute x0 -> x25, starting transfers between devices: none -> 27.7 us  [the longest x9 17.4 us: swap_row(): lax.ppermute(arr, BOTH, routes(lambda row, line, core: (row ^ turn, line,...]
    dot_general x17 -> x0, matrix products: 27.2 us -> none  [the longest x1 6.06 us: local(): jnp.einsum('ctf,fd->ctd', mixed, lax.all_gather(out_proj, 'seq', axis=0,...]
    ppermute x0 -> x25, waiting for transfers between devices: none -> 27.1 us  [the longest x9 11.7 us: swap_row(): lax.ppermute(arr, BOTH, routes(lambda row, line, core: (row ^ turn, line,...]
    another operation x9 -> x0, local copies, waits for them, and re-layouts: 26.3 us -> none  [the longest x2 20.6 us: local_update(): jnp.stack([jnp.einsum('thg,thi->hgi', grad_gate, keys_local, preferred_el...]
  transfers between devices with their start and end apart: 5 -> 28, of which waited for: 5 -> 9; matrix products, arithmetic and copies ran while one was open for 4% -> 4% of each run, Pallas kernels for 0% -> 24%
where the time goes in v3:
time: 145 us; the launch traced here: 144 us
  waiting for transfers between devices  45.8 us (32%)
  starting transfers between devices  43.3 us (30%)
  Pallas kernels  39.7 us (27%)
  local copies, waits for them, and re-layouts  10.2 us (7%)
  other arithmetic  4.67 us (3%)
    all_to_all x3, waiting for transfers between devices, exchange(): lax.all_to_all(arr, 'seq', 0, 0, axis_index_groups=groups, tiled=True)  18.7 us
    ppermute x9, starting transfers between devices, swap_row(): lax.ppermute(arr, BOTH, routes(lambda row, line, core: (row ^ turn, line,...  17.4 us
    all_to_all x3, starting transfers between devices, exchange(): lax.all_to_all(arr, 'seq', 0, 0, axis_index_groups=groups, tiled=True)  15.6 us
    ppermute x9, waiting for transfers between devices, swap_row(): lax.ppermute(arr, BOTH, routes(lambda row, line, core: (row ^ turn, line,...  11.7 us
    ppermute x4, waiting for transfers between devices, swap_line(): lax.ppermute(arr, BOTH, routes(lambda row, line, core: (row, 1 - line, co...  11.6 us
    pallas_call x1, Pallas kernels, step(): pl.pallas_call(functools.partial(step_kernel, block), in_specs=[smem()] +...  11.4 us
    pallas_call x1, Pallas kernels, update(): pl.pallas_call(update_kernel, in_specs=[hbm()] * 4 + [vmem(), vmem()], ou...  11.1 us
    unnamed x32, local copies, waits for them, and re-layouts  5.26 us
  transfers between devices with their start and end apart: 28, of which 9 were waited for; matrix products, arithmetic and copies ran while one was open for 4% of the time, Pallas kernels for 24%

profile of v3, /device:TPU:0, one launch (start us, length us, event | category | flops | bytes accessed | tf_op | source)
XLA Modules:
  0.0 143.9 jit_solution(5486544911572987238)
XLA Ops:
  0.0 0.6 pad_add_fusion.place
  0.6 3.5 %pack.1 = (bf16[6,96,1024]{2,1,0:T(8,128)(2,1)}, bf16[6,96,1024]{2,1,0:T(8,128)(2,1)}) custom-call(s32[4]{0:T(128)} %pad_add_fusion.place, bf16[2,192,1024]{2,1,0:T(8,128)(2,1)} %queries.1, bf16[2,192,1024]{2,1,0:T(8,128)(2,1)} %keys.1, bf16[2,192,1024]{2,1,0:T(8,128)(2,1)} %values.1, f32[2,2,192]{2,1,0:T(2,128)} %bitcast.18), custom_call_target="tpu_custom_call" | custom-call | flops 1 | bytes 1 | tf_op jit(solution)/shard_map/pack/pallas_call | solution.py:134
  4.1 0.0 copy-start.8
  4.2 2.8 %dynamic-slice_bitcast_fusion = bf16[3,512,512]{2,1,0:T(8,128)(2,1)} fusion(bf16[3,2,512,512]{3,2,1,0:T(8,128)(2,1)} %param.10, s32[]{:T(128)S(6)} %select_n.39), kind=kLoop, calls=%fused_computation.1 | loop fusion | bytes 3145732 | tf_op jit(solution)/shard_map/jit(dynamic_index_in_dim)/squeeze | solution.py:444
  7.0 0.5 collective-permute-start.7
  7.4 1.0 constant_dynamic-slice_fusion
  8.4 3.7 %collective-permute-start.2 = (bf16[64,2048]{1,0:T(8,128)(2,1)S(1)}, bf16[64,2048]{1,0:T(8,128)(2,1)S(1)}, u32[]{:S(2)}, u32[]{:S(2)}) collective-permute-start(bf16[64,2048]{1,0:T(8,128)(2,1)S(1)} %constant_dynamic-slice_fusion), channel_id=1, source_target_pairs={{0,8},{1,9},{2,10},{3,11},{4,12},{5,13},{6,14},{7,15},{8,0},{9,1},... | collective-permute-start | bytes 786440 | tf_op jit(solution)/shard_map/ppermute | solution.py:414
  12.1 1.6 %collective-permute-start.1 = (bf16[64,2048]{1,0:T(8,128)(2,1)S(1)}, bf16[64,2048]{1,0:T(8,128)(2,1)S(1)}, u32[]{:S(2)}, u32[]{:S(2)}) collective-permute-start(bf16[64,2048]{1,0:T(8,128)(2,1)S(1)} %constant_dynamic-slice_fusion), channel_id=1, source_target_pairs={{0,4},{1,5},{2,6},{3,7},{4,0},{5,1},{6,2},{7,3},{8,12},{9,13},{10,... | collective-permute-start | bytes 786440 | tf_op jit(solution)/shard_map/ppermute | solution.py:414
  13.6 1.5 %collective-permute-start = (bf16[64,2048]{1,0:T(8,128)(2,1)S(1)}, bf16[64,2048]{1,0:T(8,128)(2,1)S(1)}, u32[]{:S(2)}, u32[]{:S(2)}) collective-permute-start(bf16[64,2048]{1,0:T(8,128)(2,1)S(1)} %constant_dynamic-slice_fusion), channel_id=1, source_target_pairs={{0,2},{1,3},{2,0},{3,1},{4,6},{5,7},{6,4},{7,5},{8,10},{9,11},{10,... | collective-permute-start | bytes 786440 | tf_op jit(solution)/shard_map/ppermute | solution.py:406
  15.2 9.6 %collective-permute-done.2 = bf16[64,2048]{1,0:T(8,128)(2,1)S(1)} collective-permute-done((bf16[64,2048]{1,0:T(8,128)(2,1)S(1)}, bf16[64,2048]{1,0:T(8,128)(2,1)S(1)}, u32[]{:S(2)}, u32[]{:S(2)}) %collective-permute-start.2) | collective-permute-done | bytes 262176 | tf_op jit(solution)/shard_map/ppermute | solution.py:414
  24.8 0.2 collective-permute-done.1
  25.0 0.0 collective-permute-done
  25.0 0.5 copy-done.11
  25.5 0.0 collective-permute-start.3
  25.5 0.2 copy-done.13
  25.7 0.1 copy-done.15
  25.8 3.4 %collective-permute-start.4 = (bf16[64,2048]{1,0:T(8,128)(2,1)S(1)}, bf16[64,2048]{1,0:T(8,128)(2,1)}, u32[]{:S(2)}, u32[]{:S(2)}) collective-permute-start(bf16[64,2048]{1,0:T(8,128)(2,1)S(1)} %constant_dynamic-slice_fusion), channel_id=1, source_target_pairs={{0,12},{1,13},{2,14},{3,15},{4,8},{5,9},{6,10},{7,11},{8,4},{9,5},... | collective-permute-start | bytes 786440 | tf_op jit(solution)/shard_map/ppermute | solution.py:414
  29.2 0.0 collective-permute-done.3.got
  29.2 3.8 %deal.1 = (bf16[4,2,96,512]{3,2,1,0:T(8,128)(2,1)}, bf16[4,2,96,512]{3,2,1,0:T(8,128)(2,1)}, bf16[4,2,96,512]{3,2,1,0:T(8,128)(2,1)}) custom-call(s32[4]{0:T(128)} %pad_add_fusion.place, bf16[6,96,1024]{2,1,0:T(8,128)(2,1)} %get-tuple-element.33.kept, bf16[6,96,1024]{2,1,0:T(8,128)(2,1)} %collective-permute-done.3.got), custom_call_target="tpu_custom_call" | custom-call | flops 1 | bytes 1 | tf_op jit(solution)/shard_map/deal/pallas_call | solution.py:171
  33.0 0.0 collective-permute-done.7
  33.0 1.7 %multiply_reduce_fusion = (f32[3,512]{1,0:T(4,128)S(1)}, bf16[3,512,512]{2,1,0:T(8,128)(2,1)}) fusion(bf16[3,512,512]{2,1,0:T(8,128)(2,1)} %collective-permute-done.7, pred[]{:T(512)S(6)} %eq.6, bf16[3,2,512,512]{3,2,1,0:T(8,128)(2,1)S(1)} %copy-done.8, s32[]{:T(128)S(6)} %select_n.39), kind=kLoop, calls=%fused_computation | loop fusion | flops 3144192 | bytes 4724741 | tf_op jit(solution)/shard_map/reduce_sum | solution.py:447
  34.7 1.5 %collective-permute-done.4 = bf16[64,2048]{1,0:T(8,128)(2,1)} collective-permute-done((bf16[64,2048]{1,0:T(8,128)(2,1)S(1)}, bf16[64,2048]{1,0:T(8,128)(2,1)}, u32[]{:S(2)}, u32[]{:S(2)}) %collective-permute-start.4) | collective-permute-done | bytes 262176 | tf_op jit(solution)/shard_map/ppermute | solution.py:414
  36.2 6.0 %all-to-all-start = ((bf16[4,2,96,512]{3,2,1,0:T(8,128)(2,1)}), bf16[4,2,96,512]{3,2,1,0:T(8,128)(2,1)}, u32[]{:S(2)}, u32[]{:S(2)}) async-start(bf16[4,2,96,512]{3,2,1,0:T(8,128)(2,1)} %get-tuple-element.40), calls=%async_computation | async-start | bytes 1572864 | tf_op jit(solution)/shard_map/all_to_all | solution.py:427
  42.2 1.0 pad_maximum_fusion.1.refs_1_
  43.3 1.6 %collective-permute-start.6 = (bf16[3,64,2048]{2,1,0:T(8,128)(2,1)S(1)}, bf16[3,64,2048]{2,1,0:T(8,128)(2,1)S(1)}, u32[]{:S(2)}, u32[]{:S(2)}) collective-permute-start(bf16[3,64,2048]{2,1,0:T(8,128)(2,1)S(1)} %pad_maximum_fusion.1.refs_1_), channel_id=1, source_target_pairs={{0,16},{16,0},{1,17},{17,1},{2,18},{18,2},{3,19},{19,3},{4,20},{20... | collective-permute-start | bytes 2359304 | tf_op jit(solution)/shard_map/ppermute | solution.py:418
  44.8 1.5 %collective-permute-start.5 = (bf16[3,64,2048]{2,1,0:T(8,128)(2,1)S(1)}, bf16[3,64,2048]{2,1,0:T(8,128)(2,1)S(1)}, u32[]{:S(2)}, u32[]{:S(2)}) collective-permute-start(bf16[3,64,2048]{2,1,0:T(8,128)(2,1)S(1)} %pad_maximum_fusion.1.refs_1_), channel_id=1, source_target_pairs={{0,2},{1,3},{2,0},{3,1},{4,6},{5,7},{6,4},{7,5},{8,10},{9,11},{10,... | collective-permute-start | bytes 2359304 | tf_op jit(solution)/shard_map/ppermute | solution.py:406
  46.4 15.6 %all-to-all-done.refs_0_ = bf16[4,2,96,512]{3,2,1,0:T(8,128)(2,1)} async-done(((bf16[4,2,96,512]{3,2,1,0:T(8,128)(2,1)}), bf16[4,2,96,512]{3,2,1,0:T(8,128)(2,1)}, u32[]{:S(2)}, u32[]{:S(2)}) %all-to-all-start) | async-done | bytes 786464 | tf_op jit(solution)/shard_map/all_to_all | solution.py:427
  61.9 1.5 %collective-permute-start.11 = (bf16[4,2,96,512]{3,2,1,0:T(8,128)(2,1)}, bf16[4,2,96,512]{3,2,1,0:T(8,128)(2,1)}, u32[]{:S(2)}, u32[]{:S(2)}) collective-permute-start(bf16[4,2,96,512]{3,2,1,0:T(8,128)(2,1)} %all-to-all-done.refs_0_), channel_id=1, source_target_pairs={{0,2},{1,3},{2,0},{3,1},{4,6},{5,7},{6,4},{7,5},{8,10},{9,11},{10,... | collective-permute-start | bytes 2359304 | tf_op jit(solution)/shard_map/ppermute | solution.py:406
  63.4 0.0 collective-permute-done.6.refs_2_
  63.4 0.0 collective-permute-done.5
  63.4 6.1 %all-to-all-start.1 = ((bf16[4,2,96,512]{3,2,1,0:T(8,128)(2,1)}), bf16[4,2,96,512]{3,2,1,0:T(8,128)(2,1)S(1)}, u32[]{:S(2)}, u32[]{:S(2)}) async-start(bf16[4,2,96,512]{3,2,1,0:T(8,128)(2,1)} %get-tuple-element.41), calls=%async_computation.1 | async-start | bytes 1572864 | tf_op jit(solution)/shard_map/all_to_all | solution.py:427
  69.5 0.0 collective-permute-start.10
  69.5 11.6 %collective-permute-done.11.refs_2_ = bf16[4,2,96,512]{3,2,1,0:T(8,128)(2,1)} collective-permute-done((bf16[4,2,96,512]{3,2,1,0:T(8,128)(2,1)}, bf16[4,2,96,512]{3,2,1,0:T(8,128)(2,1)}, u32[]{:S(2)}, u32[]{:S(2)}) %collective-permute-start.11) | collective-permute-done | bytes 786464 | tf_op jit(solution)/shard_map/ppermute | solution.py:406
  81.2 1.3 pad_maximum_fusion.refs_3_
  82.4 1.6 %collective-permute-start.17 = (bf16[4,64,2048]{2,1,0:T(8,128)(2,1)S(1)}, bf16[4,64,2048]{2,1,0:T(8,128)(2,1)}, u32[]{:S(2)}, u32[]{:S(2)}) collective-permute-start(bf16[4,64,2048]{2,1,0:T(8,128)(2,1)S(1)} %pad_maximum_fusion.refs_3_), channel_id=1, source_target_pairs={{0,16},{16,0},{1,17},{17,1},{2,18},{18,2},{3,19},{19,3},{4,20},{20... | collective-permute-start | bytes 3145736 | tf_op jit(solution)/shard_map/ppermute | solution.py:418
  84.0 0.0 collective-permute-done.10.refs_1_
  84.0 2.7 %all-to-all-done.1.refs_0_ = bf16[4,2,96,512]{3,2,1,0:T(8,128)(2,1)S(1)} async-done(((bf16[4,2,96,512]{3,2,1,0:T(8,128)(2,1)}), bf16[4,2,96,512]{3,2,1,0:T(8,128)(2,1)S(1)}, u32[]{:S(2)}, u32[]{:S(2)}) %all-to-all-start.1) | async-done | bytes 786464 | tf_op jit(solution)/shard_map/all_to_all | solution.py:427
  86.7 0.9 copy-done.6
  87.6 3.5 %all-to-all-start.2 = ((bf16[4,2,96,512]{3,2,1,0:T(8,128)(2,1)}), bf16[4,2,96,512]{3,2,1,0:T(8,128)(2,1)S(1)}, u32[]{:S(2)}, u32[]{:S(2)}) async-start(bf16[4,2,96,512]{3,2,1,0:T(8,128)(2,1)} %get-tuple-element.43), calls=%async_computation.2 | async-start | bytes 1572864 | tf_op jit(solution)/shard_map/all_to_all | solution.py:427
  91.1 1.2 copy.7.refs_5_.refs_6_
  92.2 0.5 collective-permute-start.9
  92.8 11.1 %update.1.refs_1_.refs_5_ = bf16[3,512,512]{2,1,0:T(8,128)(2,1)} custom-call(bf16[4,2,96,512]{3,2,1,0:T(8,128)(2,1)} %all-to-all-done.refs_0_, bf16[4,2,96,512]{3,2,1,0:T(8,128)(2,1)} %collective-permute-done.10.refs_1_, bf16[4,2,96,512]{3,2,1,0:T(8,128)(2,1)} %collective-permute-done.11.refs_2_, bf16[4,2,96,512]{3,2,1,0:T(8,128)(2,1)} %collective-permute-done.12.refs_3_, ...), custom_call_target="tpu_custom_call" | custom-call | flops 1 | bytes 1 | tf_op jit(solution)/shard_map/update/pallas_call | solution.py:287
  103.8 0.1 collective-permute-start.14
  103.9 0.5 collective-permute-start.16
  104.4 3.8 %collective-permute-done.17.refs_4_ = bf16[4,64,2048]{2,1,0:T(8,128)(2,1)} collective-permute-done((bf16[4,64,2048]{2,1,0:T(8,128)(2,1)S(1)}, bf16[4,64,2048]{2,1,0:T(8,128)(2,1)}, u32[]{:S(2)}, u32[]{:S(2)}) %collective-permute-start.17) | collective-permute-done | bytes 1048608 | tf_op jit(solution)/shard_map/ppermute | solution.py:418
  108.2 0.5 collective-permute-start.15
  108.7 0.4 all-to-all-done.2.refs_0_.refs_4_
  109.1 1.4 copy-done
  110.5 2.7 %apply.1 = (bf16[96,512]{1,0:T(8,128)(2,1)S(1)}, bf16[96,512]{1,0:T(8,128)(2,1)}, bf16[96,512]{1,0:T(8,128)(2,1)S(1)}, bf16[96,512]{1,0:T(8,128)(2,1)S(1)}) custom-call(s32[4]{0:T(128)S(1)} %copy-done.4, bf16[4,2,96,512]{3,2,1,0:T(8,128)(2,1)S(1)} %all-to-all-done.2.refs_0_.refs_4_, bf16[3,512,512]{2,1,0:T(8,128)(2,1)S(1)} %copy-done), custom_call_target="tpu_custom_call" | custom-call | flops 1 | bytes 1 | tf_op jit(solution)/shard_map/apply/pallas_call | solution.py:300
  113.3 0.1 collective-permute-start.8
  113.4 0.5 collective-permute-start.13
  113.9 1.2 collective-permute-start.19
  115.1 0.9 collective-permute-start.20
  116.0 2.3 %collective-permute-start.21 = (bf16[96,512]{1,0:T(8,128)(2,1)S(1)}, bf16[96,512]{1,0:T(8,128)(2,1)S(1)}, u32[]{:S(2)}, u32[]{:S(2)}) collective-permute-start(bf16[96,512]{1,0:T(8,128)(2,1)S(1)} %get-tuple-element.55), channel_id=1, source_target_pairs={{0,12},{1,13},{2,14},{3,15},{4,8},{5,9},{6,10},{7,11},{8,4},{9,5},... | collective-permute-start | bytes 294920 | tf_op jit(solution)/shard_map/ppermute | solution.py:414
  118.3 0.9 copy-done.9
  119.2 11.4 %step.1 = (bf16[3,512,512]{2,1,0:T(8,128)(2,1)}, bf16[96,512]{1,0:T(8,128)(2,1)}, bf16[96,512]{1,0:T(8,128)(2,1)}, bf16[96,512]{1,0:T(8,128)(2,1)}, bf16[96,512]{1,0:T(8,128)(2,1)}) custom-call(s32[4]{0:T(128)} %pad_add_fusion.place, bf16[4,2,96,512]{3,2,1,0:T(8,128)(2,1)} %copy-done.6, bf16[4,2,96,512]{3,2,1,0:T(8,128)(2,1)} %copy-done.9, ...), custom_call_target="tpu_custom_call" | custom-call | flops 1 | bytes 1 | tf_op jit(solution)/shard_map/step/pallas_call | solution.py:313
  130.6 1.6 %collective-permute-start.24 = (bf16[96,512]{1,0:T(8,128)(2,1)}, bf16[96,512]{1,0:T(8,128)(2,1)S(1)}, u32[]{:S(2)}, u32[]{:S(2)}) collective-permute-start(bf16[96,512]{1,0:T(8,128)(2,1)} %get-tuple-element.60), channel_id=1, source_target_pairs={{0,12},{1,13},{2,14},{3,15},{4,8},{5,9},{6,10},{7,11},{8,4},{9,5},... | collective-permute-start | bytes 294920 | tf_op jit(solution)/shard_map/ppermute | solution.py:414
  132.2 0.2 collective-permute-start.23
  132.4 2.7 %collective-permute-start.22 = (bf16[96,512]{1,0:T(8,128)(2,1)}, bf16[96,512]{1,0:T(8,128)(2,1)S(1)}, u32[]{:S(2)}, u32[]{:S(2)}) collective-permute-start(bf16[96,512]{1,0:T(8,128)(2,1)} %get-tuple-element.56), channel_id=1, source_target_pairs={{0,4},{1,5},{2,6},{3,7},{4,0},{5,1},{6,2},{7,3},{8,12},{9,13},{10,... | collective-permute-start | bytes 294920 | tf_op jit(solution)/shard_map/ppermute | solution.py:414
  135.1 1.2 copy-done.2
  136.3 3.4 %place_slabs.1.refs_4_.refs_5_ = bf16[4,512,2048]{2,1,0:T(8,128)(2,1)S(1)} custom-call(s32[4]{0:T(128)S(1)} %copy-done.5, bf16[256,2048]{1,0:T(8,128)(2,1)S(1)} %copy-done.2, bf16[3,64,2048]{2,1,0:T(8,128)(2,1)S(1)} %pad_maximum_fusion.1.refs_1_, bf16[3,64,2048]{2,1,0:T(8,128)(2,1)S(1)} %collective-permute-done.6.refs_2_, ...), custom_call_target="tpu_custom_call" | custom-call | flops 1 | bytes 1 | tf_op jit(solution)/shard_map/place_slabs/pallas_call | solution.py:348
  139.7 1.5 %project.2.refs_4_ = bf16[96,2048]{1,0:T(8,128)(2,1)S(1)} custom-call(bf16[96,512]{1,0:T(8,128)(2,1)S(1)} %get-tuple-element.44.refs_0_, bf16[96,512]{1,0:T(8,128)(2,1)S(1)} %collective-permute-done.19.refs_1_, bf16[96,512]{1,0:T(8,128)(2,1)S(1)} %collective-permute-done.20.refs_2_, bf16[96,512]{1,0:T(8,128)(2,1)S(1)} %collective-permute-done.21.refs_3_, ...), custom_call_target="tpu_custom_call" | custom-call | flops 1 | bytes 1 | tf_op jit(solution)/shard_map/project/pallas_call | solution.py:384
  141.2 0.3 collective-permute-done.23.refs_2_
  141.6 2.3 %project.3 = bf16[2,96,2048]{2,1,0:T(8,128)(2,1)} custom-call(bf16[96,512]{1,0:T(8,128)(2,1)S(1)} %copy-done.3, bf16[96,512]{1,0:T(8,128)(2,1)S(1)} %collective-permute-done.22.refs_1_, bf16[96,512]{1,0:T(8,128)(2,1)S(1)} %collective-permute-done.23.refs_2_, bf16[96,512]{1,0:T(8,128)(2,1)S(1)} %collective-permute-done.24.refs_3_, ...), custom_call_target="tpu_custom_call" | custom-call | flops 1 | bytes 1 | tf_op jit(solution)/shard_map/project/pallas_call | solution.py:384
  (40 shorter events, 0.1 us)
Async XLA Ops:
  4.1 28.8 %copy-start.8 = (bf16[3,2,512,512]{3,2,1,0:T(8,128)(2,1)S(1)}, bf16[3,2,512,512]{3,2,1,0:T(8,128)(2,1)}, u32[]{:S(2)}) copy-start(bf16[3,2,512,512]{3,2,1,0:T(8,128)(2,1)} %param.10) | copy-start | bytes 9437188
  7.0 26.0 %collective-permute-start.7 = (bf16[3,512,512]{2,1,0:T(8,128)(2,1)}, bf16[3,512,512]{2,1,0:T(8,128)(2,1)}, u32[]{:S(2)}, u32[]{:S(2)}) collective-permute-start(bf16[3,512,512]{2,1,0:T(8,128)(2,1)} %dynamic-slice_bitcast_fusion), channel_id=1, source_target_pairs={{0,1},{1,0},{2,3},{3,2},{4,5},{5,4},{6,7},{7,6},{8,9},{9,8},{10,11... | collective-permute-start | bytes 4718600 | tf_op jit(solution)/shard_map/ppermute | solution.py:410
  8.4 16.4 %collective-permute-start.2 = (bf16[64,2048]{1,0:T(8,128)(2,1)S(1)}, bf16[64,2048]{1,0:T(8,128)(2,1)S(1)}, u32[]{:S(2)}, u32[]{:S(2)}) collective-permute-start(bf16[64,2048]{1,0:T(8,128)(2,1)S(1)} %constant_dynamic-slice_fusion), channel_id=1, source_target_pairs={{0,8},{1,9},{2,10},{3,11},{4,12},{5,13},{6,14},{7,15},{8,0},{9,1},... | collective-permute-start | bytes 786440 | tf_op jit(solution)/shard_map/ppermute | solution.py:414
  12.1 12.9 %collective-permute-start.1 = (bf16[64,2048]{1,0:T(8,128)(2,1)S(1)}, bf16[64,2048]{1,0:T(8,128)(2,1)S(1)}, u32[]{:S(2)}, u32[]{:S(2)}) collective-permute-start(bf16[64,2048]{1,0:T(8,128)(2,1)S(1)} %constant_dynamic-slice_fusion), channel_id=1, source_target_pairs={{0,4},{1,5},{2,6},{3,7},{4,0},{5,1},{6,2},{7,3},{8,12},{9,13},{10,... | collective-permute-start | bytes 786440 | tf_op jit(solution)/shard_map/ppermute | solution.py:414
  13.6 11.3 %collective-permute-start = (bf16[64,2048]{1,0:T(8,128)(2,1)S(1)}, bf16[64,2048]{1,0:T(8,128)(2,1)S(1)}, u32[]{:S(2)}, u32[]{:S(2)}) collective-permute-start(bf16[64,2048]{1,0:T(8,128)(2,1)S(1)} %constant_dynamic-slice_fusion), channel_id=1, source_target_pairs={{0,2},{1,3},{2,0},{3,1},{4,6},{5,7},{6,4},{7,5},{8,10},{9,11},{10,... | collective-permute-start | bytes 786440 | tf_op jit(solution)/shard_map/ppermute | solution.py:406
  24.8 0.7 copy-start.11
  25.0 0.7 copy-start.13
  25.0 0.8 copy-start.15
  25.5 3.7 %collective-permute-start.3 = (bf16[6,96,1024]{2,1,0:T(8,128)(2,1)}, bf16[6,96,1024]{2,1,0:T(8,128)(2,1)}, u32[]{:S(2)}, u32[]{:S(2)}) collective-permute-start(bf16[6,96,1024]{2,1,0:T(8,128)(2,1)} %get-tuple-element.35), channel_id=1, source_target_pairs={{0,1},{1,0},{2,3},{3,2},{4,5},{5,4},{6,7},{7,6},{8,9},{9,8},{10,11... | collective-permute-start | bytes 3538952 | tf_op jit(solution)/shard_map/ppermute | solution.py:410
  25.8 10.4 %collective-permute-start.4 = (bf16[64,2048]{1,0:T(8,128)(2,1)S(1)}, bf16[64,2048]{1,0:T(8,128)(2,1)}, u32[]{:S(2)}, u32[]{:S(2)}) collective-permute-start(bf16[64,2048]{1,0:T(8,128)(2,1)S(1)} %constant_dynamic-slice_fusion), channel_id=1, source_target_pairs={{0,12},{1,13},{2,14},{3,15},{4,8},{5,9},{6,10},{7,11},{8,4},{9,5},... | collective-permute-start | bytes 786440 | tf_op jit(solution)/shard_map/ppermute | solution.py:414
  34.7 7.5 %copy-start.12 = (bf16[64,2048]{1,0:T(8,128)(2,1)S(1)}, bf16[64,2048]{1,0:T(8,128)(2,1)}, u32[]{:S(2)}) copy-start(bf16[64,2048]{1,0:T(8,128)(2,1)} %copy-done.11) | copy-start | bytes 786436
  34.7 7.5 %copy-start.14 = (bf16[64,2048]{1,0:T(8,128)(2,1)S(1)}, bf16[64,2048]{1,0:T(8,128)(2,1)}, u32[]{:S(2)}) copy-start(bf16[64,2048]{1,0:T(8,128)(2,1)} %copy-done.13) | copy-start | bytes 786436
  36.2 25.7 %all-to-all-start = ((bf16[4,2,96,512]{3,2,1,0:T(8,128)(2,1)}), bf16[4,2,96,512]{3,2,1,0:T(8,128)(2,1)}, u32[]{:S(2)}, u32[]{:S(2)}) async-start(bf16[4,2,96,512]{3,2,1,0:T(8,128)(2,1)} %get-tuple-element.40), calls=%async_computation | async-start | bytes 1572864 | tf_op jit(solution)/shard_map/all_to_all | solution.py:427
  43.3 20.2 %collective-permute-start.6 = (bf16[3,64,2048]{2,1,0:T(8,128)(2,1)S(1)}, bf16[3,64,2048]{2,1,0:T(8,128)(2,1)S(1)}, u32[]{:S(2)}, u32[]{:S(2)}) collective-permute-start(bf16[3,64,2048]{2,1,0:T(8,128)(2,1)S(1)} %pad_maximum_fusion.1.refs_1_), channel_id=1, source_target_pairs={{0,16},{16,0},{1,17},{17,1},{2,18},{18,2},{3,19},{19,3},{4,20},{20... | collective-permute-start | bytes 2359304 | tf_op jit(solution)/shard_map/ppermute | solution.py:418
  44.8 18.6 %collective-permute-start.5 = (bf16[3,64,2048]{2,1,0:T(8,128)(2,1)S(1)}, bf16[3,64,2048]{2,1,0:T(8,128)(2,1)S(1)}, u32[]{:S(2)}, u32[]{:S(2)}) collective-permute-start(bf16[3,64,2048]{2,1,0:T(8,128)(2,1)S(1)} %pad_maximum_fusion.1.refs_1_), channel_id=1, source_target_pairs={{0,2},{1,3},{2,0},{3,1},{4,6},{5,7},{6,4},{7,5},{8,10},{9,11},{10,... | collective-permute-start | bytes 2359304 | tf_op jit(solution)/shard_map/ppermute | solution.py:406
  61.9 19.2 %collective-permute-start.11 = (bf16[4,2,96,512]{3,2,1,0:T(8,128)(2,1)}, bf16[4,2,96,512]{3,2,1,0:T(8,128)(2,1)}, u32[]{:S(2)}, u32[]{:S(2)}) collective-permute-start(bf16[4,2,96,512]{3,2,1,0:T(8,128)(2,1)} %all-to-all-done.refs_0_), channel_id=1, source_target_pairs={{0,2},{1,3},{2,0},{3,1},{4,6},{5,7},{6,4},{7,5},{8,10},{9,11},{10,... | collective-permute-start | bytes 2359304 | tf_op jit(solution)/shard_map/ppermute | solution.py:406
  63.4 17.7 %copy-start.10 = (bf16[3,64,2048]{2,1,0:T(8,128)(2,1)}, bf16[3,64,2048]{2,1,0:T(8,128)(2,1)S(1)}, u32[]{:S(2)}) copy-start(bf16[3,64,2048]{2,1,0:T(8,128)(2,1)S(1)} %collective-permute-done.5) | copy-start | bytes 2359300
  63.4 23.2 %all-to-all-start.1 = ((bf16[4,2,96,512]{3,2,1,0:T(8,128)(2,1)}), bf16[4,2,96,512]{3,2,1,0:T(8,128)(2,1)S(1)}, u32[]{:S(2)}, u32[]{:S(2)}) async-start(bf16[4,2,96,512]{3,2,1,0:T(8,128)(2,1)} %get-tuple-element.41), calls=%async_computation.1 | async-start | bytes 1572864 | tf_op jit(solution)/shard_map/all_to_all | solution.py:427
  69.5 14.5 %collective-permute-start.10 = (bf16[4,2,96,512]{3,2,1,0:T(8,128)(2,1)}, bf16[4,2,96,512]{3,2,1,0:T(8,128)(2,1)}, u32[]{:S(2)}, u32[]{:S(2)}) collective-permute-start(bf16[4,2,96,512]{3,2,1,0:T(8,128)(2,1)} %all-to-all-done.refs_0_), channel_id=1, source_target_pairs={{0,1},{1,0},{2,3},{3,2},{4,5},{5,4},{6,7},{7,6},{8,9},{9,8},{10,11... | collective-permute-start | bytes 2359304 | tf_op jit(solution)/shard_map/ppermute | solution.py:410
  81.2 11.6 %collective-permute-start.12 = (bf16[4,2,96,512]{3,2,1,0:T(8,128)(2,1)}, bf16[4,2,96,512]{3,2,1,0:T(8,128)(2,1)}, u32[]{:S(2)}, u32[]{:S(2)}) collective-permute-start(bf16[4,2,96,512]{3,2,1,0:T(8,128)(2,1)} %collective-permute-done.11.refs_2_), channel_id=1, source_target_pairs={{0,1},{1,0},{2,3},{3,2},{4,5},{5,4},{6,7},{7,6},{8,9},{9,8},{10,11... | collective-permute-start | bytes 2359304 | tf_op jit(solution)/shard_map/ppermute | solution.py:410
  82.4 25.7 %collective-permute-start.17 = (bf16[4,64,2048]{2,1,0:T(8,128)(2,1)S(1)}, bf16[4,64,2048]{2,1,0:T(8,128)(2,1)}, u32[]{:S(2)}, u32[]{:S(2)}) collective-permute-start(bf16[4,64,2048]{2,1,0:T(8,128)(2,1)S(1)} %pad_maximum_fusion.refs_3_), channel_id=1, source_target_pairs={{0,16},{16,0},{1,17},{17,1},{2,18},{18,2},{3,19},{19,3},{4,20},{20... | collective-permute-start | bytes 3145736 | tf_op jit(solution)/shard_map/ppermute | solution.py:418
  86.7 0.9 copy-start.6
  87.6 21.6 %all-to-all-start.2 = ((bf16[4,2,96,512]{3,2,1,0:T(8,128)(2,1)}), bf16[4,2,96,512]{3,2,1,0:T(8,128)(2,1)S(1)}, u32[]{:S(2)}, u32[]{:S(2)}) async-start(bf16[4,2,96,512]{3,2,1,0:T(8,128)(2,1)} %get-tuple-element.43), calls=%async_computation.2 | async-start | bytes 1572864 | tf_op jit(solution)/shard_map/all_to_all | solution.py:427
  92.2 21.0 %collective-permute-start.9 = (bf16[4,2,96,512]{3,2,1,0:T(8,128)(2,1)}, bf16[4,2,96,512]{3,2,1,0:T(8,128)(2,1)}, u32[]{:S(2)}, u32[]{:S(2)}) collective-permute-start(bf16[4,2,96,512]{3,2,1,0:T(8,128)(2,1)} %copy-done.6), channel_id=1, source_target_pairs={{0,2},{1,3},{2,0},{3,1},{4,6},{5,7},{6,4},{7,5},{8,10},{9,11},{10,... | collective-permute-start | bytes 2359304 | tf_op jit(solution)/shard_map/ppermute | solution.py:406
  92.8 16.4 %copy-start.4 = (s32[4]{0:T(128)S(1)}, s32[4]{0:T(128)}, u32[]{:S(2)}) copy-start(s32[4]{0:T(128)} %pad_add_fusion.place) | copy-start | bytes 52
  103.8 9.6 %collective-permute-start.14 = (bf16[3,64,2048]{2,1,0:T(8,128)(2,1)S(1)}, bf16[3,64,2048]{2,1,0:T(8,128)(2,1)}, u32[]{:S(2)}, u32[]{:S(2)}) collective-permute-start(bf16[3,64,2048]{2,1,0:T(8,128)(2,1)S(1)} %pad_maximum_fusion.1.refs_1_), channel_id=1, source_target_pairs={{0,1},{1,0},{2,3},{3,2},{4,5},{5,4},{6,7},{7,6},{8,9},{9,8},{10,11... | collective-permute-start | bytes 2359304 | tf_op jit(solution)/shard_map/ppermute | solution.py:410
  103.9 11.2 %collective-permute-start.16 = (bf16[4,64,2048]{2,1,0:T(8,128)(2,1)S(1)}, bf16[4,64,2048]{2,1,0:T(8,128)(2,1)}, u32[]{:S(2)}, u32[]{:S(2)}) collective-permute-start(bf16[4,64,2048]{2,1,0:T(8,128)(2,1)S(1)} %pad_maximum_fusion.refs_3_), channel_id=1, source_target_pairs={{0,1},{1,0},{2,3},{3,2},{4,5},{5,4},{6,7},{7,6},{8,9},{9,8},{10,11... | collective-permute-start | bytes 3145736 | tf_op jit(solution)/shard_map/ppermute | solution.py:410
  108.2 7.8 %collective-permute-start.18 = (bf16[4,64,2048]{2,1,0:T(8,128)(2,1)}, bf16[4,64,2048]{2,1,0:T(8,128)(2,1)}, u32[]{:S(2)}, u32[]{:S(2)}) collective-permute-start(bf16[4,64,2048]{2,1,0:T(8,128)(2,1)} %collective-permute-done.17.refs_4_), channel_id=1, source_target_pairs={{0,1},{1,0},{2,3},{3,2},{4,5},{5,4},{6,7},{7,6},{8,9},{9,8},{10,11... | collective-permute-start | bytes 3145736 | tf_op jit(solution)/shard_map/ppermute | solution.py:410
  108.2 5.7 %collective-permute-start.15 = (bf16[3,64,2048]{2,1,0:T(8,128)(2,1)S(1)}, bf16[3,64,2048]{2,1,0:T(8,128)(2,1)}, u32[]{:S(2)}, u32[]{:S(2)}) collective-permute-start(bf16[3,64,2048]{2,1,0:T(8,128)(2,1)S(1)} %collective-permute-done.6.refs_2_), channel_id=1, source_target_pairs={{0,1},{1,0},{2,3},{3,2},{4,5},{5,4},{6,7},{7,6},{8,9},{9,8},{10,11... | collective-permute-start | bytes 2359304 | tf_op jit(solution)/shard_map/ppermute | solution.py:410
  109.1 1.4 copy-start
  110.5 8.6 %copy-start.1 = (bf16[4,2,96,512]{3,2,1,0:T(8,128)(2,1)}, bf16[4,2,96,512]{3,2,1,0:T(8,128)(2,1)S(1)}, u32[]{:S(2)}) copy-start(bf16[4,2,96,512]{3,2,1,0:T(8,128)(2,1)S(1)} %all-to-all-done.2.refs_0_.refs_4_) | copy-start | bytes 2359300
  110.5 2.7 %copy-start.7 = (bf16[4,2,96,512]{3,2,1,0:T(8,128)(2,1)S(1)}, bf16[4,2,96,512]{3,2,1,0:T(8,128)(2,1)}, u32[]{:S(2)}) copy-start(bf16[4,2,96,512]{3,2,1,0:T(8,128)(2,1)} %copy-done.6) | copy-start | bytes 2359300
  113.3 5.0 %collective-permute-start.8 = (bf16[4,2,96,512]{3,2,1,0:T(8,128)(2,1)S(1)}, bf16[4,2,96,512]{3,2,1,0:T(8,128)(2,1)S(1)}, u32[]{:S(2)}, u32[]{:S(2)}) collective-permute-start(bf16[4,2,96,512]{3,2,1,0:T(8,128)(2,1)S(1)} %copy-done.7), channel_id=1, source_target_pairs={{0,1},{1,0},{2,3},{3,2},{4,5},{5,4},{6,7},{7,6},{8,9},{9,8},{10,11... | collective-permute-start | bytes 2359304 | tf_op jit(solution)/shard_map/ppermute | solution.py:410
  113.4 5.8 %collective-permute-start.13 = (bf16[4,2,96,512]{3,2,1,0:T(8,128)(2,1)}, bf16[4,2,96,512]{3,2,1,0:T(8,128)(2,1)}, u32[]{:S(2)}, u32[]{:S(2)}) collective-permute-start(bf16[4,2,96,512]{3,2,1,0:T(8,128)(2,1)} %collective-permute-done.9.refs_2_), channel_id=1, source_target_pairs={{0,1},{1,0},{2,3},{3,2},{4,5},{5,4},{6,7},{7,6},{8,9},{9,8},{10,11... | collective-permute-start | bytes 2359304 | tf_op jit(solution)/shard_map/ppermute | solution.py:410
  113.9 16.7 %collective-permute-start.19 = (bf16[96,512]{1,0:T(8,128)(2,1)}, bf16[96,512]{1,0:T(8,128)(2,1)S(1)}, u32[]{:S(2)}, u32[]{:S(2)}) collective-permute-start(bf16[96,512]{1,0:T(8,128)(2,1)} %get-tuple-element.53), channel_id=1, source_target_pairs={{0,4},{1,5},{2,6},{3,7},{4,0},{5,1},{6,2},{7,3},{8,12},{9,13},{10,... | collective-permute-start | bytes 294920 | tf_op jit(solution)/shard_map/ppermute | solution.py:414
  115.1 15.6 %collective-permute-start.20 = (bf16[96,512]{1,0:T(8,128)(2,1)S(1)}, bf16[96,512]{1,0:T(8,128)(2,1)S(1)}, u32[]{:S(2)}, u32[]{:S(2)}) collective-permute-start(bf16[96,512]{1,0:T(8,128)(2,1)S(1)} %get-tuple-element.54), channel_id=1, source_target_pairs={{0,8},{1,9},{2,10},{3,11},{4,12},{5,13},{6,14},{7,15},{8,0},{9,1},... | collective-permute-start | bytes 294920 | tf_op jit(solution)/shard_map/ppermute | solution.py:414
  116.0 19.1 %copy-start.5 = (s32[4]{0:T(128)S(1)}, s32[4]{0:T(128)}, u32[]{:S(2)}) copy-start(s32[4]{0:T(128)} %pad_add_fusion.place) | copy-start | bytes 52
  116.0 14.7 %collective-permute-start.21 = (bf16[96,512]{1,0:T(8,128)(2,1)S(1)}, bf16[96,512]{1,0:T(8,128)(2,1)S(1)}, u32[]{:S(2)}, u32[]{:S(2)}) collective-permute-start(bf16[96,512]{1,0:T(8,128)(2,1)S(1)} %get-tuple-element.55), channel_id=1, source_target_pairs={{0,12},{1,13},{2,14},{3,15},{4,8},{5,9},{6,10},{7,11},{8,4},{9,5},... | collective-permute-start | bytes 294920 | tf_op jit(solution)/shard_map/ppermute | solution.py:414
  118.3 0.9 copy-start.9
  130.6 10.6 %collective-permute-start.24 = (bf16[96,512]{1,0:T(8,128)(2,1)}, bf16[96,512]{1,0:T(8,128)(2,1)S(1)}, u32[]{:S(2)}, u32[]{:S(2)}) collective-permute-start(bf16[96,512]{1,0:T(8,128)(2,1)} %get-tuple-element.60), channel_id=1, source_target_pairs={{0,12},{1,13},{2,14},{3,15},{4,8},{5,9},{6,10},{7,11},{8,4},{9,5},... | collective-permute-start | bytes 294920 | tf_op jit(solution)/shard_map/ppermute | solution.py:414
  132.2 9.4 %collective-permute-start.23 = (bf16[96,512]{1,0:T(8,128)(2,1)}, bf16[96,512]{1,0:T(8,128)(2,1)S(1)}, u32[]{:S(2)}, u32[]{:S(2)}) collective-permute-start(bf16[96,512]{1,0:T(8,128)(2,1)} %get-tuple-element.58), channel_id=1, source_target_pairs={{0,8},{1,9},{2,10},{3,11},{4,12},{5,13},{6,14},{7,15},{8,0},{9,1},... | collective-permute-start | bytes 294920 | tf_op jit(solution)/shard_map/ppermute | solution.py:414
  132.4 9.1 %collective-permute-start.22 = (bf16[96,512]{1,0:T(8,128)(2,1)}, bf16[96,512]{1,0:T(8,128)(2,1)S(1)}, u32[]{:S(2)}, u32[]{:S(2)}) collective-permute-start(bf16[96,512]{1,0:T(8,128)(2,1)} %get-tuple-element.56), channel_id=1, source_target_pairs={{0,4},{1,5},{2,6},{3,7},{4,0},{5,1},{6,2},{7,3},{8,12},{9,13},{10,... | collective-permute-start | bytes 294920 | tf_op jit(solution)/shard_map/ppermute | solution.py:414
  135.1 1.2 copy-start.2
  139.7 1.8 %copy-start.3 = (bf16[96,512]{1,0:T(8,128)(2,1)S(1)}, bf16[96,512]{1,0:T(8,128)(2,1)}, u32[]{:S(2)}) copy-start(bf16[96,512]{1,0:T(8,128)(2,1)} %get-tuple-element.51.refs_0_) | copy-start | bytes 294916

commit v4 on v3

--- a/solution.py
+++ b/solution.py
@@ -8,7 +8,7 @@
 from jax.sharding import PartitionSpec as P
 
 VMEM_LIMIT = 24 * 1024 * 1024
-UPDATE_LIMIT = 60 * 1024 * 1024
+UPDATE_LIMIT = 32 * 1024 * 1024
 BOTH = ("seq", "head")
 SMALL = pl.CostEstimate(flops=1, bytes_accessed=1, transcendentals=0)
 
@@ -183,8 +183,8 @@
     )(place, kept, got)
 
 
-def form_update(pieces, weights, target, fresh, scratch):
-    keys, values, hidden, grad_gate, grad_up, sems = scratch
+def start_pieces(pieces, scratch):
+    keys, values, sems = scratch[0], scratch[1], scratch[5]
     count, half = pieces[0].shape[0], pieces[0].shape[2]
     copies = []
     for idx, piece in enumerate(pieces):
@@ -194,9 +194,14 @@
                 sem = sems.at[len(copies)]
                 copies.append(pltpu.make_async_copy(piece.at[source, kind], buf.at[rows], sem))
                 copies[-1].start()
-    tile = count * half
-    for idx in range(len(pieces)):
-        for copy in copies[2 * count * idx : 2 * count * (idx + 1)]:
+    return copies
+
+
+def form_update(copies, count, weights, target, fresh, scratch):
+    keys, values, hidden, grad_gate, grad_up, _ = scratch
+    tile, share = keys.shape[0] // count, len(copies) // count
+    for idx in range(count):
+        for copy in copies[share * idx : share * (idx + 1)]:
             copy.wait()
         rows = pl.ds(idx * tile, tile)
         key, value = keys[rows], values[rows]
@@ -240,14 +245,36 @@
     pieces, asked, weights, target, fresh = refs[:4], refs[4], refs[5], refs[6], refs[7]
     produced, (queries, query_sems) = refs[8:12], refs[12:14]
     copies = start_queries(block, place, asked, queries, query_sems)
-    form_update(pieces, weights, target, fresh, refs[14:])
+    form_update(start_pieces(pieces, refs[14:]), 4, weights, target, fresh, refs[14:])
     for copy in copies:
         copy.wait()
     form_outputs(queries[...], fresh, produced)
 
 
-def update_kernel(*refs):
-    form_update(refs[:4], refs[4], refs[5], refs[6], refs[7:])
+def first_kernel(place, *refs):
+    pieces = refs[:4]
+    held, swapped, fresh, target, weights, sem = refs[4:10]
+    row, core = place[0], place[2]
+
+    def load(source):
+        copy = pltpu.make_async_copy(source.at[:, row % 2], weights, sem.at[0])
+        copy.start()
+        copy.wait()
+
+    copies = start_pieces(pieces, refs[10:])
+
+    @pl.when(core == row // 2)
+    def _():
+        load(held)
+
+    @pl.when(core != row // 2)
+    def _():
+        load(swapped)
+
+    for idx in range(weights.shape[0]):
+        init = weights[idx].astype(jnp.float32)
+        target[idx] = jnp.sqrt(jnp.mean(init * init, axis=-1, keepdims=True))
+    form_update(copies, 4, weights, target, fresh, refs[10:])
 
 
 def apply_kernel(block, place, *refs):
@@ -283,17 +310,25 @@
     ]
 
 
-def update(pieces, weights, target):
+def first_update(place, pieces, held, swapped):
+    kinds, _, rows, cols = held.shape
     return pl.pallas_call(
-        update_kernel,
-        in_specs=[hbm()] * 4 + [vmem(), vmem()],
-        out_specs=vmem(),
-        out_shape=jax.ShapeDtypeStruct(weights.shape, jnp.bfloat16),
-        scratch_shapes=update_scratch(pieces),
+        first_kernel,
+        in_specs=[smem()] + [hbm()] * 6,
+        out_specs=[vmem(), vmem()],
+        out_shape=[
+            jax.ShapeDtypeStruct((kinds, rows, cols), jnp.bfloat16),
+            jax.ShapeDtypeStruct((kinds, rows, 1), jnp.float32),
+        ],
+        scratch_shapes=[
+            pltpu.VMEM((kinds, rows, cols), jnp.bfloat16),
+            pltpu.SemaphoreType.DMA((1,)),
+        ]
+        + update_scratch(pieces),
         compiler_params=pltpu.CompilerParams(vmem_limit_bytes=UPDATE_LIMIT),
         cost_estimate=SMALL,
-        name="update",
-    )(*pieces, weights, target)
+        name="first_update",
+    )(place, *pieces, held, swapped)
 
 
 def apply(place, block, asked, weights):
@@ -325,71 +360,68 @@
 
 
 def place_kernel(place, *refs):
-    shard, slabs, matrix, sems = refs[0], refs[1:9], refs[9], refs[10]
+    slabs, matrix, sems = refs[:8], refs[8], refs[9]
     part = slabs[0].shape[1]
     line, core, group = place[1], place[2], place[3]
-    rows = pl.ds(pl.multiple_of(line * 4 * part, 4 * part), 4 * part)
-    copies = [pltpu.make_async_copy(shard, matrix.at[0, rows], sems.at[8])]
-    copies[0].start()
+    copies = []
     for idx, slab in enumerate(slabs):
         here_line = line ^ ((idx >> 1) & 1)
         here_group = group ^ (idx & 1)
         here_core = core ^ (idx >> 2)
         at = (here_line * 4 + here_group * 2 + here_core) * part
         rows = pl.ds(pl.multiple_of(at, part), part)
-        turns = pl.ds(4 - slab.shape[0], slab.shape[0])
-        copies.append(pltpu.make_async_copy(slab, matrix.at[turns, rows], sems.at[idx]))
+        copies.append(pltpu.make_async_copy(slab, matrix.at[:, rows], sems.at[idx]))
         copies[-1].start()
     for copy in copies:
         copy.wait()
 
 
-def place_slabs(place, shard, slabs):
+def place_slabs(place, slabs):
+    count, part, depth = slabs[0].shape
     return pl.pallas_call(
         place_kernel,
-        in_specs=[smem()] + [hbm()] * 9,
+        in_specs=[smem()] + [hbm()] * 8,
         out_specs=vmem(),
-        out_shape=jax.ShapeDtypeStruct((4, 2 * shard.shape[0], shard.shape[1]), jnp.bfloat16),
-        scratch_shapes=[pltpu.SemaphoreType.DMA((9,))],
+        out_shape=jax.ShapeDtypeStruct((count, 8 * part, depth), jnp.bfloat16),
+        scratch_shapes=[pltpu.SemaphoreType.DMA((8,))],
         compiler_params=pltpu.CompilerParams(vmem_limit_bytes=VMEM_LIMIT),
         cost_estimate=SMALL,
         name="place_slabs",
-    )(place, shard, *slabs)
-
-
-def project_rows(out, mixed, matrix):
+    )(place, *slabs)
+
+
+def project_rows(row, out, mixed, matrix):
     total = None
     for turn in range(4):
-        term = dot(mixed[turn][...], matrix[turn], 1, 0)
+        term = dot(mixed[turn][...], matrix[row ^ turn], 1, 0)
         total = term if total is None else total + term
     out[...] = total.astype(jnp.bfloat16)
 
 
-def first_kernel(*refs):
-    project_rows(refs[5], refs[:4], refs[4])
-
-
-def second_kernel(*refs):
+def project_first(place, *refs):
+    project_rows(place[0], refs[5], refs[:4], refs[4])
+
+
+def project_second(place, *refs):
     mixed, first, matrix, out = refs[:4], refs[4], refs[5], refs[6]
     out[0] = first[...]
-    project_rows(out.at[1], mixed, matrix)
-
-
-def project(mixed, first, matrix):
-    half, width = mixed[0].shape
+    project_rows(place[0], out.at[1], mixed, matrix)
+
+
+def project(place, mixed, first, matrix):
+    half = mixed[0].shape[0]
     depth = matrix.shape[2]
     shape = (half, depth) if first is None else (2, half, depth)
     args = (*mixed, matrix) if first is None else (*mixed, first, matrix)
-    vmem = pl.BlockSpec(memory_space=pltpu.VMEM)
     return pl.pallas_call(
-        first_kernel if first is None else second_kernel,
-        in_specs=[vmem] * len(args),
-        out_specs=vmem,
+        project_first if first is None else project_second,
+        in_specs=[smem()] + [vmem()] * len(args),
+        out_specs=vmem(),
         out_shape=jax.ShapeDtypeStruct(shape, jnp.bfloat16),
         compiler_params=pltpu.CompilerParams(vmem_limit_bytes=VMEM_LIMIT),
         cost_estimate=SMALL,
         name="project",
-    )(*args)
+    )(place, *args)
 
 
 def routes(rule):
@@ -435,42 +467,37 @@
 
     part = out_proj.shape[0] // 4
     quarter = lax.dynamic_slice_in_dim(out_proj, (2 * group + core) * part, part, 0)
-    own_line = swap_line(quarter)
-    slab_rows = [swap_row(quarter, turn) for turn in (1, 2)]
-    kept, sent = pack(place, queries, keys, values, rates)
-    slab_rows.append(swap_row(after(quarter, kept), 3))
-    dealt = deal(place, kept, swap_core(after(sent, own_line, *slab_rows[:2])))
-
-    mine = lax.dynamic_index_in_dim(after(fast_init, kept), row % 2, 1, keepdims=False)
-    weights = jnp.where(core == row // 2, mine, swap_core(mine))
-    init_float = weights.astype(jnp.float32)
-    target = jnp.sqrt(jnp.mean(init_float * init_float, axis=-1, keepdims=True))
-
-    own = exchange(after(dealt[0], target, *slab_rows))
-    slab = jnp.stack(slab_rows)
+    quarters = jnp.broadcast_to(quarter[None], (4,) + quarter.shape)
+    slab = exchange(quarters)
+    kept, sent = pack(place, after(queries, quarters), keys, values, rates)
+    dealt = deal(place, kept, swap_core(sent))
+    swapped = swap_core(fast_init)
+
+    own = exchange(after(dealt[0], swapped, slab))
     slab_line = swap_line(slab)
     slab_group = swap_group(slab)
-    own_next = exchange(after(dealt[1], slab_line, slab_group, own))
-    slab_line = jnp.concatenate([own_line[None], slab_line])
-    other = swap_line(own)
+    own_next = exchange(after(dealt[1], own))
+    other = swap_line(after(own, slab_line, slab_group))
     own_core = swap_core(own)
     slab_both = swap_group(slab_line)
     asked = exchange(after(dealt[2], own_next, own_core, other))
     other_next = swap_line(own_next)
     own_next_core = swap_core(own_next)
-    first = update([own, own_core, other, swap_core(other)], weights, target)
+    first, target = first_update(
+        place, [own, own_core, other, swap_core(other)], fast_init, swapped
+    )
     produced = apply(place, 0, asked, first)
     mixed = [[produced[0]] + [swap_row(produced[turn], turn) for turn in (1, 2, 3)]]
-    other_next_core = swap_core(after(other_next, produced[0]))
+    other_next_core = swap_core(after(other_next, first))
     slabs = [slab, slab_group, slab_line, slab_both]
-    slabs = slabs + [swap_core(after(arr, first)) for arr in slabs]
+    slabs = slabs + [swap_core(after(arr, own_next)) for arr in slabs]
     pieces = [own_next, own_next_core, other_next, other_next_core]
     produced = step(place, 1, pieces, asked, after(first, *slabs[4:]), target)
     produced = [produced[0]] + [after(arr, *mixed[0][1:]) for arr in produced[1:]]
     mixed += [[produced[0]] + [swap_row(produced[turn], turn) for turn in (1, 2, 3)]]
 
-    matrix = place_slabs(place, out_proj, slabs)
-    return project(mixed[1], project(mixed[0], None, matrix), matrix)
+    matrix = place_slabs(place, slabs)
+    return project(place, mixed[1], project(place, mixed[0], None, matrix), matrix)
 
 
 def solution(mesh):

time: 145 us -> 140 us (0.966)
  waiting for transfers between devices: 45.8 us -> 52 us
  starting transfers between devices: 43.3 us -> 37.4 us
  other arithmetic: 4.67 us -> 0.59 us
    all_to_all x3 -> x4, waiting for transfers between devices: 18.7 us -> 30.8 us  [exchange(): lax.all_to_all(arr, 'seq', 0, 0, axis_index_groups=groups, tiled=True)]
    ppermute x9 -> x6, waiting for transfers between devices: 11.7 us -> 0.4 us  [swap_row(): lax.ppermute(arr, BOTH, routes(lambda row, line, core: (row ^ turn, line,...]
    ppermute x9 -> x6, starting transfers between devices: 17.4 us -> 8.91 us  [swap_row(): lax.ppermute(arr, BOTH, routes(lambda row, line, core: (row ^ turn, line,...]
    ppermute x4 -> x3, waiting for transfers between devices: 11.6 us -> 16.5 us  [swap_line(): lax.ppermute(arr, BOTH, routes(lambda row, line, core: (row, 1 - line, co...]
    ppermute x10, waiting for transfers between devices: 0.03 us -> 3.07 us  [swap_core(): lax.ppermute(arr, BOTH, routes(lambda row, line, core: (row, line, 1 - co...]
    all_to_all x3 -> x4, starting transfers between devices: 15.6 us -> 18.5 us  [exchange(): lax.all_to_all(arr, 'seq', 0, 0, axis_index_groups=groups, tiled=True)]
    squeeze x1 -> x0, local copies, waits for them, and re-layouts: 2.82 us -> none  [local_gathered(): lax.dynamic_index_in_dim(after(fast_init, kept), row % 2, 1, keepdims=False)]
    unnamed x32 -> x24, local copies, waits for them, and re-layouts: 5.26 us -> 8 us
  transfers between devices with their start and end apart: 28 -> 25, of which waited for: 9 -> 9; matrix products, arithmetic and copies ran while one was open for 4% -> 1% of each run, Pallas kernels for 24% -> 27%
where the time goes in v4:
time: 140 us
  waiting for transfers between devices  52 us (37%)
  Pallas kernels  40.3 us (29%)
  starting transfers between devices  37.4 us (27%)
  local copies, waits for them, and re-layouts  9.18 us (7%)
    all_to_all x4, waiting for transfers between devices, exchange(): lax.all_to_all(arr, 'seq', 0, 0, axis_index_groups=groups, tiled=True)  30.8 us
    all_to_all x4, starting transfers between devices, exchange(): lax.all_to_all(arr, 'seq', 0, 0, axis_index_groups=groups, tiled=True)  18.5 us
    ppermute x3, waiting for transfers between devices, swap_line(): lax.ppermute(arr, BOTH, routes(lambda row, line, core: (row, 1 - line, co...  16.5 us
    pallas_call x1, Pallas kernels, first_update(): pl.pallas_call(first_kernel, in_specs=[smem()] + [hbm()] * 6, out_specs=[...  11.3 us
    pallas_call x1, Pallas kernels, step(): pl.pallas_call(functools.partial(step_kernel, block), in_specs=[smem()] +...  10.6 us
    ppermute x6, starting transfers between devices, swap_row(): lax.ppermute(arr, BOTH, routes(lambda row, line, core: (row ^ turn, line,...  8.91 us
    unnamed x24, local copies, waits for them, and re-layouts  8 us
    pallas_call x2, Pallas kernels, project(): pl.pallas_call(project_first if first is None else project_second, in_spe...  4.89 us
  transfers between devices with their start and end apart: 25, of which 9 were waited for; matrix products, arithmetic and copies ran while one was open for 1% of the time, Pallas kernels for 27%

profile of v4, /device:TPU:0, one launch (start us, length us, event | category | flops | bytes accessed | tf_op | source)
XLA Modules:
  0.0 139.6 jit_solution(11117517129993615232)
XLA Ops:
  0.0 0.5 collective-permute-start.1
  0.5 0.8 copy-done
  1.2 1.2 broadcast_in_dim.2
  2.4 6.3 %all-to-all-start = ((bf16[4,64,2048]{2,1,0:T(8,128)(2,1)}), bf16[4,64,2048]{2,1,0:T(8,128)(2,1)}, u32[]{:S(2)}, u32[]{:S(2)}) async-start(bf16[4,64,2048]{2,1,0:T(8,128)(2,1)} %broadcast_in_dim.2), calls=%async_computation | async-start | bytes 2097152 | tf_op jit(solution)/shard_map/all_to_all | solution.py:459
  8.7 0.6 pad_add_fusion.place
  9.3 3.5 %pack.1 = (bf16[6,96,1024]{2,1,0:T(8,128)(2,1)}, bf16[6,96,1024]{2,1,0:T(8,128)(2,1)}) custom-call(s32[4]{0:T(128)} %pad_add_fusion.place, bf16[2,192,1024]{2,1,0:T(8,128)(2,1)} %queries, bf16[2,192,1024]{2,1,0:T(8,128)(2,1)} %keys.1, bf16[2,192,1024]{2,1,0:T(8,128)(2,1)} %values.1, f32[2,2,192]{2,1,0:T(2,128)} %bitcast.5), custom_call_target="tpu_custom_call" | custom-call | flops 1 | bytes 1 | tf_op jit(solution)/shard_map/pack/pallas_call | solution.py:134
  12.9 0.1 collective-permute-start
  12.9 3.0 %collective-permute-done.got = bf16[6,96,1024]{2,1,0:T(8,128)(2,1)S(1)} collective-permute-done((bf16[6,96,1024]{2,1,0:T(8,128)(2,1)}, bf16[6,96,1024]{2,1,0:T(8,128)(2,1)S(1)}, u32[]{:S(2)}, u32[]{:S(2)}) %collective-permute-start) | collective-permute-done | bytes 1179680 | tf_op jit(solution)/shard_map/ppermute | solution.py:442
  16.0 1.1 copy-done.11
  17.0 3.8 %deal.1 = (bf16[4,2,96,512]{3,2,1,0:T(8,128)(2,1)}, bf16[4,2,96,512]{3,2,1,0:T(8,128)(2,1)}, bf16[4,2,96,512]{3,2,1,0:T(8,128)(2,1)}) custom-call(s32[4]{0:T(128)} %pad_add_fusion.place, bf16[6,96,1024]{2,1,0:T(8,128)(2,1)} %get-tuple-element.35.kept, bf16[6,96,1024]{2,1,0:T(8,128)(2,1)} %copy-done.11), custom_call_target="tpu_custom_call" | custom-call | flops 1 | bytes 1 | tf_op jit(solution)/shard_map/deal/pallas_call | solution.py:171
  20.9 13.7 %all-to-all-done.refs_0_ = bf16[4,64,2048]{2,1,0:T(8,128)(2,1)} async-done(((bf16[4,64,2048]{2,1,0:T(8,128)(2,1)}), bf16[4,64,2048]{2,1,0:T(8,128)(2,1)}, u32[]{:S(2)}, u32[]{:S(2)}) %all-to-all-start) | async-done | bytes 1048608 | tf_op jit(solution)/shard_map/all_to_all | solution.py:459
  34.6 0.0 collective-permute-done.1.refs_5_
  34.6 3.5 %all-to-all-start.1 = ((bf16[4,2,96,512]{3,2,1,0:T(8,128)(2,1)}), bf16[4,2,96,512]{3,2,1,0:T(8,128)(2,1)S(1)}, u32[]{:S(2)}, u32[]{:S(2)}) async-start(bf16[4,2,96,512]{3,2,1,0:T(8,128)(2,1)} %get-tuple-element.39), calls=%async_computation.1 | async-start | bytes 1572864 | tf_op jit(solution)/shard_map/all_to_all | solution.py:459
  38.1 1.6 %collective-permute-start.6 = (bf16[4,64,2048]{2,1,0:T(8,128)(2,1)}, bf16[4,64,2048]{2,1,0:T(8,128)(2,1)}, u32[]{:S(2)}, u32[]{:S(2)}) collective-permute-start(bf16[4,64,2048]{2,1,0:T(8,128)(2,1)} %all-to-all-done.refs_0_), channel_id=1, source_target_pairs={{0,16},{16,0},{1,17},{17,1},{2,18},{18,2},{3,19},{19,3},{4,20},{20... | collective-permute-start | bytes 3145736 | tf_op jit(solution)/shard_map/ppermute | solution.py:450
  39.6 1.5 %collective-permute-start.5 = (bf16[4,64,2048]{2,1,0:T(8,128)(2,1)}, bf16[4,64,2048]{2,1,0:T(8,128)(2,1)}, u32[]{:S(2)}, u32[]{:S(2)}) collective-permute-start(bf16[4,64,2048]{2,1,0:T(8,128)(2,1)} %all-to-all-done.refs_0_), channel_id=1, source_target_pairs={{0,2},{1,3},{2,0},{3,1},{4,6},{5,7},{6,4},{7,5},{8,10},{9,11},{10,... | collective-permute-start | bytes 3145736 | tf_op jit(solution)/shard_map/ppermute | solution.py:438
  41.1 16.5 %all-to-all-done.1.refs_0_ = bf16[4,2,96,512]{3,2,1,0:T(8,128)(2,1)S(1)} async-done(((bf16[4,2,96,512]{3,2,1,0:T(8,128)(2,1)}), bf16[4,2,96,512]{3,2,1,0:T(8,128)(2,1)S(1)}, u32[]{:S(2)}, u32[]{:S(2)}) %all-to-all-start.1) | async-done | bytes 786464 | tf_op jit(solution)/shard_map/all_to_all | solution.py:459
  57.6 4.3 %all-to-all-start.2 = ((bf16[4,2,96,512]{3,2,1,0:T(8,128)(2,1)}), bf16[4,2,96,512]{3,2,1,0:T(8,128)(2,1)}, u32[]{:S(2)}, u32[]{:S(2)}) async-start(bf16[4,2,96,512]{3,2,1,0:T(8,128)(2,1)} %get-tuple-element.40), calls=%async_computation.2 | async-start | bytes 1572864 | tf_op jit(solution)/shard_map/all_to_all | solution.py:459
  62.0 0.6 collective-permute-done.6.refs_1_
  62.6 1.2 collective-permute-done.5.refs_2_
  63.8 1.5 %collective-permute-start.7 = (bf16[4,2,96,512]{3,2,1,0:T(8,128)(2,1)S(1)}, bf16[4,2,96,512]{3,2,1,0:T(8,128)(2,1)S(1)}, u32[]{:S(2)}, u32[]{:S(2)}) collective-permute-start(bf16[4,2,96,512]{3,2,1,0:T(8,128)(2,1)S(1)} %all-to-all-done.1.refs_0_), channel_id=1, source_target_pairs={{0,2},{1,3},{2,0},{3,1},{4,6},{5,7},{6,4},{7,5},{8,10},{9,11},{10,... | collective-permute-start | bytes 2359304 | tf_op jit(solution)/shard_map/ppermute | solution.py:438
  65.3 0.5 collective-permute-start.13
  65.8 0.0 collective-permute-start.4
  65.8 15.2 %collective-permute-done.7.refs_2_ = bf16[4,2,96,512]{3,2,1,0:T(8,128)(2,1)S(1)} collective-permute-done((bf16[4,2,96,512]{3,2,1,0:T(8,128)(2,1)S(1)}, bf16[4,2,96,512]{3,2,1,0:T(8,128)(2,1)S(1)}, u32[]{:S(2)}, u32[]{:S(2)}) %collective-permute-start.7) | collective-permute-done | bytes 786464 | tf_op jit(solution)/shard_map/ppermute | solution.py:438
  81.1 0.0 collective-permute-start.8
  81.1 0.5 all-to-all-done.2.refs_0_
  81.6 0.0 collective-permute-start.10
  81.6 1.5 %collective-permute-start.3 = (bf16[4,2,96,512]{3,2,1,0:T(8,128)(2,1)}, bf16[4,2,96,512]{3,2,1,0:T(8,128)(2,1)}, u32[]{:S(2)}, u32[]{:S(2)}) collective-permute-start(bf16[4,2,96,512]{3,2,1,0:T(8,128)(2,1)} %all-to-all-done.2.refs_0_), channel_id=1, source_target_pairs={{0,2},{1,3},{2,0},{3,1},{4,6},{5,7},{6,4},{7,5},{8,10},{9,11},{10,... | collective-permute-start | bytes 2359304 | tf_op jit(solution)/shard_map/ppermute | solution.py:438
  83.2 0.0 collective-permute-done.4.refs_1_
  83.2 4.4 %all-to-all-start.3 = ((bf16[4,2,96,512]{3,2,1,0:T(8,128)(2,1)}), bf16[4,2,96,512]{3,2,1,0:T(8,128)(2,1)S(1)}, u32[]{:S(2)}, u32[]{:S(2)}) async-start(bf16[4,2,96,512]{3,2,1,0:T(8,128)(2,1)} %get-tuple-element.45), calls=%async_computation.3 | async-start | bytes 1572864 | tf_op jit(solution)/shard_map/all_to_all | solution.py:459
  87.6 0.7 collective-permute-done.13.refs_3_
  88.3 0.0 collective-permute-start.11
  88.3 0.5 collective-permute-start.12
  88.8 0.0 collective-permute-done.8.refs_3_
  88.8 0.1 collective-permute-start.14
  88.9 0.0 copy-start.2
  88.9 1.1 copy-done.2
  90.0 1.9 %copy-done.3 = bf16[3,2,512,512]{3,2,1,0:T(8,128)(2,1)S(1)} copy-done((bf16[3,2,512,512]{3,2,1,0:T(8,128)(2,1)S(1)}, bf16[3,2,512,512]{3,2,1,0:T(8,128)(2,1)}, u32[]{:S(2)}) %copy-start.3) | copy-done | bytes 3145752
  91.9 1.1 copy-done.7
  93.0 1.1 copy-done.9
  94.2 11.3 %first_update.1 = (bf16[3,512,512]{2,1,0:T(8,128)(2,1)S(1)}, f32[3,512,1]{2,1,0:T(8,128)S(1)}) custom-call(s32[4]{0:T(128)S(1)} %copy-done.10, bf16[4,2,96,512]{3,2,1,0:T(8,128)(2,1)S(1)} %copy-done.2, bf16[4,2,96,512]{3,2,1,0:T(8,128)(2,1)S(1)} %copy-done.9, bf16[4,2,96,512]{3,2,1,0:T(8,128)(2,1)S(1)} %copy-done.7, ...), custom_call_target="tpu_custom_call" | custom-call | flops 1 | bytes 1 | tf_op jit(solution)/shard_map/first_update/pallas_call | solution.py:315
  105.5 0.0 copy-start.4
  105.5 0.9 copy-done.4
  106.3 0.0 collective-permute-done.3.refs_2_
  106.3 2.1 %collective-permute-start.2 = (bf16[4,2,96,512]{3,2,1,0:T(8,128)(2,1)}, bf16[4,2,96,512]{3,2,1,0:T(8,128)(2,1)}, u32[]{:S(2)}, u32[]{:S(2)}) collective-permute-start(bf16[4,2,96,512]{3,2,1,0:T(8,128)(2,1)} %all-to-all-done.2.refs_0_), channel_id=1, source_target_pairs={{0,1},{1,0},{2,3},{3,2},{4,5},{5,4},{6,7},{7,6},{8,9},{9,8},{10,11... | collective-permute-start | bytes 2359304 | tf_op jit(solution)/shard_map/ppermute | solution.py:442
  108.4 0.0 collective-permute-done.10.refs_4_
  108.4 0.1 collective-permute-start.9
  108.5 0.0 all-to-all-done.3.refs_4_.refs_0_
  108.5 2.1 %apply.1 = (bf16[96,512]{1,0:T(8,128)(2,1)S(1)}, bf16[96,512]{1,0:T(8,128)(2,1)S(1)}, bf16[96,512]{1,0:T(8,128)(2,1)S(1)}, bf16[96,512]{1,0:T(8,128)(2,1)S(1)}) custom-call(s32[4]{0:T(128)S(1)} %copy-done.10, bf16[4,2,96,512]{3,2,1,0:T(8,128)(2,1)S(1)} %all-to-all-done.3.refs_4_.refs_0_, bf16[3,512,512]{2,1,0:T(8,128)(2,1)S(1)} %get-tuple-element.50.refs_5_.refs_1_), custom_call_target="tpu_custom_call" | custom-call | flops 1 | bytes 1 | tf_op jit(solution)/shard_map/apply/pallas_call | solution.py:335
  110.7 0.0 collective-permute-done.11.refs_5_
  110.7 1.4 %collective-permute-start.15 = (bf16[96,512]{1,0:T(8,128)(2,1)S(1)}, bf16[96,512]{1,0:T(8,128)(2,1)S(1)}, u32[]{:S(2)}, u32[]{:S(2)}) collective-permute-start(bf16[96,512]{1,0:T(8,128)(2,1)S(1)} %get-tuple-element.54), channel_id=1, source_target_pairs={{0,4},{1,5},{2,6},{3,7},{4,0},{5,1},{6,2},{7,3},{8,12},{9,13},{10,... | collective-permute-start | bytes 294920 | tf_op jit(solution)/shard_map/ppermute | solution.py:446
  112.1 0.0 collective-permute-done.12.refs_6_
  112.1 2.3 %collective-permute-start.16 = (bf16[96,512]{1,0:T(8,128)(2,1)S(1)}, bf16[96,512]{1,0:T(8,128)(2,1)S(1)}, u32[]{:S(2)}, u32[]{:S(2)}) collective-permute-start(bf16[96,512]{1,0:T(8,128)(2,1)S(1)} %get-tuple-element.55), channel_id=1, source_target_pairs={{0,8},{1,9},{2,10},{3,11},{4,12},{5,13},{6,14},{7,15},{8,0},{9,1},... | collective-permute-start | bytes 294920 | tf_op jit(solution)/shard_map/ppermute | solution.py:446
  114.4 0.0 collective-permute-done.14.refs_7_
  114.4 0.7 collective-permute-start.17
  115.1 10.6 %step.1 = (bf16[3,512,512]{2,1,0:T(8,128)(2,1)}, bf16[96,512]{1,0:T(8,128)(2,1)S(1)}, bf16[96,512]{1,0:T(8,128)(2,1)S(1)}, bf16[96,512]{1,0:T(8,128)(2,1)S(1)}, bf16[96,512]{1,0:T(8,128)(2,1)S(1)}) custom-call(s32[4]{0:T(128)S(1)} %copy-done.10, bf16[4,2,96,512]{3,2,1,0:T(8,128)(2,1)} %all-to-all-done.2.refs_0_, ...), custom_call_target="tpu_custom_call" | custom-call | flops 1 | bytes 1 | tf_op jit(solution)/shard_map/step/pallas_call | solution.py:348
  125.8 0.0 collective-permute-done.15.refs_1_
  125.8 0.0 collective-permute-done.16.refs_2_
  125.8 3.2 %collective-permute-start.20 = (bf16[96,512]{1,0:T(8,128)(2,1)S(1)}, bf16[96,512]{1,0:T(8,128)(2,1)S(1)}, u32[]{:S(2)}, u32[]{:S(2)}) collective-permute-start(bf16[96,512]{1,0:T(8,128)(2,1)S(1)} %get-tuple-element.61), channel_id=1, source_target_pairs={{0,12},{1,13},{2,14},{3,15},{4,8},{5,9},{6,10},{7,11},{8,4},{9,5},... | collective-permute-start | bytes 294920 | tf_op jit(solution)/shard_map/ppermute | solution.py:446
  129.0 0.0 collective-permute-start.19
  129.0 1.3 collective-permute-start.18
  130.2 4.0 %place_slabs.1.refs_4_.refs_5_ = bf16[4,512,2048]{2,1,0:T(8,128)(2,1)S(1)} custom-call(s32[4]{0:T(128)S(1)} %copy-done.10, bf16[4,64,2048]{2,1,0:T(8,128)(2,1)} %all-to-all-done.refs_0_, bf16[4,64,2048]{2,1,0:T(8,128)(2,1)} %collective-permute-done.6.refs_1_, bf16[4,64,2048]{2,1,0:T(8,128)(2,1)} %collective-permute-done.5.refs_2_, ...), custom_call_target="tpu_custom_call" | custom-call | flops 1 | bytes 1 | tf_op jit(solution)/shard_map/place_slabs/pallas_call | solution.py:381
  134.3 2.0 %project.2.refs_4_ = bf16[96,2048]{1,0:T(8,128)(2,1)S(1)} custom-call(s32[4]{0:T(128)S(1)} %copy-done.10, bf16[96,512]{1,0:T(8,128)(2,1)S(1)} %get-tuple-element.62.refs_0_, bf16[96,512]{1,0:T(8,128)(2,1)S(1)} %collective-permute-done.15.refs_1_, bf16[96,512]{1,0:T(8,128)(2,1)S(1)} %collective-permute-done.16.refs_2_, ...), custom_call_target="tpu_custom_call" | custom-call | flops 1 | bytes 1 | tf_op jit(solution)/shard_map/project/pallas_call | solution.py:416
  136.3 0.4 collective-permute-done.19.refs_2_
  136.7 2.9 %project.3 = bf16[2,96,2048]{2,1,0:T(8,128)(2,1)} custom-call(s32[4]{0:T(128)S(1)} %copy-done.10, bf16[96,512]{1,0:T(8,128)(2,1)S(1)} %get-tuple-element.52.refs_0_, bf16[96,512]{1,0:T(8,128)(2,1)S(1)} %collective-permute-done.18.refs_1_, bf16[96,512]{1,0:T(8,128)(2,1)S(1)} %collective-permute-done.19.refs_2_, ...), custom_call_target="tpu_custom_call" | custom-call | flops 1 | bytes 1 | tf_op jit(solution)/shard_map/project/pallas_call | solution.py:416
  (21 shorter events, 0.1 us)
Async XLA Ops:
  0.0 1.2 copy-start
  0.0 34.6 %collective-permute-start.1 = (bf16[3,2,512,512]{3,2,1,0:T(8,128)(2,1)}, bf16[3,2,512,512]{3,2,1,0:T(8,128)(2,1)}, u32[]{:S(2)}, u32[]{:S(2)}) collective-permute-start(bf16[3,2,512,512]{3,2,1,0:T(8,128)(2,1)} %refs_4_.1), channel_id=1, source_target_pairs={{0,1},{1,0},{2,3},{3,2},{4,5},{5,4},{6,7},{7,6},{8,9},{9,8},{10,11... | collective-permute-start | bytes 9437192 | tf_op jit(solution)/shard_map/ppermute | solution.py:442
  2.4 32.1 %all-to-all-start = ((bf16[4,64,2048]{2,1,0:T(8,128)(2,1)}), bf16[4,64,2048]{2,1,0:T(8,128)(2,1)}, u32[]{:S(2)}, u32[]{:S(2)}) async-start(bf16[4,64,2048]{2,1,0:T(8,128)(2,1)} %broadcast_in_dim.2), calls=%async_computation | async-start | bytes 2097152 | tf_op jit(solution)/shard_map/all_to_all | solution.py:459
  12.9 3.1 %collective-permute-start = (bf16[6,96,1024]{2,1,0:T(8,128)(2,1)}, bf16[6,96,1024]{2,1,0:T(8,128)(2,1)S(1)}, u32[]{:S(2)}, u32[]{:S(2)}) collective-permute-start(bf16[6,96,1024]{2,1,0:T(8,128)(2,1)} %get-tuple-element.36), channel_id=1, source_target_pairs={{0,1},{1,0},{2,3},{3,2},{4,5},{5,4},{6,7},{7,6},{8,9},{9,8},{10,11... | collective-permute-start | bytes 3538952 | tf_op jit(solution)/shard_map/ppermute | solution.py:442
  16.0 1.1 copy-start.11
  34.6 23.1 %all-to-all-start.1 = ((bf16[4,2,96,512]{3,2,1,0:T(8,128)(2,1)}), bf16[4,2,96,512]{3,2,1,0:T(8,128)(2,1)S(1)}, u32[]{:S(2)}, u32[]{:S(2)}) async-start(bf16[4,2,96,512]{3,2,1,0:T(8,128)(2,1)} %get-tuple-element.39), calls=%async_computation.1 | async-start | bytes 1572864 | tf_op jit(solution)/shard_map/all_to_all | solution.py:459
  38.1 24.5 %collective-permute-start.6 = (bf16[4,64,2048]{2,1,0:T(8,128)(2,1)}, bf16[4,64,2048]{2,1,0:T(8,128)(2,1)}, u32[]{:S(2)}, u32[]{:S(2)}) collective-permute-start(bf16[4,64,2048]{2,1,0:T(8,128)(2,1)} %all-to-all-done.refs_0_), channel_id=1, source_target_pairs={{0,16},{16,0},{1,17},{17,1},{2,18},{18,2},{3,19},{19,3},{4,20},{20... | collective-permute-start | bytes 3145736 | tf_op jit(solution)/shard_map/ppermute | solution.py:450
  39.6 24.2 %collective-permute-start.5 = (bf16[4,64,2048]{2,1,0:T(8,128)(2,1)}, bf16[4,64,2048]{2,1,0:T(8,128)(2,1)}, u32[]{:S(2)}, u32[]{:S(2)}) collective-permute-start(bf16[4,64,2048]{2,1,0:T(8,128)(2,1)} %all-to-all-done.refs_0_), channel_id=1, source_target_pairs={{0,2},{1,3},{2,0},{3,1},{4,6},{5,7},{6,4},{7,5},{8,10},{9,11},{10,... | collective-permute-start | bytes 3145736 | tf_op jit(solution)/shard_map/ppermute | solution.py:438
  57.6 25.5 %copy-start.1 = (bf16[4,2,96,512]{3,2,1,0:T(8,128)(2,1)}, bf16[4,2,96,512]{3,2,1,0:T(8,128)(2,1)S(1)}, u32[]{:S(2)}) copy-start(bf16[4,2,96,512]{3,2,1,0:T(8,128)(2,1)S(1)} %all-to-all-done.1.refs_0_) | copy-start | bytes 2359300
  57.6 31.2 %copy-start.10 = (s32[4]{0:T(128)S(1)}, s32[4]{0:T(128)}, u32[]{:S(2)}) copy-start(s32[4]{0:T(128)} %pad_add_fusion.place) | copy-start | bytes 52
  57.6 24.0 %all-to-all-start.2 = ((bf16[4,2,96,512]{3,2,1,0:T(8,128)(2,1)}), bf16[4,2,96,512]{3,2,1,0:T(8,128)(2,1)}, u32[]{:S(2)}, u32[]{:S(2)}) async-start(bf16[4,2,96,512]{3,2,1,0:T(8,128)(2,1)} %get-tuple-element.40), calls=%async_computation.2 | async-start | bytes 1572864 | tf_op jit(solution)/shard_map/all_to_all | solution.py:459
  63.8 17.3 %collective-permute-start.7 = (bf16[4,2,96,512]{3,2,1,0:T(8,128)(2,1)S(1)}, bf16[4,2,96,512]{3,2,1,0:T(8,128)(2,1)S(1)}, u32[]{:S(2)}, u32[]{:S(2)}) collective-permute-start(bf16[4,2,96,512]{3,2,1,0:T(8,128)(2,1)S(1)} %all-to-all-done.1.refs_0_), channel_id=1, source_target_pairs={{0,2},{1,3},{2,0},{3,1},{4,6},{5,7},{6,4},{7,5},{8,10},{9,11},{10,... | collective-permute-start | bytes 2359304 | tf_op jit(solution)/shard_map/ppermute | solution.py:438
  65.3 23.0 %collective-permute-start.13 = (bf16[4,64,2048]{2,1,0:T(8,128)(2,1)}, bf16[4,64,2048]{2,1,0:T(8,128)(2,1)}, u32[]{:S(2)}, u32[]{:S(2)}) collective-permute-start(bf16[4,64,2048]{2,1,0:T(8,128)(2,1)} %collective-permute-done.5.refs_2_), channel_id=1, source_target_pairs={{0,16},{16,0},{1,17},{17,1},{2,18},{18,2},{3,19},{19,3},{4,20},{20... | collective-permute-start | bytes 3145736 | tf_op jit(solution)/shard_map/ppermute | solution.py:450
  65.8 17.3 %collective-permute-start.4 = (bf16[4,2,96,512]{3,2,1,0:T(8,128)(2,1)S(1)}, bf16[4,2,96,512]{3,2,1,0:T(8,128)(2,1)S(1)}, u32[]{:S(2)}, u32[]{:S(2)}) collective-permute-start(bf16[4,2,96,512]{3,2,1,0:T(8,128)(2,1)S(1)} %all-to-all-done.1.refs_0_), channel_id=1, source_target_pairs={{0,1},{1,0},{2,3},{3,2},{4,5},{5,4},{6,7},{7,6},{8,9},{9,8},{10,11... | collective-permute-start | bytes 2359304 | tf_op jit(solution)/shard_map/ppermute | solution.py:442
  81.1 7.7 %copy-start.6 = (bf16[4,2,96,512]{3,2,1,0:T(8,128)(2,1)}, bf16[4,2,96,512]{3,2,1,0:T(8,128)(2,1)S(1)}, u32[]{:S(2)}) copy-start(bf16[4,2,96,512]{3,2,1,0:T(8,128)(2,1)S(1)} %collective-permute-done.7.refs_2_) | copy-start | bytes 2359300
  81.1 7.7 %collective-permute-start.8 = (bf16[4,2,96,512]{3,2,1,0:T(8,128)(2,1)S(1)}, bf16[4,2,96,512]{3,2,1,0:T(8,128)(2,1)}, u32[]{:S(2)}, u32[]{:S(2)}) collective-permute-start(bf16[4,2,96,512]{3,2,1,0:T(8,128)(2,1)S(1)} %collective-permute-done.7.refs_2_), channel_id=1, source_target_pairs={{0,1},{1,0},{2,3},{3,2},{4,5},{5,4},{6,7},{7,6},{8,9},{9,8},{10,11... | collective-permute-start | bytes 2359304 | tf_op jit(solution)/shard_map/ppermute | solution.py:442
  81.6 26.8 %collective-permute-start.10 = (bf16[4,64,2048]{2,1,0:T(8,128)(2,1)}, bf16[4,64,2048]{2,1,0:T(8,128)(2,1)}, u32[]{:S(2)}, u32[]{:S(2)}) collective-permute-start(bf16[4,64,2048]{2,1,0:T(8,128)(2,1)} %all-to-all-done.refs_0_), channel_id=1, source_target_pairs={{0,1},{1,0},{2,3},{3,2},{4,5},{5,4},{6,7},{7,6},{8,9},{9,8},{10,11... | collective-permute-start | bytes 3145736 | tf_op jit(solution)/shard_map/ppermute | solution.py:442
  81.6 24.7 %collective-permute-start.3 = (bf16[4,2,96,512]{3,2,1,0:T(8,128)(2,1)}, bf16[4,2,96,512]{3,2,1,0:T(8,128)(2,1)}, u32[]{:S(2)}, u32[]{:S(2)}) collective-permute-start(bf16[4,2,96,512]{3,2,1,0:T(8,128)(2,1)} %all-to-all-done.2.refs_0_), channel_id=1, source_target_pairs={{0,2},{1,3},{2,0},{3,1},{4,6},{5,7},{6,4},{7,5},{8,10},{9,11},{10,... | collective-permute-start | bytes 2359304 | tf_op jit(solution)/shard_map/ppermute | solution.py:438
  83.2 5.6 %copy-start.8 = (bf16[4,2,96,512]{3,2,1,0:T(8,128)(2,1)}, bf16[4,2,96,512]{3,2,1,0:T(8,128)(2,1)S(1)}, u32[]{:S(2)}) copy-start(bf16[4,2,96,512]{3,2,1,0:T(8,128)(2,1)S(1)} %collective-permute-done.4.refs_1_) | copy-start | bytes 2359300
  83.2 25.3 %all-to-all-start.3 = ((bf16[4,2,96,512]{3,2,1,0:T(8,128)(2,1)}), bf16[4,2,96,512]{3,2,1,0:T(8,128)(2,1)S(1)}, u32[]{:S(2)}, u32[]{:S(2)}) async-start(bf16[4,2,96,512]{3,2,1,0:T(8,128)(2,1)} %get-tuple-element.45), calls=%async_computation.3 | async-start | bytes 1572864 | tf_op jit(solution)/shard_map/all_to_all | solution.py:459
  88.3 22.4 %collective-permute-start.11 = (bf16[4,64,2048]{2,1,0:T(8,128)(2,1)}, bf16[4,64,2048]{2,1,0:T(8,128)(2,1)}, u32[]{:S(2)}, u32[]{:S(2)}) collective-permute-start(bf16[4,64,2048]{2,1,0:T(8,128)(2,1)} %collective-permute-done.6.refs_1_), channel_id=1, source_target_pairs={{0,1},{1,0},{2,3},{3,2},{4,5},{5,4},{6,7},{7,6},{8,9},{9,8},{10,11... | collective-permute-start | bytes 3145736 | tf_op jit(solution)/shard_map/ppermute | solution.py:442
  88.3 23.8 %collective-permute-start.12 = (bf16[4,64,2048]{2,1,0:T(8,128)(2,1)}, bf16[4,64,2048]{2,1,0:T(8,128)(2,1)}, u32[]{:S(2)}, u32[]{:S(2)}) collective-permute-start(bf16[4,64,2048]{2,1,0:T(8,128)(2,1)} %collective-permute-done.5.refs_2_), channel_id=1, source_target_pairs={{0,1},{1,0},{2,3},{3,2},{4,5},{5,4},{6,7},{7,6},{8,9},{9,8},{10,11... | collective-permute-start | bytes 3145736 | tf_op jit(solution)/shard_map/ppermute | solution.py:442
  88.8 25.6 %collective-permute-start.14 = (bf16[4,64,2048]{2,1,0:T(8,128)(2,1)}, bf16[4,64,2048]{2,1,0:T(8,128)(2,1)}, u32[]{:S(2)}, u32[]{:S(2)}) collective-permute-start(bf16[4,64,2048]{2,1,0:T(8,128)(2,1)} %collective-permute-done.13.refs_3_), channel_id=1, source_target_pairs={{0,1},{1,0},{2,3},{3,2},{4,5},{5,4},{6,7},{7,6},{8,9},{9,8},{10,11... | collective-permute-start | bytes 3145736 | tf_op jit(solution)/shard_map/ppermute | solution.py:442
  88.9 1.1 copy-start.2
  90.0 1.9 %copy-start.3 = (bf16[3,2,512,512]{3,2,1,0:T(8,128)(2,1)S(1)}, bf16[3,2,512,512]{3,2,1,0:T(8,128)(2,1)}, u32[]{:S(2)}) copy-start(bf16[3,2,512,512]{3,2,1,0:T(8,128)(2,1)} %refs_4_.1) | copy-start | bytes 9437188
  91.9 1.1 copy-start.7
  93.0 1.1 copy-start.9
  105.5 0.9 copy-start.4
  106.3 8.8 %collective-permute-start.2 = (bf16[4,2,96,512]{3,2,1,0:T(8,128)(2,1)}, bf16[4,2,96,512]{3,2,1,0:T(8,128)(2,1)}, u32[]{:S(2)}, u32[]{:S(2)}) collective-permute-start(bf16[4,2,96,512]{3,2,1,0:T(8,128)(2,1)} %all-to-all-done.2.refs_0_), channel_id=1, source_target_pairs={{0,1},{1,0},{2,3},{3,2},{4,5},{5,4},{6,7},{7,6},{8,9},{9,8},{10,11... | collective-permute-start | bytes 2359304 | tf_op jit(solution)/shard_map/ppermute | solution.py:442
  108.4 6.7 %collective-permute-start.9 = (bf16[4,2,96,512]{3,2,1,0:T(8,128)(2,1)}, bf16[4,2,96,512]{3,2,1,0:T(8,128)(2,1)}, u32[]{:S(2)}, u32[]{:S(2)}) collective-permute-start(bf16[4,2,96,512]{3,2,1,0:T(8,128)(2,1)} %collective-permute-done.3.refs_2_), channel_id=1, source_target_pairs={{0,1},{1,0},{2,3},{3,2},{4,5},{5,4},{6,7},{7,6},{8,9},{9,8},{10,11... | collective-permute-start | bytes 2359304 | tf_op jit(solution)/shard_map/ppermute | solution.py:442
  108.5 6.6 %copy-start.5 = (f32[3,512,1]{2,1,0:T(8,128)S(1)}, f32[3,512,1]{2,1,0:T(8,128)}, u32[]{:S(2)}) copy-start(f32[3,512,1]{2,1,0:T(8,128)} %copy-done.4) | copy-start | bytes 18436
  110.7 15.1 %collective-permute-start.15 = (bf16[96,512]{1,0:T(8,128)(2,1)S(1)}, bf16[96,512]{1,0:T(8,128)(2,1)S(1)}, u32[]{:S(2)}, u32[]{:S(2)}) collective-permute-start(bf16[96,512]{1,0:T(8,128)(2,1)S(1)} %get-tuple-element.54), channel_id=1, source_target_pairs={{0,4},{1,5},{2,6},{3,7},{4,0},{5,1},{6,2},{7,3},{8,12},{9,13},{10,... | collective-permute-start | bytes 294920 | tf_op jit(solution)/shard_map/ppermute | solution.py:446
  112.1 13.7 %collective-permute-start.16 = (bf16[96,512]{1,0:T(8,128)(2,1)S(1)}, bf16[96,512]{1,0:T(8,128)(2,1)S(1)}, u32[]{:S(2)}, u32[]{:S(2)}) collective-permute-start(bf16[96,512]{1,0:T(8,128)(2,1)S(1)} %get-tuple-element.55), channel_id=1, source_target_pairs={{0,8},{1,9},{2,10},{3,11},{4,12},{5,13},{6,14},{7,15},{8,0},{9,1},... | collective-permute-start | bytes 294920 | tf_op jit(solution)/shard_map/ppermute | solution.py:446
  114.4 11.4 %collective-permute-start.17 = (bf16[96,512]{1,0:T(8,128)(2,1)S(1)}, bf16[96,512]{1,0:T(8,128)(2,1)S(1)}, u32[]{:S(2)}, u32[]{:S(2)}) collective-permute-start(bf16[96,512]{1,0:T(8,128)(2,1)S(1)} %get-tuple-element.56), channel_id=1, source_target_pairs={{0,12},{1,13},{2,14},{3,15},{4,8},{5,9},{6,10},{7,11},{8,4},{9,5},... | collective-permute-start | bytes 294920 | tf_op jit(solution)/shard_map/ppermute | solution.py:446
  125.8 10.5 %collective-permute-start.20 = (bf16[96,512]{1,0:T(8,128)(2,1)S(1)}, bf16[96,512]{1,0:T(8,128)(2,1)S(1)}, u32[]{:S(2)}, u32[]{:S(2)}) collective-permute-start(bf16[96,512]{1,0:T(8,128)(2,1)S(1)} %get-tuple-element.61), channel_id=1, source_target_pairs={{0,12},{1,13},{2,14},{3,15},{4,8},{5,9},{6,10},{7,11},{8,4},{9,5},... | collective-permute-start | bytes 294920 | tf_op jit(solution)/shard_map/ppermute | solution.py:446
  129.0 7.7 %collective-permute-start.19 = (bf16[96,512]{1,0:T(8,128)(2,1)S(1)}, bf16[96,512]{1,0:T(8,128)(2,1)S(1)}, u32[]{:S(2)}, u32[]{:S(2)}) collective-permute-start(bf16[96,512]{1,0:T(8,128)(2,1)S(1)} %get-tuple-element.59), channel_id=1, source_target_pairs={{0,8},{1,9},{2,10},{3,11},{4,12},{5,13},{6,14},{7,15},{8,0},{9,1},... | collective-permute-start | bytes 294920 | tf_op jit(solution)/shard_map/ppermute | solution.py:446
  129.0 7.7 %collective-permute-start.18 = (bf16[96,512]{1,0:T(8,128)(2,1)S(1)}, bf16[96,512]{1,0:T(8,128)(2,1)S(1)}, u32[]{:S(2)}, u32[]{:S(2)}) collective-permute-start(bf16[96,512]{1,0:T(8,128)(2,1)S(1)} %get-tuple-element.57), channel_id=1, source_target_pairs={{0,4},{1,5},{2,6},{3,7},{4,0},{5,1},{6,2},{7,3},{8,12},{9,13},{10,... | collective-permute-start | bytes 294920 | tf_op jit(solution)/shard_map/ppermute | solution.py:446

commit v5 on v4

--- a/solution.py
+++ b/solution.py
@@ -8,7 +8,7 @@
 from jax.sharding import PartitionSpec as P
 
 VMEM_LIMIT = 24 * 1024 * 1024
-UPDATE_LIMIT = 32 * 1024 * 1024
+UPDATE_LIMIT = 45 * 1024 * 1024
 BOTH = ("seq", "head")
 SMALL = pl.CostEstimate(flops=1, bytes_accessed=1, transcendentals=0)
 
@@ -245,7 +245,7 @@
     pieces, asked, weights, target, fresh = refs[:4], refs[4], refs[5], refs[6], refs[7]
     produced, (queries, query_sems) = refs[8:12], refs[12:14]
     copies = start_queries(block, place, asked, queries, query_sems)
-    form_update(start_pieces(pieces, refs[14:]), 4, weights, target, fresh, refs[14:])
+    form_update(start_pieces(pieces, refs[14:]), 2, weights, target, fresh, refs[14:])
     for copy in copies:
         copy.wait()
     form_outputs(queries[...], fresh, produced)
@@ -274,7 +274,7 @@
     for idx in range(weights.shape[0]):
         init = weights[idx].astype(jnp.float32)
         target[idx] = jnp.sqrt(jnp.mean(init * init, axis=-1, keepdims=True))
-    form_update(copies, 4, weights, target, fresh, refs[10:])
+    form_update(copies, 2, weights, target, fresh, refs[10:])
 
 
 def apply_kernel(block, place, *refs):

time: 140 us -> 140 us (level)
  transfers between devices with their start and end apart: 25 -> 25, of which waited for: 9 -> 9; matrix products, arithmetic and copies ran while one was open for 1% -> 1% of each run, Pallas kernels for 27% -> 26%
where the time goes in v5:
time: 140 us; the launch traced here: 139 us
  waiting for transfers between devices  52 us (37%)
  Pallas kernels  39.7 us (28%)
  starting transfers between devices  37.4 us (27%)
  local copies, waits for them, and re-layouts  9.18 us (7%)
    all_to_all x4, waiting for transfers between devices, exchange(): lax.all_to_all(arr, 'seq', 0, 0, axis_index_groups=groups, tiled=True)  30.8 us
    all_to_all x4, starting transfers between devices, exchange(): lax.all_to_all(arr, 'seq', 0, 0, axis_index_groups=groups, tiled=True)  18.5 us
    ppermute x3, waiting for transfers between devices, swap_line(): lax.ppermute(arr, BOTH, routes(lambda row, line, core: (row, 1 - line, co...  16.5 us
    pallas_call x1, Pallas kernels, first_update(): pl.pallas_call(first_kernel, in_specs=[smem()] + [hbm()] * 6, out_specs=[...  10.9 us
    pallas_call x1, Pallas kernels, step(): pl.pallas_call(functools.partial(step_kernel, block), in_specs=[smem()] +...  10.4 us
    ppermute x6, starting transfers between devices, swap_row(): lax.ppermute(arr, BOTH, routes(lambda row, line, core: (row ^ turn, line,...  8.91 us
    unnamed x24, local copies, waits for them, and re-layouts  8 us
    pallas_call x2, Pallas kernels, project(): pl.pallas_call(project_first if first is None else project_second, in_spe...  4.89 us
  transfers between devices with their start and end apart: 25, of which 9 were waited for; matrix products, arithmetic and copies ran while one was open for 1% of the time, Pallas kernels for 26%

profile of v5, /device:TPU:0, one launch (start us, length us, event | category | flops | bytes accessed | tf_op | source)
XLA Modules:
  0.0 139.0 jit_solution(16355556403155977730)
XLA Ops:
  0.0 0.5 collective-permute-start.1
  0.5 0.8 copy-done
  1.2 1.2 broadcast_in_dim.2
  2.4 6.3 %all-to-all-start = ((bf16[4,64,2048]{2,1,0:T(8,128)(2,1)}), bf16[4,64,2048]{2,1,0:T(8,128)(2,1)}, u32[]{:S(2)}, u32[]{:S(2)}) async-start(bf16[4,64,2048]{2,1,0:T(8,128)(2,1)} %broadcast_in_dim.2), calls=%async_computation | async-start | bytes 2097152 | tf_op jit(solution)/shard_map/all_to_all | solution.py:459
  8.7 0.6 pad_add_fusion.place
  9.3 3.5 %pack.1 = (bf16[6,96,1024]{2,1,0:T(8,128)(2,1)}, bf16[6,96,1024]{2,1,0:T(8,128)(2,1)}) custom-call(s32[4]{0:T(128)} %pad_add_fusion.place, bf16[2,192,1024]{2,1,0:T(8,128)(2,1)} %queries, bf16[2,192,1024]{2,1,0:T(8,128)(2,1)} %keys.1, bf16[2,192,1024]{2,1,0:T(8,128)(2,1)} %values.1, f32[2,2,192]{2,1,0:T(2,128)} %bitcast.5), custom_call_target="tpu_custom_call" | custom-call | flops 1 | bytes 1 | tf_op jit(solution)/shard_map/pack/pallas_call | solution.py:134
  12.9 0.1 collective-permute-start
  12.9 3.0 %collective-permute-done.got = bf16[6,96,1024]{2,1,0:T(8,128)(2,1)S(1)} collective-permute-done((bf16[6,96,1024]{2,1,0:T(8,128)(2,1)}, bf16[6,96,1024]{2,1,0:T(8,128)(2,1)S(1)}, u32[]{:S(2)}, u32[]{:S(2)}) %collective-permute-start) | collective-permute-done | bytes 1179680 | tf_op jit(solution)/shard_map/ppermute | solution.py:442
  16.0 1.1 copy-done.11
  17.0 3.8 %deal.1 = (bf16[4,2,96,512]{3,2,1,0:T(8,128)(2,1)}, bf16[4,2,96,512]{3,2,1,0:T(8,128)(2,1)}, bf16[4,2,96,512]{3,2,1,0:T(8,128)(2,1)}) custom-call(s32[4]{0:T(128)} %pad_add_fusion.place, bf16[6,96,1024]{2,1,0:T(8,128)(2,1)} %get-tuple-element.35.kept, bf16[6,96,1024]{2,1,0:T(8,128)(2,1)} %copy-done.11), custom_call_target="tpu_custom_call" | custom-call | flops 1 | bytes 1 | tf_op jit(solution)/shard_map/deal/pallas_call | solution.py:171
  20.9 13.7 %all-to-all-done.refs_0_ = bf16[4,64,2048]{2,1,0:T(8,128)(2,1)} async-done(((bf16[4,64,2048]{2,1,0:T(8,128)(2,1)}), bf16[4,64,2048]{2,1,0:T(8,128)(2,1)}, u32[]{:S(2)}, u32[]{:S(2)}) %all-to-all-start) | async-done | bytes 1048608 | tf_op jit(solution)/shard_map/all_to_all | solution.py:459
  34.6 0.0 collective-permute-done.1.refs_5_
  34.6 3.5 %all-to-all-start.1 = ((bf16[4,2,96,512]{3,2,1,0:T(8,128)(2,1)}), bf16[4,2,96,512]{3,2,1,0:T(8,128)(2,1)S(1)}, u32[]{:S(2)}, u32[]{:S(2)}) async-start(bf16[4,2,96,512]{3,2,1,0:T(8,128)(2,1)} %get-tuple-element.39), calls=%async_computation.1 | async-start | bytes 1572864 | tf_op jit(solution)/shard_map/all_to_all | solution.py:459
  38.1 1.6 %collective-permute-start.6 = (bf16[4,64,2048]{2,1,0:T(8,128)(2,1)}, bf16[4,64,2048]{2,1,0:T(8,128)(2,1)}, u32[]{:S(2)}, u32[]{:S(2)}) collective-permute-start(bf16[4,64,2048]{2,1,0:T(8,128)(2,1)} %all-to-all-done.refs_0_), channel_id=1, source_target_pairs={{0,16},{16,0},{1,17},{17,1},{2,18},{18,2},{3,19},{19,3},{4,20},{20... | collective-permute-start | bytes 3145736 | tf_op jit(solution)/shard_map/ppermute | solution.py:450
  39.6 1.5 %collective-permute-start.5 = (bf16[4,64,2048]{2,1,0:T(8,128)(2,1)}, bf16[4,64,2048]{2,1,0:T(8,128)(2,1)}, u32[]{:S(2)}, u32[]{:S(2)}) collective-permute-start(bf16[4,64,2048]{2,1,0:T(8,128)(2,1)} %all-to-all-done.refs_0_), channel_id=1, source_target_pairs={{0,2},{1,3},{2,0},{3,1},{4,6},{5,7},{6,4},{7,5},{8,10},{9,11},{10,... | collective-permute-start | bytes 3145736 | tf_op jit(solution)/shard_map/ppermute | solution.py:438
  41.1 16.5 %all-to-all-done.1.refs_0_ = bf16[4,2,96,512]{3,2,1,0:T(8,128)(2,1)S(1)} async-done(((bf16[4,2,96,512]{3,2,1,0:T(8,128)(2,1)}), bf16[4,2,96,512]{3,2,1,0:T(8,128)(2,1)S(1)}, u32[]{:S(2)}, u32[]{:S(2)}) %all-to-all-start.1) | async-done | bytes 786464 | tf_op jit(solution)/shard_map/all_to_all | solution.py:459
  57.6 4.3 %all-to-all-start.2 = ((bf16[4,2,96,512]{3,2,1,0:T(8,128)(2,1)}), bf16[4,2,96,512]{3,2,1,0:T(8,128)(2,1)}, u32[]{:S(2)}, u32[]{:S(2)}) async-start(bf16[4,2,96,512]{3,2,1,0:T(8,128)(2,1)} %get-tuple-element.40), calls=%async_computation.2 | async-start | bytes 1572864 | tf_op jit(solution)/shard_map/all_to_all | solution.py:459
  62.0 0.6 collective-permute-done.6.refs_1_
  62.6 1.2 collective-permute-done.5.refs_2_
  63.8 1.5 %collective-permute-start.7 = (bf16[4,2,96,512]{3,2,1,0:T(8,128)(2,1)S(1)}, bf16[4,2,96,512]{3,2,1,0:T(8,128)(2,1)S(1)}, u32[]{:S(2)}, u32[]{:S(2)}) collective-permute-start(bf16[4,2,96,512]{3,2,1,0:T(8,128)(2,1)S(1)} %all-to-all-done.1.refs_0_), channel_id=1, source_target_pairs={{0,2},{1,3},{2,0},{3,1},{4,6},{5,7},{6,4},{7,5},{8,10},{9,11},{10,... | collective-permute-start | bytes 2359304 | tf_op jit(solution)/shard_map/ppermute | solution.py:438
  65.3 0.5 collective-permute-start.13
  65.8 0.0 collective-permute-start.4
  65.8 15.2 %collective-permute-done.7.refs_2_ = bf16[4,2,96,512]{3,2,1,0:T(8,128)(2,1)S(1)} collective-permute-done((bf16[4,2,96,512]{3,2,1,0:T(8,128)(2,1)S(1)}, bf16[4,2,96,512]{3,2,1,0:T(8,128)(2,1)S(1)}, u32[]{:S(2)}, u32[]{:S(2)}) %collective-permute-start.7) | collective-permute-done | bytes 786464 | tf_op jit(solution)/shard_map/ppermute | solution.py:438
  81.1 0.0 collective-permute-start.8
  81.1 0.5 all-to-all-done.2.refs_0_
  81.6 0.0 collective-permute-start.10
  81.6 1.5 %collective-permute-start.3 = (bf16[4,2,96,512]{3,2,1,0:T(8,128)(2,1)}, bf16[4,2,96,512]{3,2,1,0:T(8,128)(2,1)}, u32[]{:S(2)}, u32[]{:S(2)}) collective-permute-start(bf16[4,2,96,512]{3,2,1,0:T(8,128)(2,1)} %all-to-all-done.2.refs_0_), channel_id=1, source_target_pairs={{0,2},{1,3},{2,0},{3,1},{4,6},{5,7},{6,4},{7,5},{8,10},{9,11},{10,... | collective-permute-start | bytes 2359304 | tf_op jit(solution)/shard_map/ppermute | solution.py:438
  83.2 0.0 collective-permute-done.4.refs_1_
  83.2 4.4 %all-to-all-start.3 = ((bf16[4,2,96,512]{3,2,1,0:T(8,128)(2,1)}), bf16[4,2,96,512]{3,2,1,0:T(8,128)(2,1)S(1)}, u32[]{:S(2)}, u32[]{:S(2)}) async-start(bf16[4,2,96,512]{3,2,1,0:T(8,128)(2,1)} %get-tuple-element.45), calls=%async_computation.3 | async-start | bytes 1572864 | tf_op jit(solution)/shard_map/all_to_all | solution.py:459
  87.6 0.7 collective-permute-done.13.refs_3_
  88.3 0.0 collective-permute-start.11
  88.3 0.5 collective-permute-start.12
  88.8 0.0 collective-permute-done.8.refs_3_
  88.8 0.1 collective-permute-start.14
  88.9 0.0 copy-start.2
  88.9 1.1 copy-done.2
  90.0 1.9 %copy-done.3 = bf16[3,2,512,512]{3,2,1,0:T(8,128)(2,1)S(1)} copy-done((bf16[3,2,512,512]{3,2,1,0:T(8,128)(2,1)S(1)}, bf16[3,2,512,512]{3,2,1,0:T(8,128)(2,1)}, u32[]{:S(2)}) %copy-start.3) | copy-done | bytes 3145752
  91.9 1.1 copy-done.7
  93.0 1.1 copy-done.9
  94.2 10.9 %first_update.1 = (bf16[3,512,512]{2,1,0:T(8,128)(2,1)S(1)}, f32[3,512,1]{2,1,0:T(8,128)S(1)}) custom-call(s32[4]{0:T(128)S(1)} %copy-done.10, bf16[4,2,96,512]{3,2,1,0:T(8,128)(2,1)S(1)} %copy-done.2, bf16[4,2,96,512]{3,2,1,0:T(8,128)(2,1)S(1)} %copy-done.9, bf16[4,2,96,512]{3,2,1,0:T(8,128)(2,1)S(1)} %copy-done.7, ...), custom_call_target="tpu_custom_call" | custom-call | flops 1 | bytes 1 | tf_op jit(solution)/shard_map/first_update/pallas_call | solution.py:315
  105.1 0.0 copy-start.4
  105.1 0.9 copy-done.4
  106.0 0.0 collective-permute-done.3.refs_2_
  106.0 2.1 %collective-permute-start.2 = (bf16[4,2,96,512]{3,2,1,0:T(8,128)(2,1)}, bf16[4,2,96,512]{3,2,1,0:T(8,128)(2,1)}, u32[]{:S(2)}, u32[]{:S(2)}) collective-permute-start(bf16[4,2,96,512]{3,2,1,0:T(8,128)(2,1)} %all-to-all-done.2.refs_0_), channel_id=1, source_target_pairs={{0,1},{1,0},{2,3},{3,2},{4,5},{5,4},{6,7},{7,6},{8,9},{9,8},{10,11... | collective-permute-start | bytes 2359304 | tf_op jit(solution)/shard_map/ppermute | solution.py:442
  108.0 0.0 collective-permute-done.10.refs_4_
  108.1 0.1 collective-permute-start.9
  108.1 0.0 all-to-all-done.3.refs_4_.refs_0_
  108.1 2.1 %apply.1 = (bf16[96,512]{1,0:T(8,128)(2,1)S(1)}, bf16[96,512]{1,0:T(8,128)(2,1)S(1)}, bf16[96,512]{1,0:T(8,128)(2,1)S(1)}, bf16[96,512]{1,0:T(8,128)(2,1)S(1)}) custom-call(s32[4]{0:T(128)S(1)} %copy-done.10, bf16[4,2,96,512]{3,2,1,0:T(8,128)(2,1)S(1)} %all-to-all-done.3.refs_4_.refs_0_, bf16[3,512,512]{2,1,0:T(8,128)(2,1)S(1)} %get-tuple-element.50.refs_5_.refs_1_), custom_call_target="tpu_custom_call" | custom-call | flops 1 | bytes 1 | tf_op jit(solution)/shard_map/apply/pallas_call | solution.py:335
  110.3 0.0 collective-permute-done.11.refs_5_
  110.3 1.4 %collective-permute-start.15 = (bf16[96,512]{1,0:T(8,128)(2,1)S(1)}, bf16[96,512]{1,0:T(8,128)(2,1)S(1)}, u32[]{:S(2)}, u32[]{:S(2)}) collective-permute-start(bf16[96,512]{1,0:T(8,128)(2,1)S(1)} %get-tuple-element.54), channel_id=1, source_target_pairs={{0,4},{1,5},{2,6},{3,7},{4,0},{5,1},{6,2},{7,3},{8,12},{9,13},{10,... | collective-permute-start | bytes 294920 | tf_op jit(solution)/shard_map/ppermute | solution.py:446
  111.7 2.3 %collective-permute-start.16 = (bf16[96,512]{1,0:T(8,128)(2,1)S(1)}, bf16[96,512]{1,0:T(8,128)(2,1)S(1)}, u32[]{:S(2)}, u32[]{:S(2)}) collective-permute-start(bf16[96,512]{1,0:T(8,128)(2,1)S(1)} %get-tuple-element.55), channel_id=1, source_target_pairs={{0,8},{1,9},{2,10},{3,11},{4,12},{5,13},{6,14},{7,15},{8,0},{9,1},... | collective-permute-start | bytes 294920 | tf_op jit(solution)/shard_map/ppermute | solution.py:446
  114.0 0.0 collective-permute-done.14.refs_7_
  114.0 0.7 collective-permute-start.17
  114.8 10.4 %step.1 = (bf16[3,512,512]{2,1,0:T(8,128)(2,1)}, bf16[96,512]{1,0:T(8,128)(2,1)S(1)}, bf16[96,512]{1,0:T(8,128)(2,1)S(1)}, bf16[96,512]{1,0:T(8,128)(2,1)S(1)}, bf16[96,512]{1,0:T(8,128)(2,1)S(1)}) custom-call(s32[4]{0:T(128)S(1)} %copy-done.10, bf16[4,2,96,512]{3,2,1,0:T(8,128)(2,1)} %all-to-all-done.2.refs_0_, ...), custom_call_target="tpu_custom_call" | custom-call | flops 1 | bytes 1 | tf_op jit(solution)/shard_map/step/pallas_call | solution.py:348
  125.2 0.0 collective-permute-done.15.refs_1_
  125.2 0.0 collective-permute-done.16.refs_2_
  125.2 3.2 %collective-permute-start.20 = (bf16[96,512]{1,0:T(8,128)(2,1)S(1)}, bf16[96,512]{1,0:T(8,128)(2,1)S(1)}, u32[]{:S(2)}, u32[]{:S(2)}) collective-permute-start(bf16[96,512]{1,0:T(8,128)(2,1)S(1)} %get-tuple-element.61), channel_id=1, source_target_pairs={{0,12},{1,13},{2,14},{3,15},{4,8},{5,9},{6,10},{7,11},{8,4},{9,5},... | collective-permute-start | bytes 294920 | tf_op jit(solution)/shard_map/ppermute | solution.py:446
  128.4 0.0 collective-permute-start.19
  128.4 1.3 collective-permute-start.18
  129.7 4.0 %place_slabs.1.refs_4_.refs_5_ = bf16[4,512,2048]{2,1,0:T(8,128)(2,1)S(1)} custom-call(s32[4]{0:T(128)S(1)} %copy-done.10, bf16[4,64,2048]{2,1,0:T(8,128)(2,1)} %all-to-all-done.refs_0_, bf16[4,64,2048]{2,1,0:T(8,128)(2,1)} %collective-permute-done.6.refs_1_, bf16[4,64,2048]{2,1,0:T(8,128)(2,1)} %collective-permute-done.5.refs_2_, ...), custom_call_target="tpu_custom_call" | custom-call | flops 1 | bytes 1 | tf_op jit(solution)/shard_map/place_slabs/pallas_call | solution.py:381
  133.7 2.0 %project.2.refs_4_ = bf16[96,2048]{1,0:T(8,128)(2,1)S(1)} custom-call(s32[4]{0:T(128)S(1)} %copy-done.10, bf16[96,512]{1,0:T(8,128)(2,1)S(1)} %get-tuple-element.62.refs_0_, bf16[96,512]{1,0:T(8,128)(2,1)S(1)} %collective-permute-done.15.refs_1_, bf16[96,512]{1,0:T(8,128)(2,1)S(1)} %collective-permute-done.16.refs_2_, ...), custom_call_target="tpu_custom_call" | custom-call | flops 1 | bytes 1 | tf_op jit(solution)/shard_map/project/pallas_call | solution.py:416
  135.7 0.0 collective-permute-done.20.refs_3_
  135.7 0.4 collective-permute-done.19.refs_2_
  136.1 2.9 %project.3 = bf16[2,96,2048]{2,1,0:T(8,128)(2,1)} custom-call(s32[4]{0:T(128)S(1)} %copy-done.10, bf16[96,512]{1,0:T(8,128)(2,1)S(1)} %get-tuple-element.52.refs_0_, bf16[96,512]{1,0:T(8,128)(2,1)S(1)} %collective-permute-done.18.refs_1_, bf16[96,512]{1,0:T(8,128)(2,1)S(1)} %collective-permute-done.19.refs_2_, ...), custom_call_target="tpu_custom_call" | custom-call | flops 1 | bytes 1 | tf_op jit(solution)/shard_map/project/pallas_call | solution.py:416
  (21 shorter events, 0.1 us)
Async XLA Ops:
  0.0 1.2 copy-start
  0.0 34.6 %collective-permute-start.1 = (bf16[3,2,512,512]{3,2,1,0:T(8,128)(2,1)}, bf16[3,2,512,512]{3,2,1,0:T(8,128)(2,1)}, u32[]{:S(2)}, u32[]{:S(2)}) collective-permute-start(bf16[3,2,512,512]{3,2,1,0:T(8,128)(2,1)} %refs_4_.1), channel_id=1, source_target_pairs={{0,1},{1,0},{2,3},{3,2},{4,5},{5,4},{6,7},{7,6},{8,9},{9,8},{10,11... | collective-permute-start | bytes 9437192 | tf_op jit(solution)/shard_map/ppermute | solution.py:442
  2.4 32.1 %all-to-all-start = ((bf16[4,64,2048]{2,1,0:T(8,128)(2,1)}), bf16[4,64,2048]{2,1,0:T(8,128)(2,1)}, u32[]{:S(2)}, u32[]{:S(2)}) async-start(bf16[4,64,2048]{2,1,0:T(8,128)(2,1)} %broadcast_in_dim.2), calls=%async_computation | async-start | bytes 2097152 | tf_op jit(solution)/shard_map/all_to_all | solution.py:459
  12.9 3.1 %collective-permute-start = (bf16[6,96,1024]{2,1,0:T(8,128)(2,1)}, bf16[6,96,1024]{2,1,0:T(8,128)(2,1)S(1)}, u32[]{:S(2)}, u32[]{:S(2)}) collective-permute-start(bf16[6,96,1024]{2,1,0:T(8,128)(2,1)} %get-tuple-element.36), channel_id=1, source_target_pairs={{0,1},{1,0},{2,3},{3,2},{4,5},{5,4},{6,7},{7,6},{8,9},{9,8},{10,11... | collective-permute-start | bytes 3538952 | tf_op jit(solution)/shard_map/ppermute | solution.py:442
  16.0 1.1 copy-start.11
  34.6 23.1 %all-to-all-start.1 = ((bf16[4,2,96,512]{3,2,1,0:T(8,128)(2,1)}), bf16[4,2,96,512]{3,2,1,0:T(8,128)(2,1)S(1)}, u32[]{:S(2)}, u32[]{:S(2)}) async-start(bf16[4,2,96,512]{3,2,1,0:T(8,128)(2,1)} %get-tuple-element.39), calls=%async_computation.1 | async-start | bytes 1572864 | tf_op jit(solution)/shard_map/all_to_all | solution.py:459
  38.1 24.5 %collective-permute-start.6 = (bf16[4,64,2048]{2,1,0:T(8,128)(2,1)}, bf16[4,64,2048]{2,1,0:T(8,128)(2,1)}, u32[]{:S(2)}, u32[]{:S(2)}) collective-permute-start(bf16[4,64,2048]{2,1,0:T(8,128)(2,1)} %all-to-all-done.refs_0_), channel_id=1, source_target_pairs={{0,16},{16,0},{1,17},{17,1},{2,18},{18,2},{3,19},{19,3},{4,20},{20... | collective-permute-start | bytes 3145736 | tf_op jit(solution)/shard_map/ppermute | solution.py:450
  39.6 24.2 %collective-permute-start.5 = (bf16[4,64,2048]{2,1,0:T(8,128)(2,1)}, bf16[4,64,2048]{2,1,0:T(8,128)(2,1)}, u32[]{:S(2)}, u32[]{:S(2)}) collective-permute-start(bf16[4,64,2048]{2,1,0:T(8,128)(2,1)} %all-to-all-done.refs_0_), channel_id=1, source_target_pairs={{0,2},{1,3},{2,0},{3,1},{4,6},{5,7},{6,4},{7,5},{8,10},{9,11},{10,... | collective-permute-start | bytes 3145736 | tf_op jit(solution)/shard_map/ppermute | solution.py:438
  57.6 25.5 %copy-start.1 = (bf16[4,2,96,512]{3,2,1,0:T(8,128)(2,1)}, bf16[4,2,96,512]{3,2,1,0:T(8,128)(2,1)S(1)}, u32[]{:S(2)}) copy-start(bf16[4,2,96,512]{3,2,1,0:T(8,128)(2,1)S(1)} %all-to-all-done.1.refs_0_) | copy-start | bytes 2359300
  57.6 31.2 %copy-start.10 = (s32[4]{0:T(128)S(1)}, s32[4]{0:T(128)}, u32[]{:S(2)}) copy-start(s32[4]{0:T(128)} %pad_add_fusion.place) | copy-start | bytes 52
  57.6 24.0 %all-to-all-start.2 = ((bf16[4,2,96,512]{3,2,1,0:T(8,128)(2,1)}), bf16[4,2,96,512]{3,2,1,0:T(8,128)(2,1)}, u32[]{:S(2)}, u32[]{:S(2)}) async-start(bf16[4,2,96,512]{3,2,1,0:T(8,128)(2,1)} %get-tuple-element.40), calls=%async_computation.2 | async-start | bytes 1572864 | tf_op jit(solution)/shard_map/all_to_all | solution.py:459
  63.8 17.3 %collective-permute-start.7 = (bf16[4,2,96,512]{3,2,1,0:T(8,128)(2,1)S(1)}, bf16[4,2,96,512]{3,2,1,0:T(8,128)(2,1)S(1)}, u32[]{:S(2)}, u32[]{:S(2)}) collective-permute-start(bf16[4,2,96,512]{3,2,1,0:T(8,128)(2,1)S(1)} %all-to-all-done.1.refs_0_), channel_id=1, source_target_pairs={{0,2},{1,3},{2,0},{3,1},{4,6},{5,7},{6,4},{7,5},{8,10},{9,11},{10,... | collective-permute-start | bytes 2359304 | tf_op jit(solution)/shard_map/ppermute | solution.py:438
  65.3 23.0 %collective-permute-start.13 = (bf16[4,64,2048]{2,1,0:T(8,128)(2,1)}, bf16[4,64,2048]{2,1,0:T(8,128)(2,1)}, u32[]{:S(2)}, u32[]{:S(2)}) collective-permute-start(bf16[4,64,2048]{2,1,0:T(8,128)(2,1)} %collective-permute-done.5.refs_2_), channel_id=1, source_target_pairs={{0,16},{16,0},{1,17},{17,1},{2,18},{18,2},{3,19},{19,3},{4,20},{20... | collective-permute-start | bytes 3145736 | tf_op jit(solution)/shard_map/ppermute | solution.py:450
  65.8 17.3 %collective-permute-start.4 = (bf16[4,2,96,512]{3,2,1,0:T(8,128)(2,1)S(1)}, bf16[4,2,96,512]{3,2,1,0:T(8,128)(2,1)S(1)}, u32[]{:S(2)}, u32[]{:S(2)}) collective-permute-start(bf16[4,2,96,512]{3,2,1,0:T(8,128)(2,1)S(1)} %all-to-all-done.1.refs_0_), channel_id=1, source_target_pairs={{0,1},{1,0},{2,3},{3,2},{4,5},{5,4},{6,7},{7,6},{8,9},{9,8},{10,11... | collective-permute-start | bytes 2359304 | tf_op jit(solution)/shard_map/ppermute | solution.py:442
  81.1 7.7 %copy-start.6 = (bf16[4,2,96,512]{3,2,1,0:T(8,128)(2,1)}, bf16[4,2,96,512]{3,2,1,0:T(8,128)(2,1)S(1)}, u32[]{:S(2)}) copy-start(bf16[4,2,96,512]{3,2,1,0:T(8,128)(2,1)S(1)} %collective-permute-done.7.refs_2_) | copy-start | bytes 2359300
  81.1 7.7 %collective-permute-start.8 = (bf16[4,2,96,512]{3,2,1,0:T(8,128)(2,1)S(1)}, bf16[4,2,96,512]{3,2,1,0:T(8,128)(2,1)}, u32[]{:S(2)}, u32[]{:S(2)}) collective-permute-start(bf16[4,2,96,512]{3,2,1,0:T(8,128)(2,1)S(1)} %collective-permute-done.7.refs_2_), channel_id=1, source_target_pairs={{0,1},{1,0},{2,3},{3,2},{4,5},{5,4},{6,7},{7,6},{8,9},{9,8},{10,11... | collective-permute-start | bytes 2359304 | tf_op jit(solution)/shard_map/ppermute | solution.py:442
  81.6 26.4 %collective-permute-start.10 = (bf16[4,64,2048]{2,1,0:T(8,128)(2,1)}, bf16[4,64,2048]{2,1,0:T(8,128)(2,1)}, u32[]{:S(2)}, u32[]{:S(2)}) collective-permute-start(bf16[4,64,2048]{2,1,0:T(8,128)(2,1)} %all-to-all-done.refs_0_), channel_id=1, source_target_pairs={{0,1},{1,0},{2,3},{3,2},{4,5},{5,4},{6,7},{7,6},{8,9},{9,8},{10,11... | collective-permute-start | bytes 3145736 | tf_op jit(solution)/shard_map/ppermute | solution.py:442
  81.6 24.3 %collective-permute-start.3 = (bf16[4,2,96,512]{3,2,1,0:T(8,128)(2,1)}, bf16[4,2,96,512]{3,2,1,0:T(8,128)(2,1)}, u32[]{:S(2)}, u32[]{:S(2)}) collective-permute-start(bf16[4,2,96,512]{3,2,1,0:T(8,128)(2,1)} %all-to-all-done.2.refs_0_), channel_id=1, source_target_pairs={{0,2},{1,3},{2,0},{3,1},{4,6},{5,7},{6,4},{7,5},{8,10},{9,11},{10,... | collective-permute-start | bytes 2359304 | tf_op jit(solution)/shard_map/ppermute | solution.py:438
  83.2 5.6 %copy-start.8 = (bf16[4,2,96,512]{3,2,1,0:T(8,128)(2,1)}, bf16[4,2,96,512]{3,2,1,0:T(8,128)(2,1)S(1)}, u32[]{:S(2)}) copy-start(bf16[4,2,96,512]{3,2,1,0:T(8,128)(2,1)S(1)} %collective-permute-done.4.refs_1_) | copy-start | bytes 2359300
  83.2 25.0 %all-to-all-start.3 = ((bf16[4,2,96,512]{3,2,1,0:T(8,128)(2,1)}), bf16[4,2,96,512]{3,2,1,0:T(8,128)(2,1)S(1)}, u32[]{:S(2)}, u32[]{:S(2)}) async-start(bf16[4,2,96,512]{3,2,1,0:T(8,128)(2,1)} %get-tuple-element.45), calls=%async_computation.3 | async-start | bytes 1572864 | tf_op jit(solution)/shard_map/all_to_all | solution.py:459
  88.3 22.0 %collective-permute-start.11 = (bf16[4,64,2048]{2,1,0:T(8,128)(2,1)}, bf16[4,64,2048]{2,1,0:T(8,128)(2,1)}, u32[]{:S(2)}, u32[]{:S(2)}) collective-permute-start(bf16[4,64,2048]{2,1,0:T(8,128)(2,1)} %collective-permute-done.6.refs_1_), channel_id=1, source_target_pairs={{0,1},{1,0},{2,3},{3,2},{4,5},{5,4},{6,7},{7,6},{8,9},{9,8},{10,11... | collective-permute-start | bytes 3145736 | tf_op jit(solution)/shard_map/ppermute | solution.py:442
  88.3 23.5 %collective-permute-start.12 = (bf16[4,64,2048]{2,1,0:T(8,128)(2,1)}, bf16[4,64,2048]{2,1,0:T(8,128)(2,1)}, u32[]{:S(2)}, u32[]{:S(2)}) collective-permute-start(bf16[4,64,2048]{2,1,0:T(8,128)(2,1)} %collective-permute-done.5.refs_2_), channel_id=1, source_target_pairs={{0,1},{1,0},{2,3},{3,2},{4,5},{5,4},{6,7},{7,6},{8,9},{9,8},{10,11... | collective-permute-start | bytes 3145736 | tf_op jit(solution)/shard_map/ppermute | solution.py:442
  88.8 25.3 %collective-permute-start.14 = (bf16[4,64,2048]{2,1,0:T(8,128)(2,1)}, bf16[4,64,2048]{2,1,0:T(8,128)(2,1)}, u32[]{:S(2)}, u32[]{:S(2)}) collective-permute-start(bf16[4,64,2048]{2,1,0:T(8,128)(2,1)} %collective-permute-done.13.refs_3_), channel_id=1, source_target_pairs={{0,1},{1,0},{2,3},{3,2},{4,5},{5,4},{6,7},{7,6},{8,9},{9,8},{10,11... | collective-permute-start | bytes 3145736 | tf_op jit(solution)/shard_map/ppermute | solution.py:442
  88.9 1.1 copy-start.2
  90.0 1.9 %copy-start.3 = (bf16[3,2,512,512]{3,2,1,0:T(8,128)(2,1)S(1)}, bf16[3,2,512,512]{3,2,1,0:T(8,128)(2,1)}, u32[]{:S(2)}) copy-start(bf16[3,2,512,512]{3,2,1,0:T(8,128)(2,1)} %refs_4_.1) | copy-start | bytes 9437188
  91.9 1.1 copy-start.7
  93.0 1.1 copy-start.9
  105.1 0.9 copy-start.4
  106.0 8.8 %collective-permute-start.2 = (bf16[4,2,96,512]{3,2,1,0:T(8,128)(2,1)}, bf16[4,2,96,512]{3,2,1,0:T(8,128)(2,1)}, u32[]{:S(2)}, u32[]{:S(2)}) collective-permute-start(bf16[4,2,96,512]{3,2,1,0:T(8,128)(2,1)} %all-to-all-done.2.refs_0_), channel_id=1, source_target_pairs={{0,1},{1,0},{2,3},{3,2},{4,5},{5,4},{6,7},{7,6},{8,9},{9,8},{10,11... | collective-permute-start | bytes 2359304 | tf_op jit(solution)/shard_map/ppermute | solution.py:442
  108.1 6.7 %collective-permute-start.9 = (bf16[4,2,96,512]{3,2,1,0:T(8,128)(2,1)}, bf16[4,2,96,512]{3,2,1,0:T(8,128)(2,1)}, u32[]{:S(2)}, u32[]{:S(2)}) collective-permute-start(bf16[4,2,96,512]{3,2,1,0:T(8,128)(2,1)} %collective-permute-done.3.refs_2_), channel_id=1, source_target_pairs={{0,1},{1,0},{2,3},{3,2},{4,5},{5,4},{6,7},{7,6},{8,9},{9,8},{10,11... | collective-permute-start | bytes 2359304 | tf_op jit(solution)/shard_map/ppermute | solution.py:442
  108.1 6.6 %copy-start.5 = (f32[3,512,1]{2,1,0:T(8,128)S(1)}, f32[3,512,1]{2,1,0:T(8,128)}, u32[]{:S(2)}) copy-start(f32[3,512,1]{2,1,0:T(8,128)} %copy-done.4) | copy-start | bytes 18436
  110.3 14.9 %collective-permute-start.15 = (bf16[96,512]{1,0:T(8,128)(2,1)S(1)}, bf16[96,512]{1,0:T(8,128)(2,1)S(1)}, u32[]{:S(2)}, u32[]{:S(2)}) collective-permute-start(bf16[96,512]{1,0:T(8,128)(2,1)S(1)} %get-tuple-element.54), channel_id=1, source_target_pairs={{0,4},{1,5},{2,6},{3,7},{4,0},{5,1},{6,2},{7,3},{8,12},{9,13},{10,... | collective-permute-start | bytes 294920 | tf_op jit(solution)/shard_map/ppermute | solution.py:446
  111.7 13.5 %collective-permute-start.16 = (bf16[96,512]{1,0:T(8,128)(2,1)S(1)}, bf16[96,512]{1,0:T(8,128)(2,1)S(1)}, u32[]{:S(2)}, u32[]{:S(2)}) collective-permute-start(bf16[96,512]{1,0:T(8,128)(2,1)S(1)} %get-tuple-element.55), channel_id=1, source_target_pairs={{0,8},{1,9},{2,10},{3,11},{4,12},{5,13},{6,14},{7,15},{8,0},{9,1},... | collective-permute-start | bytes 294920 | tf_op jit(solution)/shard_map/ppermute | solution.py:446
  114.0 11.2 %collective-permute-start.17 = (bf16[96,512]{1,0:T(8,128)(2,1)S(1)}, bf16[96,512]{1,0:T(8,128)(2,1)S(1)}, u32[]{:S(2)}, u32[]{:S(2)}) collective-permute-start(bf16[96,512]{1,0:T(8,128)(2,1)S(1)} %get-tuple-element.56), channel_id=1, source_target_pairs={{0,12},{1,13},{2,14},{3,15},{4,8},{5,9},{6,10},{7,11},{8,4},{9,5},... | collective-permute-start | bytes 294920 | tf_op jit(solution)/shard_map/ppermute | solution.py:446
  125.2 10.5 %collective-permute-start.20 = (bf16[96,512]{1,0:T(8,128)(2,1)S(1)}, bf16[96,512]{1,0:T(8,128)(2,1)S(1)}, u32[]{:S(2)}, u32[]{:S(2)}) collective-permute-start(bf16[96,512]{1,0:T(8,128)(2,1)S(1)} %get-tuple-element.61), channel_id=1, source_target_pairs={{0,12},{1,13},{2,14},{3,15},{4,8},{5,9},{6,10},{7,11},{8,4},{9,5},... | collective-permute-start | bytes 294920 | tf_op jit(solution)/shard_map/ppermute | solution.py:446
  128.4 7.7 %collective-permute-start.19 = (bf16[96,512]{1,0:T(8,128)(2,1)S(1)}, bf16[96,512]{1,0:T(8,128)(2,1)S(1)}, u32[]{:S(2)}, u32[]{:S(2)}) collective-permute-start(bf16[96,512]{1,0:T(8,128)(2,1)S(1)} %get-tuple-element.59), channel_id=1, source_target_pairs={{0,8},{1,9},{2,10},{3,11},{4,12},{5,13},{6,14},{7,15},{8,0},{9,1},... | collective-permute-start | bytes 294920 | tf_op jit(solution)/shard_map/ppermute | solution.py:446
  128.4 7.7 %collective-permute-start.18 = (bf16[96,512]{1,0:T(8,128)(2,1)S(1)}, bf16[96,512]{1,0:T(8,128)(2,1)S(1)}, u32[]{:S(2)}, u32[]{:S(2)}) collective-permute-start(bf16[96,512]{1,0:T(8,128)(2,1)S(1)} %get-tuple-element.57), channel_id=1, source_target_pairs={{0,4},{1,5},{2,6},{3,7},{4,0},{5,1},{6,2},{7,3},{8,12},{9,13},{10,... | collective-permute-start | bytes 294920 | tf_op jit(solution)/shard_map/ppermute | solution.py:446

commit v6 on v5

--- a/solution.py
+++ b/solution.py
@@ -289,7 +289,7 @@
 
 
 def hbm():
-    return pl.BlockSpec(memory_space=pltpu.HBM)
+    return pl.BlockSpec(memory_space=pl.ANY)
 
 
 def smem():

time: 140 us -> 140 us (level)
  no operation moved by 1% of the time
where the time goes in v6:
time: 140 us; the launch traced here: 139 us
  waiting for transfers between devices  52 us (37%)
  Pallas kernels  39.7 us (28%)
  starting transfers between devices  37.4 us (27%)
  local copies, waits for them, and re-layouts  9.18 us (7%)
    all_to_all x4, waiting for transfers between devices, exchange(): lax.all_to_all(arr, 'seq', 0, 0, axis_index_groups=groups, tiled=True)  30.8 us
    all_to_all x4, starting transfers between devices, exchange(): lax.all_to_all(arr, 'seq', 0, 0, axis_index_groups=groups, tiled=True)  18.5 us
    ppermute x3, waiting for transfers between devices, swap_line(): lax.ppermute(arr, BOTH, routes(lambda row, line, core: (row, 1 - line, co...  16.5 us
    pallas_call x1, Pallas kernels, first_update(): pl.pallas_call(first_kernel, in_specs=[smem()] + [hbm()] * 6, out_specs=[...  10.9 us
    pallas_call x1, Pallas kernels, step(): pl.pallas_call(functools.partial(step_kernel, block), in_specs=[smem()] +...  10.4 us
    ppermute x6, starting transfers between devices, swap_row(): lax.ppermute(arr, BOTH, routes(lambda row, line, core: (row ^ turn, line,...  8.91 us
    unnamed x24, local copies, waits for them, and re-layouts  8 us
    pallas_call x2, Pallas kernels, project(): pl.pallas_call(project_first if first is None else project_second, in_spe...  4.89 us
  transfers between devices with their start and end apart: 25, of which 9 were waited for; matrix products, arithmetic and copies ran while one was open for 1% of the time, Pallas kernels for 26%

profile of v6, /device:TPU:0, one launch (start us, length us, event | category | flops | bytes accessed | tf_op | source)
XLA Modules:
  0.0 139.0 jit_solution(16355556403155977730)
XLA Ops:
  0.0 0.5 collective-permute-start.1
  0.5 0.8 copy-done
  1.2 1.2 broadcast_in_dim.2
  2.4 6.3 %all-to-all-start = ((bf16[4,64,2048]{2,1,0:T(8,128)(2,1)}), bf16[4,64,2048]{2,1,0:T(8,128)(2,1)}, u32[]{:S(2)}, u32[]{:S(2)}) async-start(bf16[4,64,2048]{2,1,0:T(8,128)(2,1)} %broadcast_in_dim.2), calls=%async_computation | async-start | bytes 2097152 | tf_op jit(solution)/shard_map/all_to_all | solution.py:459
  8.7 0.6 pad_add_fusion.place
  9.3 3.5 %pack.1 = (bf16[6,96,1024]{2,1,0:T(8,128)(2,1)}, bf16[6,96,1024]{2,1,0:T(8,128)(2,1)}) custom-call(s32[4]{0:T(128)} %pad_add_fusion.place, bf16[2,192,1024]{2,1,0:T(8,128)(2,1)} %queries, bf16[2,192,1024]{2,1,0:T(8,128)(2,1)} %keys.1, bf16[2,192,1024]{2,1,0:T(8,128)(2,1)} %values.1, f32[2,2,192]{2,1,0:T(2,128)} %bitcast.5), custom_call_target="tpu_custom_call" | custom-call | flops 1 | bytes 1 | tf_op jit(solution)/shard_map/pack/pallas_call | solution.py:134
  12.9 0.1 collective-permute-start
  12.9 3.0 %collective-permute-done.got = bf16[6,96,1024]{2,1,0:T(8,128)(2,1)S(1)} collective-permute-done((bf16[6,96,1024]{2,1,0:T(8,128)(2,1)}, bf16[6,96,1024]{2,1,0:T(8,128)(2,1)S(1)}, u32[]{:S(2)}, u32[]{:S(2)}) %collective-permute-start) | collective-permute-done | bytes 1179680 | tf_op jit(solution)/shard_map/ppermute | solution.py:442
  16.0 1.1 copy-done.11
  17.0 3.8 %deal.1 = (bf16[4,2,96,512]{3,2,1,0:T(8,128)(2,1)}, bf16[4,2,96,512]{3,2,1,0:T(8,128)(2,1)}, bf16[4,2,96,512]{3,2,1,0:T(8,128)(2,1)}) custom-call(s32[4]{0:T(128)} %pad_add_fusion.place, bf16[6,96,1024]{2,1,0:T(8,128)(2,1)} %get-tuple-element.35.kept, bf16[6,96,1024]{2,1,0:T(8,128)(2,1)} %copy-done.11), custom_call_target="tpu_custom_call" | custom-call | flops 1 | bytes 1 | tf_op jit(solution)/shard_map/deal/pallas_call | solution.py:171
  20.9 13.7 %all-to-all-done.refs_0_ = bf16[4,64,2048]{2,1,0:T(8,128)(2,1)} async-done(((bf16[4,64,2048]{2,1,0:T(8,128)(2,1)}), bf16[4,64,2048]{2,1,0:T(8,128)(2,1)}, u32[]{:S(2)}, u32[]{:S(2)}) %all-to-all-start) | async-done | bytes 1048608 | tf_op jit(solution)/shard_map/all_to_all | solution.py:459
  34.6 0.0 collective-permute-done.1.refs_5_
  34.6 3.5 %all-to-all-start.1 = ((bf16[4,2,96,512]{3,2,1,0:T(8,128)(2,1)}), bf16[4,2,96,512]{3,2,1,0:T(8,128)(2,1)S(1)}, u32[]{:S(2)}, u32[]{:S(2)}) async-start(bf16[4,2,96,512]{3,2,1,0:T(8,128)(2,1)} %get-tuple-element.39), calls=%async_computation.1 | async-start | bytes 1572864 | tf_op jit(solution)/shard_map/all_to_all | solution.py:459
  38.1 1.6 %collective-permute-start.6 = (bf16[4,64,2048]{2,1,0:T(8,128)(2,1)}, bf16[4,64,2048]{2,1,0:T(8,128)(2,1)}, u32[]{:S(2)}, u32[]{:S(2)}) collective-permute-start(bf16[4,64,2048]{2,1,0:T(8,128)(2,1)} %all-to-all-done.refs_0_), channel_id=1, source_target_pairs={{0,16},{16,0},{1,17},{17,1},{2,18},{18,2},{3,19},{19,3},{4,20},{20... | collective-permute-start | bytes 3145736 | tf_op jit(solution)/shard_map/ppermute | solution.py:450
  39.6 1.5 %collective-permute-start.5 = (bf16[4,64,2048]{2,1,0:T(8,128)(2,1)}, bf16[4,64,2048]{2,1,0:T(8,128)(2,1)}, u32[]{:S(2)}, u32[]{:S(2)}) collective-permute-start(bf16[4,64,2048]{2,1,0:T(8,128)(2,1)} %all-to-all-done.refs_0_), channel_id=1, source_target_pairs={{0,2},{1,3},{2,0},{3,1},{4,6},{5,7},{6,4},{7,5},{8,10},{9,11},{10,... | collective-permute-start | bytes 3145736 | tf_op jit(solution)/shard_map/ppermute | solution.py:438
  41.1 16.5 %all-to-all-done.1.refs_0_ = bf16[4,2,96,512]{3,2,1,0:T(8,128)(2,1)S(1)} async-done(((bf16[4,2,96,512]{3,2,1,0:T(8,128)(2,1)}), bf16[4,2,96,512]{3,2,1,0:T(8,128)(2,1)S(1)}, u32[]{:S(2)}, u32[]{:S(2)}) %all-to-all-start.1) | async-done | bytes 786464 | tf_op jit(solution)/shard_map/all_to_all | solution.py:459
  57.6 4.3 %all-to-all-start.2 = ((bf16[4,2,96,512]{3,2,1,0:T(8,128)(2,1)}), bf16[4,2,96,512]{3,2,1,0:T(8,128)(2,1)}, u32[]{:S(2)}, u32[]{:S(2)}) async-start(bf16[4,2,96,512]{3,2,1,0:T(8,128)(2,1)} %get-tuple-element.40), calls=%async_computation.2 | async-start | bytes 1572864 | tf_op jit(solution)/shard_map/all_to_all | solution.py:459
  62.0 0.6 collective-permute-done.6.refs_1_
  62.6 1.2 collective-permute-done.5.refs_2_
  63.8 1.5 %collective-permute-start.7 = (bf16[4,2,96,512]{3,2,1,0:T(8,128)(2,1)S(1)}, bf16[4,2,96,512]{3,2,1,0:T(8,128)(2,1)S(1)}, u32[]{:S(2)}, u32[]{:S(2)}) collective-permute-start(bf16[4,2,96,512]{3,2,1,0:T(8,128)(2,1)S(1)} %all-to-all-done.1.refs_0_), channel_id=1, source_target_pairs={{0,2},{1,3},{2,0},{3,1},{4,6},{5,7},{6,4},{7,5},{8,10},{9,11},{10,... | collective-permute-start | bytes 2359304 | tf_op jit(solution)/shard_map/ppermute | solution.py:438
  65.3 0.5 collective-permute-start.13
  65.8 0.0 collective-permute-start.4
  65.8 15.2 %collective-permute-done.7.refs_2_ = bf16[4,2,96,512]{3,2,1,0:T(8,128)(2,1)S(1)} collective-permute-done((bf16[4,2,96,512]{3,2,1,0:T(8,128)(2,1)S(1)}, bf16[4,2,96,512]{3,2,1,0:T(8,128)(2,1)S(1)}, u32[]{:S(2)}, u32[]{:S(2)}) %collective-permute-start.7) | collective-permute-done | bytes 786464 | tf_op jit(solution)/shard_map/ppermute | solution.py:438
  81.1 0.0 collective-permute-start.8
  81.1 0.5 all-to-all-done.2.refs_0_
  81.6 0.0 collective-permute-start.10
  81.6 1.5 %collective-permute-start.3 = (bf16[4,2,96,512]{3,2,1,0:T(8,128)(2,1)}, bf16[4,2,96,512]{3,2,1,0:T(8,128)(2,1)}, u32[]{:S(2)}, u32[]{:S(2)}) collective-permute-start(bf16[4,2,96,512]{3,2,1,0:T(8,128)(2,1)} %all-to-all-done.2.refs_0_), channel_id=1, source_target_pairs={{0,2},{1,3},{2,0},{3,1},{4,6},{5,7},{6,4},{7,5},{8,10},{9,11},{10,... | collective-permute-start | bytes 2359304 | tf_op jit(solution)/shard_map/ppermute | solution.py:438
  83.2 0.0 collective-permute-done.4.refs_1_
  83.2 4.4 %all-to-all-start.3 = ((bf16[4,2,96,512]{3,2,1,0:T(8,128)(2,1)}), bf16[4,2,96,512]{3,2,1,0:T(8,128)(2,1)S(1)}, u32[]{:S(2)}, u32[]{:S(2)}) async-start(bf16[4,2,96,512]{3,2,1,0:T(8,128)(2,1)} %get-tuple-element.45), calls=%async_computation.3 | async-start | bytes 1572864 | tf_op jit(solution)/shard_map/all_to_all | solution.py:459
  87.6 0.7 collective-permute-done.13.refs_3_
  88.3 0.0 collective-permute-start.11
  88.3 0.5 collective-permute-start.12
  88.8 0.0 collective-permute-done.8.refs_3_
  88.8 0.1 collective-permute-start.14
  88.9 0.0 copy-start.2
  88.9 1.1 copy-done.2
  90.0 1.9 %copy-done.3 = bf16[3,2,512,512]{3,2,1,0:T(8,128)(2,1)S(1)} copy-done((bf16[3,2,512,512]{3,2,1,0:T(8,128)(2,1)S(1)}, bf16[3,2,512,512]{3,2,1,0:T(8,128)(2,1)}, u32[]{:S(2)}) %copy-start.3) | copy-done | bytes 3145752
  91.9 1.1 copy-done.7
  93.0 1.1 copy-done.9
  94.2 10.9 %first_update.1 = (bf16[3,512,512]{2,1,0:T(8,128)(2,1)S(1)}, f32[3,512,1]{2,1,0:T(8,128)S(1)}) custom-call(s32[4]{0:T(128)S(1)} %copy-done.10, bf16[4,2,96,512]{3,2,1,0:T(8,128)(2,1)S(1)} %copy-done.2, bf16[4,2,96,512]{3,2,1,0:T(8,128)(2,1)S(1)} %copy-done.9, bf16[4,2,96,512]{3,2,1,0:T(8,128)(2,1)S(1)} %copy-done.7, ...), custom_call_target="tpu_custom_call" | custom-call | flops 1 | bytes 1 | tf_op jit(solution)/shard_map/first_update/pallas_call | solution.py:315
  105.1 0.0 copy-start.4
  105.1 0.9 copy-done.4
  106.0 0.0 collective-permute-done.3.refs_2_
  106.0 2.1 %collective-permute-start.2 = (bf16[4,2,96,512]{3,2,1,0:T(8,128)(2,1)}, bf16[4,2,96,512]{3,2,1,0:T(8,128)(2,1)}, u32[]{:S(2)}, u32[]{:S(2)}) collective-permute-start(bf16[4,2,96,512]{3,2,1,0:T(8,128)(2,1)} %all-to-all-done.2.refs_0_), channel_id=1, source_target_pairs={{0,1},{1,0},{2,3},{3,2},{4,5},{5,4},{6,7},{7,6},{8,9},{9,8},{10,11... | collective-permute-start | bytes 2359304 | tf_op jit(solution)/shard_map/ppermute | solution.py:442
  108.0 0.0 collective-permute-done.10.refs_4_
  108.1 0.1 collective-permute-start.9
  108.1 0.0 all-to-all-done.3.refs_4_.refs_0_
  108.1 2.1 %apply.1 = (bf16[96,512]{1,0:T(8,128)(2,1)S(1)}, bf16[96,512]{1,0:T(8,128)(2,1)S(1)}, bf16[96,512]{1,0:T(8,128)(2,1)S(1)}, bf16[96,512]{1,0:T(8,128)(2,1)S(1)}) custom-call(s32[4]{0:T(128)S(1)} %copy-done.10, bf16[4,2,96,512]{3,2,1,0:T(8,128)(2,1)S(1)} %all-to-all-done.3.refs_4_.refs_0_, bf16[3,512,512]{2,1,0:T(8,128)(2,1)S(1)} %get-tuple-element.50.refs_5_.refs_1_), custom_call_target="tpu_custom_call" | custom-call | flops 1 | bytes 1 | tf_op jit(solution)/shard_map/apply/pallas_call | solution.py:335
  110.3 0.0 collective-permute-done.11.refs_5_
  110.3 1.4 %collective-permute-start.15 = (bf16[96,512]{1,0:T(8,128)(2,1)S(1)}, bf16[96,512]{1,0:T(8,128)(2,1)S(1)}, u32[]{:S(2)}, u32[]{:S(2)}) collective-permute-start(bf16[96,512]{1,0:T(8,128)(2,1)S(1)} %get-tuple-element.54), channel_id=1, source_target_pairs={{0,4},{1,5},{2,6},{3,7},{4,0},{5,1},{6,2},{7,3},{8,12},{9,13},{10,... | collective-permute-start | bytes 294920 | tf_op jit(solution)/shard_map/ppermute | solution.py:446
  111.7 2.3 %collective-permute-start.16 = (bf16[96,512]{1,0:T(8,128)(2,1)S(1)}, bf16[96,512]{1,0:T(8,128)(2,1)S(1)}, u32[]{:S(2)}, u32[]{:S(2)}) collective-permute-start(bf16[96,512]{1,0:T(8,128)(2,1)S(1)} %get-tuple-element.55), channel_id=1, source_target_pairs={{0,8},{1,9},{2,10},{3,11},{4,12},{5,13},{6,14},{7,15},{8,0},{9,1},... | collective-permute-start | bytes 294920 | tf_op jit(solution)/shard_map/ppermute | solution.py:446
  114.0 0.0 collective-permute-done.14.refs_7_
  114.0 0.7 collective-permute-start.17
  114.8 10.4 %step.1 = (bf16[3,512,512]{2,1,0:T(8,128)(2,1)}, bf16[96,512]{1,0:T(8,128)(2,1)S(1)}, bf16[96,512]{1,0:T(8,128)(2,1)S(1)}, bf16[96,512]{1,0:T(8,128)(2,1)S(1)}, bf16[96,512]{1,0:T(8,128)(2,1)S(1)}) custom-call(s32[4]{0:T(128)S(1)} %copy-done.10, bf16[4,2,96,512]{3,2,1,0:T(8,128)(2,1)} %all-to-all-done.2.refs_0_, ...), custom_call_target="tpu_custom_call" | custom-call | flops 1 | bytes 1 | tf_op jit(solution)/shard_map/step/pallas_call | solution.py:348
  125.2 0.0 collective-permute-done.15.refs_1_
  125.2 0.0 collective-permute-done.16.refs_2_
  125.2 3.2 %collective-permute-start.20 = (bf16[96,512]{1,0:T(8,128)(2,1)S(1)}, bf16[96,512]{1,0:T(8,128)(2,1)S(1)}, u32[]{:S(2)}, u32[]{:S(2)}) collective-permute-start(bf16[96,512]{1,0:T(8,128)(2,1)S(1)} %get-tuple-element.61), channel_id=1, source_target_pairs={{0,12},{1,13},{2,14},{3,15},{4,8},{5,9},{6,10},{7,11},{8,4},{9,5},... | collective-permute-start | bytes 294920 | tf_op jit(solution)/shard_map/ppermute | solution.py:446
  128.4 0.0 collective-permute-start.19
  128.4 1.3 collective-permute-start.18
  129.7 4.0 %place_slabs.1.refs_4_.refs_5_ = bf16[4,512,2048]{2,1,0:T(8,128)(2,1)S(1)} custom-call(s32[4]{0:T(128)S(1)} %copy-done.10, bf16[4,64,2048]{2,1,0:T(8,128)(2,1)} %all-to-all-done.refs_0_, bf16[4,64,2048]{2,1,0:T(8,128)(2,1)} %collective-permute-done.6.refs_1_, bf16[4,64,2048]{2,1,0:T(8,128)(2,1)} %collective-permute-done.5.refs_2_, ...), custom_call_target="tpu_custom_call" | custom-call | flops 1 | bytes 1 | tf_op jit(solution)/shard_map/place_slabs/pallas_call | solution.py:381
  133.7 2.0 %project.2.refs_4_ = bf16[96,2048]{1,0:T(8,128)(2,1)S(1)} custom-call(s32[4]{0:T(128)S(1)} %copy-done.10, bf16[96,512]{1,0:T(8,128)(2,1)S(1)} %get-tuple-element.62.refs_0_, bf16[96,512]{1,0:T(8,128)(2,1)S(1)} %collective-permute-done.15.refs_1_, bf16[96,512]{1,0:T(8,128)(2,1)S(1)} %collective-permute-done.16.refs_2_, ...), custom_call_target="tpu_custom_call" | custom-call | flops 1 | bytes 1 | tf_op jit(solution)/shard_map/project/pallas_call | solution.py:416
  135.7 0.0 collective-permute-done.20.refs_3_
  135.7 0.4 collective-permute-done.19.refs_2_
  136.1 2.9 %project.3 = bf16[2,96,2048]{2,1,0:T(8,128)(2,1)} custom-call(s32[4]{0:T(128)S(1)} %copy-done.10, bf16[96,512]{1,0:T(8,128)(2,1)S(1)} %get-tuple-element.52.refs_0_, bf16[96,512]{1,0:T(8,128)(2,1)S(1)} %collective-permute-done.18.refs_1_, bf16[96,512]{1,0:T(8,128)(2,1)S(1)} %collective-permute-done.19.refs_2_, ...), custom_call_target="tpu_custom_call" | custom-call | flops 1 | bytes 1 | tf_op jit(solution)/shard_map/project/pallas_call | solution.py:416
  (21 shorter events, 0.1 us)
Async XLA Ops:
  0.0 1.2 copy-start
  0.0 34.6 %collective-permute-start.1 = (bf16[3,2,512,512]{3,2,1,0:T(8,128)(2,1)}, bf16[3,2,512,512]{3,2,1,0:T(8,128)(2,1)}, u32[]{:S(2)}, u32[]{:S(2)}) collective-permute-start(bf16[3,2,512,512]{3,2,1,0:T(8,128)(2,1)} %refs_4_.1), channel_id=1, source_target_pairs={{0,1},{1,0},{2,3},{3,2},{4,5},{5,4},{6,7},{7,6},{8,9},{9,8},{10,11... | collective-permute-start | bytes 9437192 | tf_op jit(solution)/shard_map/ppermute | solution.py:442
  2.4 32.1 %all-to-all-start = ((bf16[4,64,2048]{2,1,0:T(8,128)(2,1)}), bf16[4,64,2048]{2,1,0:T(8,128)(2,1)}, u32[]{:S(2)}, u32[]{:S(2)}) async-start(bf16[4,64,2048]{2,1,0:T(8,128)(2,1)} %broadcast_in_dim.2), calls=%async_computation | async-start | bytes 2097152 | tf_op jit(solution)/shard_map/all_to_all | solution.py:459
  12.9 3.1 %collective-permute-start = (bf16[6,96,1024]{2,1,0:T(8,128)(2,1)}, bf16[6,96,1024]{2,1,0:T(8,128)(2,1)S(1)}, u32[]{:S(2)}, u32[]{:S(2)}) collective-permute-start(bf16[6,96,1024]{2,1,0:T(8,128)(2,1)} %get-tuple-element.36), channel_id=1, source_target_pairs={{0,1},{1,0},{2,3},{3,2},{4,5},{5,4},{6,7},{7,6},{8,9},{9,8},{10,11... | collective-permute-start | bytes 3538952 | tf_op jit(solution)/shard_map/ppermute | solution.py:442
  16.0 1.1 copy-start.11
  34.6 23.1 %all-to-all-start.1 = ((bf16[4,2,96,512]{3,2,1,0:T(8,128)(2,1)}), bf16[4,2,96,512]{3,2,1,0:T(8,128)(2,1)S(1)}, u32[]{:S(2)}, u32[]{:S(2)}) async-start(bf16[4,2,96,512]{3,2,1,0:T(8,128)(2,1)} %get-tuple-element.39), calls=%async_computation.1 | async-start | bytes 1572864 | tf_op jit(solution)/shard_map/all_to_all | solution.py:459
  38.1 24.5 %collective-permute-start.6 = (bf16[4,64,2048]{2,1,0:T(8,128)(2,1)}, bf16[4,64,2048]{2,1,0:T(8,128)(2,1)}, u32[]{:S(2)}, u32[]{:S(2)}) collective-permute-start(bf16[4,64,2048]{2,1,0:T(8,128)(2,1)} %all-to-all-done.refs_0_), channel_id=1, source_target_pairs={{0,16},{16,0},{1,17},{17,1},{2,18},{18,2},{3,19},{19,3},{4,20},{20... | collective-permute-start | bytes 3145736 | tf_op jit(solution)/shard_map/ppermute | solution.py:450
  39.6 24.2 %collective-permute-start.5 = (bf16[4,64,2048]{2,1,0:T(8,128)(2,1)}, bf16[4,64,2048]{2,1,0:T(8,128)(2,1)}, u32[]{:S(2)}, u32[]{:S(2)}) collective-permute-start(bf16[4,64,2048]{2,1,0:T(8,128)(2,1)} %all-to-all-done.refs_0_), channel_id=1, source_target_pairs={{0,2},{1,3},{2,0},{3,1},{4,6},{5,7},{6,4},{7,5},{8,10},{9,11},{10,... | collective-permute-start | bytes 3145736 | tf_op jit(solution)/shard_map/ppermute | solution.py:438
  57.6 25.5 %copy-start.1 = (bf16[4,2,96,512]{3,2,1,0:T(8,128)(2,1)}, bf16[4,2,96,512]{3,2,1,0:T(8,128)(2,1)S(1)}, u32[]{:S(2)}) copy-start(bf16[4,2,96,512]{3,2,1,0:T(8,128)(2,1)S(1)} %all-to-all-done.1.refs_0_) | copy-start | bytes 2359300
  57.6 31.2 %copy-start.10 = (s32[4]{0:T(128)S(1)}, s32[4]{0:T(128)}, u32[]{:S(2)}) copy-start(s32[4]{0:T(128)} %pad_add_fusion.place) | copy-start | bytes 52
  57.6 24.0 %all-to-all-start.2 = ((bf16[4,2,96,512]{3,2,1,0:T(8,128)(2,1)}), bf16[4,2,96,512]{3,2,1,0:T(8,128)(2,1)}, u32[]{:S(2)}, u32[]{:S(2)}) async-start(bf16[4,2,96,512]{3,2,1,0:T(8,128)(2,1)} %get-tuple-element.40), calls=%async_computation.2 | async-start | bytes 1572864 | tf_op jit(solution)/shard_map/all_to_all | solution.py:459
  63.8 17.3 %collective-permute-start.7 = (bf16[4,2,96,512]{3,2,1,0:T(8,128)(2,1)S(1)}, bf16[4,2,96,512]{3,2,1,0:T(8,128)(2,1)S(1)}, u32[]{:S(2)}, u32[]{:S(2)}) collective-permute-start(bf16[4,2,96,512]{3,2,1,0:T(8,128)(2,1)S(1)} %all-to-all-done.1.refs_0_), channel_id=1, source_target_pairs={{0,2},{1,3},{2,0},{3,1},{4,6},{5,7},{6,4},{7,5},{8,10},{9,11},{10,... | collective-permute-start | bytes 2359304 | tf_op jit(solution)/shard_map/ppermute | solution.py:438
  65.3 23.0 %collective-permute-start.13 = (bf16[4,64,2048]{2,1,0:T(8,128)(2,1)}, bf16[4,64,2048]{2,1,0:T(8,128)(2,1)}, u32[]{:S(2)}, u32[]{:S(2)}) collective-permute-start(bf16[4,64,2048]{2,1,0:T(8,128)(2,1)} %collective-permute-done.5.refs_2_), channel_id=1, source_target_pairs={{0,16},{16,0},{1,17},{17,1},{2,18},{18,2},{3,19},{19,3},{4,20},{20... | collective-permute-start | bytes 3145736 | tf_op jit(solution)/shard_map/ppermute | solution.py:450
  65.8 17.3 %collective-permute-start.4 = (bf16[4,2,96,512]{3,2,1,0:T(8,128)(2,1)S(1)}, bf16[4,2,96,512]{3,2,1,0:T(8,128)(2,1)S(1)}, u32[]{:S(2)}, u32[]{:S(2)}) collective-permute-start(bf16[4,2,96,512]{3,2,1,0:T(8,128)(2,1)S(1)} %all-to-all-done.1.refs_0_), channel_id=1, source_target_pairs={{0,1},{1,0},{2,3},{3,2},{4,5},{5,4},{6,7},{7,6},{8,9},{9,8},{10,11... | collective-permute-start | bytes 2359304 | tf_op jit(solution)/shard_map/ppermute | solution.py:442
  81.1 7.7 %copy-start.6 = (bf16[4,2,96,512]{3,2,1,0:T(8,128)(2,1)}, bf16[4,2,96,512]{3,2,1,0:T(8,128)(2,1)S(1)}, u32[]{:S(2)}) copy-start(bf16[4,2,96,512]{3,2,1,0:T(8,128)(2,1)S(1)} %collective-permute-done.7.refs_2_) | copy-start | bytes 2359300
  81.1 7.7 %collective-permute-start.8 = (bf16[4,2,96,512]{3,2,1,0:T(8,128)(2,1)S(1)}, bf16[4,2,96,512]{3,2,1,0:T(8,128)(2,1)}, u32[]{:S(2)}, u32[]{:S(2)}) collective-permute-start(bf16[4,2,96,512]{3,2,1,0:T(8,128)(2,1)S(1)} %collective-permute-done.7.refs_2_), channel_id=1, source_target_pairs={{0,1},{1,0},{2,3},{3,2},{4,5},{5,4},{6,7},{7,6},{8,9},{9,8},{10,11... | collective-permute-start | bytes 2359304 | tf_op jit(solution)/shard_map/ppermute | solution.py:442
  81.6 26.4 %collective-permute-start.10 = (bf16[4,64,2048]{2,1,0:T(8,128)(2,1)}, bf16[4,64,2048]{2,1,0:T(8,128)(2,1)}, u32[]{:S(2)}, u32[]{:S(2)}) collective-permute-start(bf16[4,64,2048]{2,1,0:T(8,128)(2,1)} %all-to-all-done.refs_0_), channel_id=1, source_target_pairs={{0,1},{1,0},{2,3},{3,2},{4,5},{5,4},{6,7},{7,6},{8,9},{9,8},{10,11... | collective-permute-start | bytes 3145736 | tf_op jit(solution)/shard_map/ppermute | solution.py:442
  81.6 24.3 %collective-permute-start.3 = (bf16[4,2,96,512]{3,2,1,0:T(8,128)(2,1)}, bf16[4,2,96,512]{3,2,1,0:T(8,128)(2,1)}, u32[]{:S(2)}, u32[]{:S(2)}) collective-permute-start(bf16[4,2,96,512]{3,2,1,0:T(8,128)(2,1)} %all-to-all-done.2.refs_0_), channel_id=1, source_target_pairs={{0,2},{1,3},{2,0},{3,1},{4,6},{5,7},{6,4},{7,5},{8,10},{9,11},{10,... | collective-permute-start | bytes 2359304 | tf_op jit(solution)/shard_map/ppermute | solution.py:438
  83.2 5.6 %copy-start.8 = (bf16[4,2,96,512]{3,2,1,0:T(8,128)(2,1)}, bf16[4,2,96,512]{3,2,1,0:T(8,128)(2,1)S(1)}, u32[]{:S(2)}) copy-start(bf16[4,2,96,512]{3,2,1,0:T(8,128)(2,1)S(1)} %collective-permute-done.4.refs_1_) | copy-start | bytes 2359300
  83.2 25.0 %all-to-all-start.3 = ((bf16[4,2,96,512]{3,2,1,0:T(8,128)(2,1)}), bf16[4,2,96,512]{3,2,1,0:T(8,128)(2,1)S(1)}, u32[]{:S(2)}, u32[]{:S(2)}) async-start(bf16[4,2,96,512]{3,2,1,0:T(8,128)(2,1)} %get-tuple-element.45), calls=%async_computation.3 | async-start | bytes 1572864 | tf_op jit(solution)/shard_map/all_to_all | solution.py:459
  88.3 22.0 %collective-permute-start.11 = (bf16[4,64,2048]{2,1,0:T(8,128)(2,1)}, bf16[4,64,2048]{2,1,0:T(8,128)(2,1)}, u32[]{:S(2)}, u32[]{:S(2)}) collective-permute-start(bf16[4,64,2048]{2,1,0:T(8,128)(2,1)} %collective-permute-done.6.refs_1_), channel_id=1, source_target_pairs={{0,1},{1,0},{2,3},{3,2},{4,5},{5,4},{6,7},{7,6},{8,9},{9,8},{10,11... | collective-permute-start | bytes 3145736 | tf_op jit(solution)/shard_map/ppermute | solution.py:442
  88.3 23.5 %collective-permute-start.12 = (bf16[4,64,2048]{2,1,0:T(8,128)(2,1)}, bf16[4,64,2048]{2,1,0:T(8,128)(2,1)}, u32[]{:S(2)}, u32[]{:S(2)}) collective-permute-start(bf16[4,64,2048]{2,1,0:T(8,128)(2,1)} %collective-permute-done.5.refs_2_), channel_id=1, source_target_pairs={{0,1},{1,0},{2,3},{3,2},{4,5},{5,4},{6,7},{7,6},{8,9},{9,8},{10,11... | collective-permute-start | bytes 3145736 | tf_op jit(solution)/shard_map/ppermute | solution.py:442
  88.8 25.3 %collective-permute-start.14 = (bf16[4,64,2048]{2,1,0:T(8,128)(2,1)}, bf16[4,64,2048]{2,1,0:T(8,128)(2,1)}, u32[]{:S(2)}, u32[]{:S(2)}) collective-permute-start(bf16[4,64,2048]{2,1,0:T(8,128)(2,1)} %collective-permute-done.13.refs_3_), channel_id=1, source_target_pairs={{0,1},{1,0},{2,3},{3,2},{4,5},{5,4},{6,7},{7,6},{8,9},{9,8},{10,11... | collective-permute-start | bytes 3145736 | tf_op jit(solution)/shard_map/ppermute | solution.py:442
  88.9 1.1 copy-start.2
  90.0 1.9 %copy-start.3 = (bf16[3,2,512,512]{3,2,1,0:T(8,128)(2,1)S(1)}, bf16[3,2,512,512]{3,2,1,0:T(8,128)(2,1)}, u32[]{:S(2)}) copy-start(bf16[3,2,512,512]{3,2,1,0:T(8,128)(2,1)} %refs_4_.1) | copy-start | bytes 9437188
  91.9 1.1 copy-start.7
  93.0 1.1 copy-start.9
  105.1 0.9 copy-start.4
  106.0 8.8 %collective-permute-start.2 = (bf16[4,2,96,512]{3,2,1,0:T(8,128)(2,1)}, bf16[4,2,96,512]{3,2,1,0:T(8,128)(2,1)}, u32[]{:S(2)}, u32[]{:S(2)}) collective-permute-start(bf16[4,2,96,512]{3,2,1,0:T(8,128)(2,1)} %all-to-all-done.2.refs_0_), channel_id=1, source_target_pairs={{0,1},{1,0},{2,3},{3,2},{4,5},{5,4},{6,7},{7,6},{8,9},{9,8},{10,11... | collective-permute-start | bytes 2359304 | tf_op jit(solution)/shard_map/ppermute | solution.py:442
  108.1 6.7 %collective-permute-start.9 = (bf16[4,2,96,512]{3,2,1,0:T(8,128)(2,1)}, bf16[4,2,96,512]{3,2,1,0:T(8,128)(2,1)}, u32[]{:S(2)}, u32[]{:S(2)}) collective-permute-start(bf16[4,2,96,512]{3,2,1,0:T(8,128)(2,1)} %collective-permute-done.3.refs_2_), channel_id=1, source_target_pairs={{0,1},{1,0},{2,3},{3,2},{4,5},{5,4},{6,7},{7,6},{8,9},{9,8},{10,11... | collective-permute-start | bytes 2359304 | tf_op jit(solution)/shard_map/ppermute | solution.py:442
  108.1 6.6 %copy-start.5 = (f32[3,512,1]{2,1,0:T(8,128)S(1)}, f32[3,512,1]{2,1,0:T(8,128)}, u32[]{:S(2)}) copy-start(f32[3,512,1]{2,1,0:T(8,128)} %copy-done.4) | copy-start | bytes 18436
  110.3 14.9 %collective-permute-start.15 = (bf16[96,512]{1,0:T(8,128)(2,1)S(1)}, bf16[96,512]{1,0:T(8,128)(2,1)S(1)}, u32[]{:S(2)}, u32[]{:S(2)}) collective-permute-start(bf16[96,512]{1,0:T(8,128)(2,1)S(1)} %get-tuple-element.54), channel_id=1, source_target_pairs={{0,4},{1,5},{2,6},{3,7},{4,0},{5,1},{6,2},{7,3},{8,12},{9,13},{10,... | collective-permute-start | bytes 294920 | tf_op jit(solution)/shard_map/ppermute | solution.py:446
  111.7 13.5 %collective-permute-start.16 = (bf16[96,512]{1,0:T(8,128)(2,1)S(1)}, bf16[96,512]{1,0:T(8,128)(2,1)S(1)}, u32[]{:S(2)}, u32[]{:S(2)}) collective-permute-start(bf16[96,512]{1,0:T(8,128)(2,1)S(1)} %get-tuple-element.55), channel_id=1, source_target_pairs={{0,8},{1,9},{2,10},{3,11},{4,12},{5,13},{6,14},{7,15},{8,0},{9,1},... | collective-permute-start | bytes 294920 | tf_op jit(solution)/shard_map/ppermute | solution.py:446
  114.0 11.2 %collective-permute-start.17 = (bf16[96,512]{1,0:T(8,128)(2,1)S(1)}, bf16[96,512]{1,0:T(8,128)(2,1)S(1)}, u32[]{:S(2)}, u32[]{:S(2)}) collective-permute-start(bf16[96,512]{1,0:T(8,128)(2,1)S(1)} %get-tuple-element.56), channel_id=1, source_target_pairs={{0,12},{1,13},{2,14},{3,15},{4,8},{5,9},{6,10},{7,11},{8,4},{9,5},... | collective-permute-start | bytes 294920 | tf_op jit(solution)/shard_map/ppermute | solution.py:446
  125.2 10.5 %collective-permute-start.20 = (bf16[96,512]{1,0:T(8,128)(2,1)S(1)}, bf16[96,512]{1,0:T(8,128)(2,1)S(1)}, u32[]{:S(2)}, u32[]{:S(2)}) collective-permute-start(bf16[96,512]{1,0:T(8,128)(2,1)S(1)} %get-tuple-element.61), channel_id=1, source_target_pairs={{0,12},{1,13},{2,14},{3,15},{4,8},{5,9},{6,10},{7,11},{8,4},{9,5},... | collective-permute-start | bytes 294920 | tf_op jit(solution)/shard_map/ppermute | solution.py:446
  128.4 7.7 %collective-permute-start.19 = (bf16[96,512]{1,0:T(8,128)(2,1)S(1)}, bf16[96,512]{1,0:T(8,128)(2,1)S(1)}, u32[]{:S(2)}, u32[]{:S(2)}) collective-permute-start(bf16[96,512]{1,0:T(8,128)(2,1)S(1)} %get-tuple-element.59), channel_id=1, source_target_pairs={{0,8},{1,9},{2,10},{3,11},{4,12},{5,13},{6,14},{7,15},{8,0},{9,1},... | collective-permute-start | bytes 294920 | tf_op jit(solution)/shard_map/ppermute | solution.py:446
  128.4 7.7 %collective-permute-start.18 = (bf16[96,512]{1,0:T(8,128)(2,1)S(1)}, bf16[96,512]{1,0:T(8,128)(2,1)S(1)}, u32[]{:S(2)}, u32[]{:S(2)}) collective-permute-start(bf16[96,512]{1,0:T(8,128)(2,1)S(1)} %get-tuple-element.57), channel_id=1, source_target_pairs={{0,4},{1,5},{2,6},{3,7},{4,0},{5,1},{6,2},{7,3},{8,12},{9,13},{10,... | collective-permute-start | bytes 294920 | tf_op jit(solution)/shard_map/ppermute | solution.py:446
